TPU v7x, 32 devices: a whole 2x2x4 slice. The times are simulated.
32 devices in a mesh: dp: 8 (over z, y), section: 4 (over x, core).
Axes of the slice: x: 2, y: 2, z: 4, core: 2. Of those that a mesh axis runs over, the one named last changes fastest.
Arguments:
- images: bfloat16 [32, 14, 14, 768], P(('dp', 'section')), may hold values from -6 to 6
- cotangent: bfloat16 [32, 14, 14, 768], P(('dp', 'section')), may hold values from -6 to 6
- window_rows: int32 [32], P('dp'), may hold values from 1 to 2
- window_cols: int32 [32], P('dp'), may hold values from 1 to 2
- pos_kernel: bfloat16 [4, 9, 768], P('section'), may hold values from -2 to 2
- pos_bias: bfloat16 [4, 768], P('section'), may hold values from -3 to 3
- norm_gain: bfloat16 [4, 768], P('section'), may hold values from 0.5 to 1.5
- norm_shift: bfloat16 [4, 768], P('section'), may hold values from -2 to 2
- first_weight: bfloat16 [4, 768, 3072], P('section'), may hold values from -1 to 1
- second_weight: bfloat16 [6144, 768], P('section'), may hold values from -0.15625 to 0.15625
Outputs:
- activations: bfloat16 [32, 14, 14, 768], P(('dp', 'section'))
- input_grad: float32 [32, 14, 14, 768], P(('dp', 'section'))
- first_grad: float32 [4, 768, 3072], P('section')
- second_grad: float32 [6144, 768], P('section')
- kernel_grad: float32 [4, 9, 768], P('section')
- bias_grad: float32 [4, 768], P('section')
- gain_grad: float32 [4, 768], P('section')
- shift_grad: float32 [4, 768], P('section')
Inputs may be any that keep to these rules, and one draw needn't show every extreme that they name: Image i covers the top 7 * window_rows[i] patch rows of its slot. Image i covers the left 7 * window_cols[i] patch columns of its slot.
All inputs are finite; a program needn't handle non-finite values.
Results may differ from a plain program's by a relative error of at most 0.035.
Values may be sent and summed in bfloat16 or wider, within the bound.
A program may use at most 576 MiB of HBM per device.

v0:
```python
from functools import partial

import jax
import jax.numpy as jnp
from jax import lax
from jax.sharding import PartitionSpec as P

D = 768
FF = 3072
HEADS = 24
HEAD = 32
WIN = 7
SIDE = 2


eps_norm = 1e-05


def shifted(block, axis, distance):
    devices = range(lax.axis_size(axis))
    route = [(i - distance, i) for i in devices if i - distance in devices]
    return lax.ppermute(block, axis, route)


def as_sent(value):

    def short(part):
        return part.astype(jnp.bfloat16) if part.dtype == jnp.float32 else part

    return jax.tree.map(short, value)


def grid_mask(height, width):
    positions = jnp.arange(SIDE * WIN)
    rows_in = positions[None, :] < (WIN * height)[:, None]
    cols_in = positions[None, :] < (WIN * width)[:, None]
    return (rows_in[:, :, None] & cols_in[:, None, :]).astype(jnp.float32)


def front(section_in, inside, kernel, conv_bias, gain_vec, shift_vec):
    grid = SIDE * WIN
    masked = section_in * inside[..., None]
    padded = jnp.pad(masked, ((0, 0), (1, 1), (1, 1), (0, 0)))
    mixed_in = section_in + conv_bias
    for row_off in range(3):
        for col_off in range(3):
            mixed_in = (
                mixed_in
                + padded[:, row_off : row_off + grid, col_off : col_off + grid, :]
                * kernel[3 * row_off + col_off]
            )
    average = jnp.mean(mixed_in, axis=-1, keepdims=True)
    centred = mixed_in - average
    spread = jnp.mean(centred * centred, axis=-1, keepdims=True)
    normed = centred * lax.rsqrt(spread + eps_norm) * gain_vec + shift_vec
    return (mixed_in, normed)


def front_back(section_in, inside, params, grad_mixed, grad_normed):

    def local_front(state, kernel, conv_bias, gain_vec, shift_vec):
        return front(state, inside, kernel, conv_bias, gain_vec, shift_vec)

    unused, pull = jax.vjp(local_front, section_in, params[0], params[1], params[2], params[3])
    return pull((grad_mixed, grad_normed))


def to_windows(tensor):
    number = tensor.shape[0]
    channels = tensor.shape[-1]
    shaped = tensor.reshape(number, SIDE, WIN, SIDE, WIN, channels).transpose(0, 1, 3, 2, 4, 5)
    return shaped.reshape(number * SIDE * SIDE, WIN * WIN, channels)


def from_windows(tensor, number):
    channels = tensor.shape[-1]
    shaped = tensor.reshape(number, SIDE, SIDE, WIN, WIN, channels).transpose(0, 1, 3, 2, 4, 5)
    return shaped.reshape(number, SIDE * WIN, SIDE * WIN, channels)


def outer(former, latter):
    return lax.dot_general(
        former, latter, (((0, 1, 2), (0, 1, 2)), ((), ())), preferred_element_type=jnp.float32
    )


def back_dot(grads, weight):
    return lax.dot_general(
        grads, weight, (((3,), (1,)), ((), ())), preferred_element_type=jnp.float32
    )


def window_parts(qkv_low):
    windows = to_windows(qkv_low)
    groups = windows.shape[0]
    queries = windows[..., :D].reshape(groups, WIN * WIN, HEADS, HEAD)
    key_rows = windows[..., D : 2 * D].reshape(groups, WIN * WIN, HEADS, HEAD)
    values = windows[..., 2 * D :].reshape(groups, WIN * WIN, HEADS, HEAD)
    scores = jnp.einsum(
        "wqhe,wkhe->whqk", queries, key_rows, preferred_element_type=jnp.float32
    ) * HEAD ** (-0.5)
    attend = jax.nn.softmax(scores, axis=-1)
    return (queries, key_rows, values, attend)


def window_forward(qkv_low, inside):
    queries, key_rows, values, attend = window_parts(qkv_low)
    mixed = jnp.einsum(
        "whqk,wkhe->wqhe", attend.astype(jnp.bfloat16), values, preferred_element_type=jnp.float32
    )
    mixed = mixed.reshape(mixed.shape[0], WIN * WIN, D).astype(jnp.bfloat16)
    return from_windows(mixed, qkv_low.shape[0])


def window_backward(qkv_low, grad_mixed, inside):
    queries, key_rows, values, attend = window_parts(qkv_low)
    groups = queries.shape[0]
    grad_win = to_windows(grad_mixed).reshape(queries.shape)
    grad_attend = jnp.einsum(
        "wqhe,wkhe->whqk", grad_win, values, preferred_element_type=jnp.float32
    )
    grad_values = jnp.einsum(
        "whqk,wqhe->wkhe", attend.astype(jnp.bfloat16), grad_win, preferred_element_type=jnp.float32
    )
    grad_scores = (
        attend * (grad_attend - jnp.sum(grad_attend * attend, axis=-1, keepdims=True))
    ).astype(jnp.bfloat16)
    grad_queries = jnp.einsum(
        "whqk,wkhe->wqhe", grad_scores, key_rows, preferred_element_type=jnp.float32
    ) * HEAD ** (-0.5)
    grad_keys = jnp.einsum(
        "whqk,wqhe->wkhe", grad_scores, queries, preferred_element_type=jnp.float32
    ) * HEAD ** (-0.5)
    joined = jnp.concatenate(
        [
            grad_queries.reshape(groups, WIN * WIN, D),
            grad_keys.reshape(groups, WIN * WIN, D),
            grad_values.reshape(groups, WIN * WIN, D),
        ],
        axis=-1,
    )
    return from_windows(joined.astype(jnp.bfloat16), qkv_low.shape[0])


def channel_parts(qkv_low, inside):
    number = qkv_low.shape[0]
    tokens_img = qkv_low.shape[1] * qkv_low.shape[2]
    flattened = qkv_low.reshape(number, tokens_img, 3 * D)
    inside_low = inside.reshape(number, tokens_img, 1, 1).astype(jnp.bfloat16)
    queries = flattened[..., :D].reshape(number, tokens_img, HEADS, HEAD)
    key_rows = flattened[..., D : 2 * D].reshape(number, tokens_img, HEADS, HEAD) * inside_low
    values = flattened[..., 2 * D :].reshape(number, tokens_img, HEADS, HEAD)
    scores = jnp.einsum(
        "bnhi,bnhj->bhij", queries, key_rows, preferred_element_type=jnp.float32
    ) * HEAD ** (-0.5)
    attend = jax.nn.softmax(scores, axis=-1)
    return (queries, key_rows, values, attend, inside_low)


def channel_forward(qkv_low, inside):
    queries, key_rows, values, attend, inside_low = channel_parts(qkv_low, inside)
    mixed = jnp.einsum(
        "bhij,bnhj->bnhi", attend.astype(jnp.bfloat16), values, preferred_element_type=jnp.float32
    )
    return mixed.reshape(qkv_low.shape[:3] + (D,)).astype(jnp.bfloat16)


def channel_backward(qkv_low, grad_mixed, inside):
    queries, key_rows, values, attend, inside_low = channel_parts(qkv_low, inside)
    grad_heads = grad_mixed.reshape(queries.shape)
    grad_attend = jnp.einsum(
        "bnhi,bnhj->bhij", grad_heads, values, preferred_element_type=jnp.float32
    )
    grad_values = jnp.einsum(
        "bhij,bnhi->bnhj",
        attend.astype(jnp.bfloat16),
        grad_heads,
        preferred_element_type=jnp.float32,
    )
    grad_scores = (
        attend * (grad_attend - jnp.sum(grad_attend * attend, axis=-1, keepdims=True))
    ).astype(jnp.bfloat16)
    grad_queries = jnp.einsum(
        "bhij,bnhj->bnhi", grad_scores, key_rows, preferred_element_type=jnp.float32
    ) * HEAD ** (-0.5)
    grad_keys = (
        jnp.einsum("bhij,bnhi->bnhj", grad_scores, queries, preferred_element_type=jnp.float32)
        * HEAD ** (-0.5)
        * inside_low
    )
    flat_shape = qkv_low.shape[:3] + (D,)
    joined = jnp.concatenate(
        [
            grad_queries.reshape(flat_shape),
            grad_keys.reshape(flat_shape),
            grad_values.reshape(flat_shape),
        ],
        axis=-1,
    )
    return joined.astype(jnp.bfloat16)


def attention_forward(section_in, inside, params, first_mat, core):
    mixed_in, normed = front(section_in, inside, params[0], params[1], params[2], params[3])
    normed_low = normed.astype(jnp.bfloat16)
    qkv_low = jnp.dot(normed_low, first_mat[:, : 3 * D], preferred_element_type=jnp.float32).astype(
        jnp.bfloat16
    )
    attended = core(qkv_low, inside)
    result = (
        mixed_in + jnp.dot(attended, first_mat[:, 3 * D :], preferred_element_type=jnp.float32)
    ).astype(jnp.bfloat16)
    middle = jnp.concatenate([qkv_low, attended], axis=-1).astype(jnp.float32)
    return (result, normed_low, middle)


def mlp_forward(section_in, inside, params, first_mat, second):
    mixed_in, normed = front(section_in, inside, params[0], params[1], params[2], params[3])
    normed_low = normed.astype(jnp.bfloat16)
    hidden = jnp.dot(normed_low, first_mat, preferred_element_type=jnp.float32)
    active = jax.nn.gelu(hidden, approximate=False).astype(jnp.bfloat16)
    result = (mixed_in + jnp.dot(active, second, preferred_element_type=jnp.float32)).astype(
        jnp.bfloat16
    )
    return (result, normed_low, hidden)


def attention_backward(
    section_in, inside, normed_low, middle, grad_out, params, first_mat, core_back
):
    grad_low = grad_out.astype(jnp.bfloat16)
    qkv_low = middle[..., : 3 * D].astype(jnp.bfloat16)
    attended = middle[..., 3 * D :].astype(jnp.bfloat16)
    grad_proj = outer(attended, grad_low)
    grad_attended = back_dot(grad_low, first_mat[:, 3 * D :]).astype(jnp.bfloat16)
    grad_qkv = core_back(qkv_low, grad_attended, inside)
    grad_first = jnp.concatenate([outer(normed_low, grad_qkv), grad_proj], axis=-1)
    grad_normed = back_dot(grad_qkv, first_mat[:, : 3 * D])
    grad_in, grad_kernel, grad_bias, grad_gain, grad_shift = front_back(
        section_in, inside, params, grad_out, grad_normed
    )
    grad_second = jnp.zeros((FF, D), jnp.float32)
    return (grad_in, grad_first, grad_second, grad_kernel, grad_bias, grad_gain, grad_shift)


def mlp_backward(section_in, inside, normed_low, middle, grad_out, params, first_mat, second):
    grad_low = grad_out.astype(jnp.bfloat16)
    active, gelu_pull = jax.vjp(partial(jax.nn.gelu, approximate=False), middle)
    grad_second = outer(active.astype(jnp.bfloat16), grad_low)
    grad_active = back_dot(grad_low, second)
    grad_hidden = gelu_pull(grad_active)[0].astype(jnp.bfloat16)
    grad_first = outer(normed_low, grad_hidden)
    grad_normed = back_dot(grad_hidden, first_mat)
    grad_in, grad_kernel, grad_bias, grad_gain, grad_shift = front_back(
        section_in, inside, params, grad_out, grad_normed
    )
    return (grad_in, grad_first, grad_second, grad_kernel, grad_bias, grad_gain, grad_shift)


def store(buffer, value, slot_id, active):
    current = lax.dynamic_index_in_dim(buffer, slot_id, 0, keepdims=False)
    return lax.dynamic_update_index_in_dim(buffer, jnp.where(active, value, current), slot_id, 0)


def per_device(
    images,
    cotangent,
    window_rows,
    window_cols,
    pos_kernel,
    pos_bias,
    norm_gain,
    norm_shift,
    first_weight,
    second_weight,
):
    section_id = lax.axis_index("section")
    sections = lax.axis_size("section")
    last_section = sections - 1
    per_micro = images.shape[0]
    act_shape = images.shape
    mid_shape = act_shape[:3] + (FF,)
    params = (
        pos_kernel[0].astype(jnp.float32),
        pos_bias[0].astype(jnp.float32),
        norm_gain[0].astype(jnp.float32),
        norm_shift[0].astype(jnp.float32),
    )
    first_mat = first_weight[0]
    received = shifted(second_weight, "section", 1)
    second_full = jnp.concatenate([received, second_weight], axis=0)
    all_images, all_cotangents = (
        lax.all_gather(images, "section", axis=0, tiled=True),
        lax.all_gather(cotangent, "section", axis=0, tiled=True),
    )

    def micro_mask(slot_id):
        height = lax.dynamic_slice_in_dim(window_rows, slot_id * per_micro, per_micro)
        width = lax.dynamic_slice_in_dim(window_cols, slot_id * per_micro, per_micro)
        return grid_mask(height, width)

    forward_kinds = [
        partial(attention_forward, params=params, first_mat=first_mat, core=window_forward),
        partial(mlp_forward, params=params, first_mat=first_mat, second=second_full),
        partial(attention_forward, params=params, first_mat=first_mat, core=channel_forward),
        partial(mlp_forward, params=params, first_mat=first_mat, second=second_full),
    ]
    backward_kinds = [
        partial(attention_backward, params=params, first_mat=first_mat, core_back=window_backward),
        partial(mlp_backward, params=params, first_mat=first_mat, second=second_full),
        partial(attention_backward, params=params, first_mat=first_mat, core_back=channel_backward),
        partial(mlp_backward, params=params, first_mat=first_mat, second=second_full),
    ]

    def forward_section(section_in, inside):
        return lax.switch(section_id, forward_kinds, section_in, inside)

    def spare_forward(section_in, inside):
        return (
            jnp.zeros(act_shape, jnp.bfloat16),
            jnp.zeros(act_shape, jnp.bfloat16),
            jnp.zeros(mid_shape, jnp.float32),
        )

    def backward_section(section_in, inside, normed_low, middle, grad_out):
        return lax.switch(
            section_id, backward_kinds, section_in, inside, normed_low, middle, grad_out
        )

    def recompute_backward(section_in, inside, grad_out):
        unused, normed_again, middle_again = forward_section(section_in, inside)
        return backward_section(section_in, inside, normed_again, middle_again, grad_out)

    def spare_backward(*ignored):
        return (
            jnp.zeros(act_shape, jnp.float32),
            jnp.zeros((D, FF), jnp.float32),
            jnp.zeros((FF, D), jnp.float32),
            jnp.zeros((9, D), jnp.float32),
            jnp.zeros((D,), jnp.float32),
            jnp.zeros((D,), jnp.float32),
            jnp.zeros((D,), jnp.float32),
        )

    ticks = 2 * sections - 1
    passing = jnp.zeros(act_shape, jnp.bfloat16)
    kept_in = jnp.zeros((sections,) + act_shape, jnp.bfloat16)
    outputs = jnp.zeros((sections,) + act_shape, jnp.bfloat16)
    for moment in range(ticks):
        micro_id = moment - section_id
        active = (micro_id >= 0) & (micro_id < sections)
        slot_id = jnp.clip(micro_id, 0, last_section)
        first_slot = min(moment, last_section)
        incoming = all_images[first_slot * per_micro : (first_slot + 1) * per_micro]
        section_in = jnp.where(section_id == 0, incoming, passing)
        inside = micro_mask(slot_id)
        result, normed_low, middle = lax.cond(
            active, forward_section, spare_forward, section_in.astype(jnp.float32), inside
        )
        kept_in = store(kept_in, section_in, slot_id, active)
        outputs = store(outputs, result * inside.astype(jnp.bfloat16)[..., None], slot_id, active)
        if moment + 1 < ticks:
            passing = jax.tree.map(
                lambda part, own: part.astype(own.dtype),
                shifted(as_sent(result), "section", 1),
                result,
            )
    totals = spare_backward()[1:]
    input_all = jnp.zeros((sections,) + act_shape, jnp.float32)
    passing_grad = jnp.zeros(act_shape, jnp.bfloat16)
    for moment in range(ticks):
        micro_id = moment - (last_section - section_id)
        active = (micro_id >= 0) & (micro_id < sections)
        slot_id = jnp.clip(micro_id, 0, last_section)
        top_slot = min(moment, last_section)
        inside = micro_mask(slot_id)
        incoming = (
            all_cotangents[top_slot * per_micro : (top_slot + 1) * per_micro].astype(jnp.float32)
            * inside[..., None]
        )
        grad_out = jnp.where(section_id == last_section, incoming, passing_grad.astype(jnp.float32))
        section_in = lax.dynamic_index_in_dim(kept_in, slot_id, 0, keepdims=False).astype(
            jnp.float32
        )
        found = lax.cond(active, recompute_backward, spare_backward, section_in, inside, grad_out)
        totals = tuple((total + part for total, part in zip(totals, found[1:])))
        input_all = store(input_all, found[0], slot_id, active)
        if moment + 1 < ticks:
            passing_grad = shifted(found[0].astype(jnp.bfloat16), "section", -1)
    grad_first, grad_second, grad_kernel, grad_bias, grad_gain, grad_shift = totals
    half_rows = grad_second.shape[0] // 2
    summed = lax.psum(
        (grad_first, grad_second, grad_kernel, grad_bias, grad_gain, grad_shift), "dp"
    )
    grad_first, full_second, grad_kernel, grad_bias, grad_gain, grad_shift = summed
    returned = shifted(full_second[:half_rows].astype(jnp.bfloat16), "section", -1).astype(
        jnp.float32
    )
    grad_half = jnp.where(section_id % 2 == 1, full_second[half_rows:], returned)
    stacked = outputs.reshape((sections * per_micro,) + act_shape[1:])
    delivered = lax.all_to_all(stacked, "section", split_axis=0, concat_axis=0, tiled=True)
    activations = delivered[last_section * per_micro :]
    grads_stack = input_all.reshape((sections * per_micro,) + act_shape[1:])
    returned_in = lax.all_to_all(
        grads_stack.astype(jnp.bfloat16), "section", split_axis=0, concat_axis=0, tiled=True
    ).astype(grads_stack.dtype)
    input_grad = returned_in[:per_micro]
    return (
        activations,
        input_grad,
        grad_first[None],
        grad_half,
        grad_kernel[None],
        grad_bias[None],
        grad_gain[None],
        grad_shift[None],
    )


def solution(mesh):
    in_specs = (
        P(("dp", "section"), None, None, None),
        P(("dp", "section"), None, None, None),
        P("dp"),
        P("dp"),
        P("section", None, None),
        P("section", None),
        P("section", None),
        P("section", None),
        P("section", None, None),
        P("section", None),
    )
    out_specs = (
        P(("dp", "section"), None, None, None),
        P(("dp", "section"), None, None, None),
        P("section", None, None),
        P("section", None),
        P("section", None, None),
        P("section", None),
        P("section", None),
        P("section", None),
    )
    return jax.shard_map(
        per_device, mesh=mesh, in_specs=in_specs, out_specs=out_specs, check_vma=False
    )
```

profile of v0, /device:TPU:0, one launch (start us, length us, event | category | flops | bytes accessed | tf_op | source)
XLA Modules:
  0.0 1987.6 jit_solution(17502551018447543660)
XLA Ops:
  49.2 50.2 %conditional.126 = (bf16[1,14,14,768]{3,2,1,0:T(8,128)(2,1)}) conditional(s32[]{:T(128)} %convert_element_type.2600, () %tuple.575, (s32[]{:T(128)}, f32[768]{0:T(1024)S(1)}, f32[1,14,14,768]{3,2,1,0:T(8,128)S(1)}, f32[1,14,14]{2,1,0:T(8,128)S(1)}, f32[9,768]{1,0:T(8,128)S(1)}, /*index=5*/f32[768]{0:T(1024)S(1)}, f32[768]{0:T(1024)S(1)}, ...), branch_computations={%region_0.1_spmd, %region_1.18_spmd} | conditional | flops 1904243968 | bytes 25666864 | solution.py:357
  49.2 42.5 %conditional.53 = (bf16[1,14,14,768]{3,2,1,0:T(8,128)(2,1)}) conditional(s32[]{:T(128)} %clamp.42, (f32[768]{0:T(1024)S(1)}, f32[1,14,14,768]{3,2,1,0:T(8,128)S(1)}, f32[1,14,14]{2,1,0:T(8,128)S(1)}, f32[9,768]{1,0:T(8,128)S(1)}, f32[768]{0:T(1024)S(1)}, /*index=5*/f32[768]{0:T(1024)S(1)}, ...), branch_computations={%region_2.6_spmd, %region_7.9_spmd, %region_10.14_spmd, %region_15... | conditional | flops 1904243968 | bytes 25666728
  104.5 56.6 %conditional.127 = (bf16[1,14,14,768]{3,2,1,0:T(8,128)(2,1)}) conditional(s32[]{:T(128)} %convert_element_type.2613, () %tuple.577, (s32[]{:T(128)}, f32[768]{0:T(1024)S(1)}, f32[1,14,14,768]{3,2,1,0:T(8,128)S(1)}, f32[1,14,14]{2,1,0:T(8,128)S(1)}, f32[9,768]{1,0:T(8,128)S(1)}, /*index=5*/f32[768]{0:T(1024)S(1)}, f32[768]{0:T(1024)S(1)}, ...), branch_computations={%region_18.19_spmd, %region_19.36_spmd} | conditional | flops 1904243968 | bytes 30526824 | solution.py:357
  104.5 49.0 %conditional.54 = (bf16[1,14,14,768]{3,2,1,0:T(8,128)(2,1)}) conditional(s32[]{:T(128)} %clamp.43, (f32[768]{0:T(1024)S(1)}, f32[1,14,14,768]{3,2,1,0:T(8,128)S(1)}, f32[1,14,14]{2,1,0:T(8,128)S(1)}, f32[9,768]{1,0:T(8,128)S(1)}, f32[768]{0:T(1024)S(1)}, /*index=5*/f32[768]{0:T(1024)S(1)}, ...), branch_computations={%region_20.24_spmd, %region_25.27_spmd, %region_28.32_spmd, %regio... | conditional | flops 1904243968 | bytes 30526688
  165.1 56.6 %conditional.128 = (bf16[1,14,14,768]{3,2,1,0:T(8,128)(2,1)}) conditional(s32[]{:T(128)} %convert_element_type.2618, () %tuple.579, (s32[]{:T(128)}, f32[768]{0:T(1024)S(1)}, f32[1,14,14,768]{3,2,1,0:T(8,128)S(1)}, f32[1,14,14]{2,1,0:T(8,128)S(1)}, f32[9,768]{1,0:T(8,128)S(1)}, /*index=5*/f32[768]{0:T(1024)S(1)}, f32[768]{0:T(1024)S(1)}, ...), branch_computations={%region_36.37_spmd, %region_37.54_spmd} | conditional | flops 1904243968 | bytes 30526824 | solution.py:357
  165.1 49.0 %conditional.60 = (bf16[1,14,14,768]{3,2,1,0:T(8,128)(2,1)}) conditional(s32[]{:T(128)} %clamp.44, (f32[768]{0:T(1024)S(1)}, f32[1,14,14,768]{3,2,1,0:T(8,128)S(1)}, f32[1,14,14]{2,1,0:T(8,128)S(1)}, f32[9,768]{1,0:T(8,128)S(1)}, f32[768]{0:T(1024)S(1)}, /*index=5*/f32[768]{0:T(1024)S(1)}, ...), branch_computations={%region_38.42_spmd, %region_43.45_spmd, %region_46.50_spmd, %regio... | conditional | flops 1904243968 | bytes 30526688
  225.7 49.3 %conditional.129 = (bf16[1,14,14,768]{3,2,1,0:T(8,128)(2,1)}) conditional(s32[]{:T(128)} %convert_element_type.2623, () %tuple.581, (s32[]{:T(128)}, f32[768]{0:T(1024)S(1)}, f32[1,14,14,768]{3,2,1,0:T(8,128)S(1)}, f32[1,14,14]{2,1,0:T(8,128)S(1)}, f32[9,768]{1,0:T(8,128)S(1)}, /*index=5*/f32[768]{0:T(1024)S(1)}, f32[768]{0:T(1024)S(1)}, ...), branch_computations={%region_54.55_spmd, %region_55.72_spmd} | conditional | flops 1904243968 | bytes 30526824 | solution.py:357
  225.7 49.3 %conditional.61 = (bf16[1,14,14,768]{3,2,1,0:T(8,128)(2,1)}) conditional(s32[]{:T(128)} %clamp.45, (f32[768]{0:T(1024)S(1)}, f32[1,14,14,768]{3,2,1,0:T(8,128)S(1)}, f32[1,14,14]{2,1,0:T(8,128)S(1)}, f32[9,768]{1,0:T(8,128)S(1)}, f32[768]{0:T(1024)S(1)}, /*index=5*/f32[768]{0:T(1024)S(1)}, ...), branch_computations={%region_56.60_spmd, %region_61.63_spmd, %region_64.68_spmd, %regio... | conditional | flops 1904243968 | bytes 30526688
  279.0 14.1 conditional.130
  293.1 11.4 collective-permute-start.5
  307.2 11.1 conditional.131
  325.4 22.4 %conditional.140 = (bf16[1,14,14,768]{3,2,1,0:T(8,128)(2,1)}, f32[3072,768]{1,0:T(8,128)}, f32[9,768]{1,0:T(8,128)}, f32[768]{0:T(1024)}, f32[768]{0:T(1024)}, /*index=5*/f32[768]{0:T(1024)}, f32[768,3072]{1,0:T(8,128)}) conditional(s32[]{:T(128)} %convert_element_type.2643, () %tuple.589, (s32[]{:T(128)}, f32[1,14,14,1]{2,1,3,0:T(8,128)S(1)}, ...), branch_computations={%region_126.127_spmd, %region_127.218_spmd} | conditional | flops 4724761600 | bytes 217511776 | solution.py:385
  350.2 29.2 %collective-permute-done.7 = bf16[1,14,14,768]{3,2,1,0:T(8,128)(2,1)S(1)} collective-permute-done((bf16[1,14,14,768]{3,2,1,0:T(8,128)(2,1)}, bf16[1,14,14,768]{3,2,1,0:T(8,128)(2,1)S(1)}, u32[]{:S(2)}, u32[]{:S(2)}) %collective-permute-start.7) | collective-permute-done | bytes 301088 | tf_op jit(solution)/shard_map/ppermute | solution.py:22
  380.4 22.4 %conditional.141 = (bf16[1,14,14,768]{3,2,1,0:T(8,128)(2,1)}, f32[3072,768]{1,0:T(8,128)}, f32[9,768]{1,0:T(8,128)}, f32[768]{0:T(1024)}, f32[768]{0:T(1024)}, /*index=5*/f32[768]{0:T(1024)}, f32[768,3072]{1,0:T(8,128)}) conditional(s32[]{:T(128)} %convert_element_type.2647, () %tuple.591, (s32[]{:T(128)}, f32[1,14,14,1]{2,1,3,0:T(8,128)S(1)}, ...), branch_computations={%region_218.219_spmd, %region_219.310_spmd} | conditional | flops 4724761600 | bytes 215263456 | solution.py:385
  405.9 6.2 collective-permute-done.8
  413.1 21.4 %conditional.142 = (bf16[1,14,14,768]{3,2,1,0:T(8,128)(2,1)}, f32[3072,768]{1,0:T(8,128)}, f32[9,768]{1,0:T(8,128)}, f32[768]{0:T(1024)}, f32[768]{0:T(1024)}, /*index=5*/f32[768]{0:T(1024)}, f32[768,3072]{1,0:T(8,128)}) conditional(s32[]{:T(128)} %convert_element_type.2653, () %tuple.593, (s32[]{:T(128)}, f32[1,14,14,1]{2,1,3,0:T(8,128)}, ...), branch_computations={%region_310.311_spmd, %region_311.402_spmd} | conditional | flops 4724761600 | bytes 217675104 | solution.py:385
  437.5 191.8 %collective-permute-done.9 = bf16[1,14,14,768]{3,2,1,0:T(8,128)(2,1)S(1)} collective-permute-done((bf16[1,14,14,768]{3,2,1,0:T(8,128)(2,1)}, bf16[1,14,14,768]{3,2,1,0:T(8,128)(2,1)S(1)}, u32[]{:S(2)}, u32[]{:S(2)}) %collective-permute-start.9) | collective-permute-done | bytes 301088 | tf_op jit(solution)/shard_map/ppermute | solution.py:22
  630.3 171.3 %conditional.143 = (bf16[1,14,14,768]{3,2,1,0:T(8,128)(2,1)}, f32[3072,768]{1,0:T(8,128)}, f32[9,768]{1,0:T(8,128)}, f32[768]{0:T(1024)}, f32[768]{0:T(1024)}, /*index=5*/f32[768]{0:T(1024)}, f32[768,3072]{1,0:T(8,128)}) conditional(s32[]{:T(128)} %convert_element_type.2659, () %tuple.595, (s32[]{:T(128)}, f32[1,14,14,1]{2,1,3,0:T(8,128)}, ...), branch_computations={%region_402.403_spmd, %region_403.494_spmd} | conditional | flops 4724761600 | bytes 217675104 | solution.py:385
  630.3 35.8 %conditional.157 = (f32[1,14,14,3072]{3,2,1,0:T(8,128)S(1)}, bf16[1,14,14,768]{3,2,1,0:T(8,128)(2,1)}) conditional(s32[]{:T(128)} %clamp.52, (f32[768]{0:T(1024)S(1)}, f32[1,14,14,768]{3,2,1,0:T(8,128)S(1)}, f32[1,14,14]{2,1,0:T(8,128)S(1)}, f32[9,768]{1,0:T(8,128)S(1)}, f32[768]{0:T(1024)S(1)}, ...), branch_computations={%region_404.408_spmd, %region_409.411_spmd, %region_412.416_spmd, ... | conditional | flops 929209536 | bytes 46372044
  667.6 124.4 %conditional.84 = (bf16[1,14,14,768]{3,2,1,0:T(8,128)(2,1)}, f32[768,3072]{0,1:T(8,128)}, f32[3072,768]{1,0:T(8,128)}, f32[9,768]{1,0:T(8,128)}, f32[768]{0:T(1024)}, /*index=5*/f32[768]{0:T(1024)}, f32[768]{0:T(1024)}) conditional(s32[]{:T(128)} %clamp.52, (f32[1,14,14,3072]{3,2,1,0:T(8,128)S(1)}, ...), branch_computations={%region_420.439_spmd, %region_440.456_spmd, %region_457.476_spmd, ... | conditional | flops 3795100416 | bytes 149564352 | solution.py:326
  750.3 5.1 convolution_bitcast_fusion.41
  755.5 7.2 pad_maximum_fusion.6
  792.0 9.6 copy.1040
  806.3 162.9 %conditional.144 = (bf16[1,14,14,768]{3,2,1,0:T(8,128)(2,1)}, f32[3072,768]{1,0:T(8,128)}, f32[9,768]{1,0:T(8,128)}, f32[768]{0:T(1024)}, f32[768]{0:T(1024)}, /*index=5*/f32[768]{0:T(1024)}, f32[768,3072]{1,0:T(8,128)}) conditional(s32[]{:T(128)} %convert_element_type.2665, () %tuple.597, (s32[]{:T(128)}, f32[1,14,14,1]{2,1,3,0:T(8,128)}, ...), branch_computations={%region_494.495_spmd, %region_495.586_spmd} | conditional | flops 4724761600 | bytes 217625824 | solution.py:385
  806.4 36.0 %conditional.158 = (f32[1,14,14,3072]{3,2,1,0:T(8,128)S(1)}, bf16[1,14,14,768]{3,2,1,0:T(8,128)(2,1)}) conditional(s32[]{:T(128)} %clamp.53, (f32[768]{0:T(1024)S(1)}, f32[1,14,14,768]{3,2,1,0:T(8,128)S(1)}, f32[1,14,14]{2,1,0:T(8,128)S(1)}, f32[9,768]{1,0:T(8,128)S(1)}, f32[768]{0:T(1024)S(1)}, ...), branch_computations={%region_496.500_spmd, %region_501.503_spmd, %region_504.508_spmd, ... | conditional | flops 929209536 | bytes 46372044
  843.8 115.3 %conditional.86 = (bf16[1,14,14,768]{3,2,1,0:T(8,128)(2,1)}, f32[768,3072]{0,1:T(8,128)}, f32[3072,768]{1,0:T(8,128)}, f32[9,768]{1,0:T(8,128)}, f32[768]{0:T(1024)}, /*index=5*/f32[768]{0:T(1024)}, f32[768]{0:T(1024)}) conditional(s32[]{:T(128)} %clamp.53, (f32[1,14,14,3072]{3,2,1,0:T(8,128)S(1)}, ...), branch_computations={%region_512.531_spmd, %region_532.548_spmd, %region_549.568_spmd, ... | conditional | flops 3795100416 | bytes 149515072 | solution.py:326
  926.3 5.2 convolution_bitcast_fusion.50
  931.6 7.2 pad_maximum_fusion.8
  959.1 9.6 copy.1042
  974.0 162.6 %conditional.145 = (bf16[1,14,14,768]{3,2,1,0:T(8,128)(2,1)}, f32[3072,768]{1,0:T(8,128)}, f32[9,768]{1,0:T(8,128)}, f32[768]{0:T(1024)}, f32[768]{0:T(1024)}, /*index=5*/f32[768]{0:T(1024)}, f32[768,3072]{1,0:T(8,128)}) conditional(s32[]{:T(128)} %convert_element_type.2670, () %tuple.599, (s32[]{:T(128)}, f32[1,14,14,1]{2,1,3,0:T(8,128)}, ...), branch_computations={%region_586.587_spmd, %region_587.678_spmd} | conditional | flops 4724761600 | bytes 217625824 | solution.py:385
  974.0 35.8 %conditional.159 = (f32[1,14,14,3072]{3,2,1,0:T(8,128)S(1)}, bf16[1,14,14,768]{3,2,1,0:T(8,128)(2,1)}) conditional(s32[]{:T(128)} %clamp.54, (f32[768]{0:T(1024)S(1)}, f32[1,14,14,768]{3,2,1,0:T(8,128)S(1)}, f32[1,14,14]{2,1,0:T(8,128)S(1)}, f32[9,768]{1,0:T(8,128)S(1)}, f32[768]{0:T(1024)S(1)}, ...), branch_computations={%region_588.592_spmd, %region_593.595_spmd, %region_596.600_spmd, ... | conditional | flops 929209536 | bytes 46372044
  1011.2 115.5 %conditional.88 = (bf16[1,14,14,768]{3,2,1,0:T(8,128)(2,1)}, f32[768,3072]{0,1:T(8,128)}, f32[3072,768]{1,0:T(8,128)}, f32[9,768]{1,0:T(8,128)}, f32[768]{0:T(1024)}, /*index=5*/f32[768]{0:T(1024)}, f32[768]{0:T(1024)}) conditional(s32[]{:T(128)} %clamp.54, (f32[1,14,14,3072]{3,2,1,0:T(8,128)S(1)}, ...), branch_computations={%region_604.623_spmd, %region_624.640_spmd, %region_641.660_spmd, ... | conditional | flops 3795100416 | bytes 149515072 | solution.py:326
  1094.0 5.1 convolution_bitcast_fusion.59
  1099.2 7.2 pad_maximum_fusion.10
  1126.8 9.7 copy.1044
  1140.4 147.8 %conditional.146 = (bf16[1,14,14,768]{3,2,1,0:T(8,128)(2,1)}, f32[3072,768]{1,0:T(8,128)}, f32[9,768]{1,0:T(8,128)}, f32[768]{0:T(1024)}, f32[768]{0:T(1024)}, /*index=5*/f32[768]{0:T(1024)}, f32[768,3072]{1,0:T(8,128)}) conditional(s32[]{:T(128)} %convert_element_type.2675, () %tuple.601, (s32[]{:T(128)}, f32[1,14,14,1]{2,1,3,0:T(8,128)S(1)}, ...), branch_computations={%region_678.679_spmd, %region_679.770_spmd} | conditional | flops 4724761600 | bytes 203406176 | solution.py:385
  1140.5 34.2 %conditional.160 = (f32[1,14,14,3072]{3,2,1,0:T(8,128)S(1)}, bf16[1,14,14,768]{3,2,1,0:T(8,128)(2,1)}) conditional(s32[]{:T(128)} %clamp.55, (f32[768]{0:T(1024)S(1)}, f32[1,14,14,768]{3,2,1,0:T(8,128)S(1)}, f32[1,14,14]{2,1,0:T(8,128)S(1)}, f32[9,768]{1,0:T(8,128)S(1)}, f32[768]{0:T(1024)S(1)}, ...), branch_computations={%region_680.684_spmd, %region_685.687_spmd, %region_688.692_spmd, ... | conditional | flops 929209536 | bytes 46372044
  1174.9 103.5 %conditional.90 = (bf16[1,14,14,768]{3,2,1,0:T(8,128)(2,1)}, f32[768,3072]{0,1:T(8,128)}, f32[3072,768]{1,0:T(8,128)}, f32[9,768]{1,0:T(8,128)}, f32[768]{0:T(1024)}, /*index=5*/f32[768]{0:T(1024)}, f32[768]{0:T(1024)}) conditional(s32[]{:T(128)} %clamp.55, (f32[1,14,14,3072]{3,2,1,0:T(8,128)S(1)}, ...), branch_computations={%region_696.715_spmd, %region_716.732_spmd, %region_733.752_spmd, ... | conditional | flops 3795100416 | bytes 134696448 | solution.py:326
  1179.4 6.0 reshape.14482
  1251.9 7.3 pad_maximum_fusion.12
  1278.5 9.6 copy.1046
  1288.3 26.7 %add_bitcast_fusion = f32[1,768,3072]{2,1,0:T(8,128)} fusion(f32[768,3072]{1,0:T(8,128)} %get-tuple-element.3389, f32[768,3072]{1,0:T(8,128)} %get-tuple-element.3381, f32[768,3072]{1,0:T(8,128)} %get-tuple-element.3373, f32[768,3072]{1,0:T(8,128)} %get-tuple-element.3365, f32[768,3072]{1,0:T(8,128)} %get-tuple-element.3357, ...), kind=kLoop, calls=%fused_computation.6819 | loop fusion | flops 14155776 | bytes 75497472 | tf_op jit(solution)/shard_map/broadcast_in_dim | solution.py:411
  1314.9 25.4 %add_add_fusion.56 = f32[3072,768]{1,0:T(8,128)} fusion(f32[3072,768]{1,0:T(8,128)} %get-tuple-element.2975, f32[3072,768]{1,0:T(8,128)} %get-tuple-element.2974, f32[3072,768]{1,0:T(8,128)} %get-tuple-element.2973, f32[3072,768]{1,0:T(8,128)} %get-tuple-element.2972, f32[3072,768]{1,0:T(8,128)} %get-tuple-element.2971, ...), kind=kLoop, calls=%fused_computation.6818 | loop fusion | flops 14155776 | bytes 75497472 | tf_op jit(solution)/shard_map/add | solution.py:386
  1362.4 17.4 all-to-all-done
  1380.6 529.9 %all-reduce.592.cloned.1.call-done = (f32[1,768,3072]{2,1,0:T(8,128)}, f32[3072,768]{1,0:T(8,128)}) async-done(((f32[1,768,3072]{2,1,0:T(8,128)}, f32[3072,768]{1,0:T(8,128)}), (f32[1,768,3072]{2,1,0:T(8,128)}, f32[3072,768]{1,0:T(8,128)})) %all-reduce.592.cloned.1.call-update) | async-done | bytes 18874384 | tf_op jit(solution)/shard_map/psum | solution.py:392
  1928.7 36.0 %all-reduce.588 = (f32[1,9,768]{2,0,1:T(1,128)}, f32[1,768]{1,0:T(1,128)}, f32[1,768]{1,0:T(1,128)}, f32[1,768]{1,0:T(1,128)}) all-reduce(f32[1,9,768]{2,0,1:T(1,128)S(1)} %broadcast_in_dim.1330, f32[1,768]{1,0:T(1,128)S(1)} %broadcast_in_dim.1331, ...), channel_id=1, replica_groups=mesh['dp'=8,'section'=4] {'dp'}, use_global_device_ids=true, to_apply=%region_772.773 | all-reduce | flops 9216 | bytes 73728 | tf_op jit(solution)/shard_map/psum | solution.py:392
  1966.1 5.7 slice_select_fusion
  1971.9 8.6 copy.1491
  (884 shorter events, 803.6 us)
Async XLA Ops:
  7.2 33.9 %all-gather.3.cloned.1.call-start = ((), (), s32[]{:S(2)}) async-start(), calls=%async_computation.2 | async-start | bytes 1720320 | tf_op jit(solution)/shard_map/all_gather | solution.py:293
  7.9 92.9 %all-gather.5.cloned.1.call-start = ((), (), s32[]{:S(2)}) async-start(), calls=%async_computation.3 | async-start | bytes 1720320 | tf_op jit(solution)/shard_map/all_gather | solution.py:294
  7.9 36.3 %collective-permute-start = (bf16[1536,768]{1,0:T(8,128)(2,1)}, bf16[1536,768]{1,0:T(8,128)(2,1)}, u32[]{:S(2)}, u32[]{:S(2)}) collective-permute-start(bf16[1536,768]{1,0:T(8,128)(2,1)} %param.131), channel_id=1, source_target_pairs={{0,1},{1,2},{2,3},{4,5},{5,6},{6,7},{8,9},{9,10},{10,11},{12,13},{... | collective-permute-start | bytes 7077896 | tf_op jit(solution)/shard_map/ppermute | solution.py:22
  11.8 1898.7 %all-reduce.592.cloned.1.call-start = ((), (), s32[]{:S(2)}) async-start(), calls=%async_computation.4 | async-start | bytes 37748736 | tf_op jit(solution)/shard_map/psum | solution.py:392
  23.1 15.7 copy-start.326
  23.8 15.7 copy-start.328
  24.4 15.2 copy-start.330
  25.0 14.6 copy-start.332
  25.7 13.9 copy-start.334
  26.3 13.2 copy-start.336
  27.0 12.6 copy-start.338
  27.6 11.9 copy-start.340
  28.3 11.3 copy-start.342
  29.0 10.7 copy-start.344
  29.7 10.0 copy-start.346
  31.0 16.6 copy-start.350
  31.7 16.0 copy-start.352
  99.5 4.3 collective-permute-start.1
  104.5 57.9 %copy-start.29 = (bf16[4,1,14,14,768]{4,3,2,0,1:T(8,128)(2,1)S(1)}, bf16[4,1,14,14,768]{4,3,2,0,1:T(8,128)(2,1)}, u32[]{:S(2)}) copy-start(bf16[4,1,14,14,768]{4,3,2,0,1:T(8,128)(2,1)} %copy-done.28) | copy-start | bytes 3612676
  161.1 3.3 collective-permute-start.2
  194.2 9.6 copy-start.111
  221.8 3.2 collective-permute-start.3
  275.0 3.2 collective-permute-start.4
  293.1 13.4 copy-start.180
  293.1 13.3 collective-permute-start.5
  318.3 5.9 collective-permute-start.6
  324.4 56.0 %copy-start.45 = (pred[1,14,14,768]{3,2,1,0:T(8,128)(4,1)}, pred[1,14,14,768]{3,2,1,0:T(8,128)(4,1)S(1)}, u32[]{:S(2)}) copy-start(pred[1,14,14,768]{3,2,1,0:T(8,128)(4,1)S(1)} %select_n.309) | copy-start | bytes 451588
  325.4 24.2 %copy-start.351 = (pred[14]{0:T(512)(128)(4,1)S(1)}, pred[14]{0:T(512)(128)(4,1)}, u32[]{:S(2)}) copy-start(pred[14]{0:T(512)(128)(4,1)} %copy-done.350) | copy-start | bytes 46
  325.4 24.2 %copy-start.353 = (pred[14]{0:T(512)(128)(4,1)S(1)}, pred[14]{0:T(512)(128)(4,1)}, u32[]{:S(2)}) copy-start(pred[14]{0:T(512)(128)(4,1)} %copy-done.352) | copy-start | bytes 46
  325.4 55.0 %copy-start.159 = (f32[1,14,14]{2,1,0:T(8,128)S(1)}, f32[1,14,14]{2,1,0:T(8,128)}, u32[]{:S(2)}) copy-start(f32[1,14,14]{2,1,0:T(8,128)} %and_convert_fusion.38) | copy-start | bytes 2356
  325.4 55.0 %copy-start.218 = (f32[1,14,14,1]{2,1,3,0:T(8,128)S(1)}, f32[1,14,14,1]{2,1,3,0:T(8,128)}, u32[]{:S(2)}) copy-start(f32[1,14,14,1]{2,1,3,0:T(8,128)} %and_convert_fusion.39) | copy-start | bytes 2356
  347.7 31.7 %collective-permute-start.7 = (bf16[1,14,14,768]{3,2,1,0:T(8,128)(2,1)}, bf16[1,14,14,768]{3,2,1,0:T(8,128)(2,1)S(1)}, u32[]{:S(2)}, u32[]{:S(2)}) collective-permute-start(bf16[1,14,14,768]{3,2,1,0:T(8,128)(2,1)} %get-tuple-element.2955), channel_id=1, source_target_pairs={{1,0},{2,1},{3,2},{5,4},{6,5},{7,6},{9,8},{10,9},{11,10},{13,12},{... | collective-permute-start | bytes 903176 | tf_op jit(solution)/shard_map/ppermute | solution.py:22
  380.3 32.7 %copy-start.158 = (f32[1,14,14]{2,1,0:T(8,128)S(1)}, f32[1,14,14]{2,1,0:T(8,128)}, u32[]{:S(2)}) copy-start(f32[1,14,14]{2,1,0:T(8,128)} %and_convert_fusion.36) | copy-start | bytes 2356
  402.7 9.4 collective-permute-start.8
  413.1 217.2 %copy-start.37 = (f32[1,14,14,768]{3,2,1,0:T(8,128)S(1)}, f32[1,14,14,768]{3,2,1,0:T(8,128)}, u32[]{:S(2)}) copy-start(f32[1,14,14,768]{3,2,1,0:T(8,128)} %get-tuple-element.5356) | copy-start | bytes 1806340
  413.1 217.2 %copy-start.160 = (f32[1,14,14]{2,1,0:T(8,128)S(1)}, f32[1,14,14]{2,1,0:T(8,128)}, u32[]{:S(2)}) copy-start(f32[1,14,14]{2,1,0:T(8,128)} %and_convert_fusion.34) | copy-start | bytes 2356
  434.4 194.9 %collective-permute-start.9 = (bf16[1,14,14,768]{3,2,1,0:T(8,128)(2,1)}, bf16[1,14,14,768]{3,2,1,0:T(8,128)(2,1)S(1)}, u32[]{:S(2)}, u32[]{:S(2)}) collective-permute-start(bf16[1,14,14,768]{3,2,1,0:T(8,128)(2,1)} %get-tuple-element.2957), channel_id=1, source_target_pairs={{1,0},{2,1},{3,2},{5,4},{6,5},{7,6},{9,8},{10,9},{11,10},{13,12},{... | collective-permute-start | bytes 903176 | tf_op jit(solution)/shard_map/ppermute | solution.py:22
  630.3 176.0 %copy-start.162 = (f32[1,14,14]{2,1,0:T(8,128)S(1)}, f32[1,14,14]{2,1,0:T(8,128)}, u32[]{:S(2)}) copy-start(f32[1,14,14]{2,1,0:T(8,128)} %and_convert_fusion.32) | copy-start | bytes 2356
  630.3 35.8 %copy-start.216 = (f32[1,14,14,1]{2,1,3,0:T(8,128)S(1)}, f32[1,14,14,1]{2,1,3,0:T(8,128)}, u32[]{:S(2)}) copy-start(f32[1,14,14,1]{2,1,3,0:T(8,128)} %get-tuple-element.2648) | copy-start | bytes 2356 | tf_op jit(solution)/shard_map/cond
  801.6 3.7 collective-permute-start.10
  806.4 36.0 %copy-start.219 = (f32[1,14,14,1]{2,1,3,0:T(8,128)S(1)}, f32[1,14,14,1]{2,1,3,0:T(8,128)}, u32[]{:S(2)}) copy-start(f32[1,14,14,1]{2,1,3,0:T(8,128)} %get-tuple-element.2730) | copy-start | bytes 2356 | tf_op jit(solution)/shard_map/cond
  969.2 3.8 collective-permute-start.11
  974.0 35.8 %copy-start.221 = (f32[1,14,14,1]{2,1,3,0:T(8,128)S(1)}, f32[1,14,14,1]{2,1,3,0:T(8,128)}, u32[]{:S(2)}) copy-start(f32[1,14,14,1]{2,1,3,0:T(8,128)} %get-tuple-element.2812) | copy-start | bytes 2356 | tf_op jit(solution)/shard_map/cond
  1136.6 3.8 collective-permute-start.12
  1140.5 34.2 %copy-start.46 = (pred[1,14,14,768]{3,2,1,0:T(8,128)(4,1)S(1)}, pred[1,14,14,768]{3,2,1,0:T(8,128)(4,1)}, u32[]{:S(2)}) copy-start(pred[1,14,14,768]{3,2,1,0:T(8,128)(4,1)} %get-tuple-element.2892) | copy-start | bytes 451588 | tf_op jit(solution)/shard_map/cond
  1358.3 21.5 %all-to-all-start = ((bf16[4,14,14,768]{3,2,1,0:T(8,128)(2,1)}), bf16[4,14,14,768]{3,2,1,0:T(8,128)(2,1)S(1)}, u32[]{:S(2)}, u32[]{:S(2)}) async-start(bf16[4,14,14,768]{3,2,1,0:T(8,128)(2,1)} %fusion.3704), calls=%async_computation | async-start | bytes 2752512 | tf_op jit(solution)/shard_map/all_to_all | solution.py:401
  1914.4 51.7 %collective-permute-start.13 = (bf16[1536,768]{1,0:T(8,128)(2,1)}, bf16[1536,768]{1,0:T(8,128)(2,1)}, u32[]{:S(2)}, u32[]{:S(2)}) collective-permute-start(bf16[1536,768]{1,0:T(8,128)(2,1)} %slice.10684), channel_id=1, source_target_pairs={{1,0},{2,1},{3,2},{5,4},{6,5},{7,6},{9,8},{10,9},{11,10},{13,12},{... | collective-permute-start | bytes 7077896 | tf_op jit(solution)/shard_map/ppermute | solution.py:22
  1921.9 42.7 %all-to-all-start.1 = ((bf16[4,14,14,768]{3,2,1,0:T(8,128)(2,1)}), bf16[4,14,14,768]{3,2,1,0:T(8,128)(2,1)S(1)}, u32[]{:S(2)}, u32[]{:S(2)}) async-start(bf16[4,14,14,768]{3,2,1,0:T(8,128)(2,1)} %fusion.3703), calls=%async_computation.1 | async-start | bytes 2752512 | tf_op jit(solution)/shard_map/all_to_all | solution.py:404
  (119 other events, 507.1 us)
Sparse Core Ops, SparseCore 0:
  9.6 21.4 all-gather.2
  32.6 22.0 all-gather.4
  1340.6 569.7 all-reduce.591
where the time goes:
time: 2000 us; the launch traced here: 1990 us
  waiting for transfers between devices  778 us (39%)
  local copies, waits for them, and re-layouts  484 us (24%)
  other arithmetic  221 us (11%)
  matrix products  216 us (11%)
  loops' own time  178 us (9%)
  starting transfers between devices  41.1 us (2%)
  blocking collectives  36 us (2%)
  between operations  33.2 us (2%)
    psum x1, waiting for transfers between devices, per_device(): lax.psum((grad_first, grad_second, grad_kernel, grad_bias, grad_gain, gra...  530 us
    ppermute x14, waiting for transfers between devices, shifted(): return lax.ppermute(block, axis, route)  230 us
    another operation x51, local copies, waits for them, and re-layouts  71.9 us
    another operation x4, loops' own time, backward_section(): lax.switch(section_id, backward_kinds, section_in, inside, normed_low, mi...  64.7 us
    sub x12, matrix products, window_parts(): attend = jax.nn.softmax(scores, axis=-1)  50.6 us
    another operation x7, loops' own time, per_device(): lax.cond(active, forward_section, spare_forward, section_in.astype(jnp.fl...  50.3 us
    convert_element_type x16, local copies, waits for them, and re-layouts, window_forward(): mixed = mixed.reshape(mixed.shape[0], WIN * WIN, D).astype(jnp.bfloat16)  45.7 us
  transfers between devices with their start and end apart: 19, of which 9 were waited for; matrix products, arithmetic and copies ran while one was open for 5% of the time, Pallas kernels for 0%

commit v1 on v0

v1 whole, which is shorter than its diff:
```python
from functools import partial

import jax
import jax.numpy as jnp
from jax import lax
from jax.experimental import pallas as pl
from jax.experimental.pallas import tpu as pltpu
from jax.sharding import PartitionSpec as P

D = 768
FF = 3072
HEADS = 24
HEAD = 32
WIN = 7
SIDE = 2
GRID = SIDE * WIN
CELL = 8
WROWS = WIN * CELL
HALF = GRID * CELL
ROWS = SIDE * HALF
GROUP = 256
PACK = GROUP // HEAD
NGROUP = D // GROUP
UNITS = NGROUP * SIDE * SIDE
LANE = 128
FTILE = 512
EPS = 1e-05
SCALE = HEAD ** (-0.5)
BF = jnp.bfloat16
F32 = jnp.float32
MESH = pl.DeviceIdType.MESH


def dot(a, b, ca=1, cb=0):
    return lax.dot_general(a, b, (((ca,), (cb,)), ((), ())), preferred_element_type=F32)


def lanes(index, width=LANE):
    return pl.ds(pl.multiple_of(index * width, width), width)


def halves(value):
    return value.reshape(SIDE, GRID, CELL, value.shape[-1])


def shifts(left, right):
    column = lax.broadcasted_iota(jnp.int32, left.shape, 1)
    before0 = pltpu.roll(left, 1, 1)
    after0 = jnp.where(column == WIN - 1, pltpu.roll(right, CELL - 2, 1), pltpu.roll(left, CELL - 1, 1))
    before1 = jnp.where(column == 0, pltpu.roll(left, 2, 1), pltpu.roll(right, 1, 1))
    after1 = pltpu.roll(right, CELL - 1, 1)
    return ((before0, left, after0), (before1, right, after1))


def gelu_parts(h):
    expo = jnp.exp(h * h * -0.5)
    t = 1.0 / (1.0 + (0.3275911 * 0.7071067811865476) * jnp.abs(h))
    poly = t * (0.127414796 + t * (-0.142248368 + t * (0.7107068705 + t * (-0.7265760135 + t * 0.5307027145))))
    tail = poly * expo
    phi = jnp.where(h >= 0, 1.0 - tail, tail)
    return h * phi, phi + h * expo * 0.3989422804014327


def front_forward(sec, m, ubuf, msk, pr, U, C, zb, xh, rs):
    zero = jnp.zeros((ROWS, LANE), F32)

    def conv(i, total):
        ls = lanes(i)
        u = ubuf[sec, m, :, ls].astype(F32)
        masked = halves(u * msk[m])
        U[0, 1 : GRID + 1, :, ls] = masked[0]
        U[1, 1 : GRID + 1, :, ls] = masked[1]
        moved = shifts(U[0, :, :, ls], U[1, :, :, ls])
        taps = pr[sec, :, ls]
        uh = halves(u)
        sums = []
        for wc in range(SIDE):
            acc = uh[wc] + taps[9:10, :][None]
            for a in range(3):
                for b in range(3):
                    acc = acc + moved[wc][b][a : a + GRID] * taps[3 * a + b : 3 * a + b + 1, :][None]
            acc = acc.reshape(HALF, LANE)
            C[pl.ds(wc * HALF, HALF), ls] = acc
            sums.append(acc)
        return total + jnp.concatenate(sums, axis=0)

    mean = jnp.sum(lax.fori_loop(0, D // LANE, conv, zero), axis=-1, keepdims=True) * (1.0 / D)

    def spread(i, total):
        centred = C[:, lanes(i)] - mean
        return total + centred * centred

    var = jnp.sum(lax.fori_loop(0, D // LANE, spread, zero), axis=-1, keepdims=True) * (1.0 / D)
    rstd = lax.rsqrt(var + EPS)
    rs[sec, m] = jnp.broadcast_to(rstd, (ROWS, LANE))

    def norm(i, carry):
        ls = lanes(i)
        xhat = (C[:, ls] - mean) * rstd
        xh[sec, m, :, ls] = xhat.astype(BF)
        zb[sec, m, :, ls] = (xhat * pr[sec, 10:11, ls] + pr[sec, 11:12, ls]).astype(BF)
        return carry

    lax.fori_loop(0, D // LANE, norm, 0)


def front_backward(sec, m, ubuf, msk, pr, U, T, gfull, xh, rs, sgp, out):
    zero = jnp.zeros((ROWS, LANE), F32)

    def fold(value):
        return jnp.sum(value.reshape(ROWS // CELL, CELL, LANE), axis=0)

    def sums(i, carry):
        s1, s2 = carry
        ls = lanes(i)
        dz = T[:, ls]
        xhat = xh[sec, m, :, ls].astype(F32)
        both = xhat * dz
        sgp[sec, 10, :, ls] += fold(both)
        sgp[sec, 11, :, ls] += fold(dz)
        gain = pr[sec, 10:11, ls]
        return s1 + dz * gain, s2 + both * gain

    s1, s2 = lax.fori_loop(0, D // LANE, sums, (zero, zero))
    m1 = jnp.sum(s1, axis=-1, keepdims=True) * (1.0 / D)
    m2 = jnp.sum(s2, axis=-1, keepdims=True) * (1.0 / D)

    def back(i, carry):
        ls = lanes(i)
        xhat = xh[sec, m, :, ls].astype(F32)
        inner = T[:, ls] * pr[sec, 10:11, ls] - m1 - xhat * m2
        gc = gfull[m, :, ls].astype(F32) + rs[sec, m] * inner
        sgp[sec, 9, :, ls] += fold(gc)
        gh = halves(gc)
        U[0, 1 : GRID + 1, :, ls] = gh[0]
        U[1, 1 : GRID + 1, :, ls] = gh[1]
        moved = shifts(U[0, :, :, ls], U[1, :, :, ls])
        taps = pr[sec, :, ls]
        mask = halves(msk[m])
        um = halves(ubuf[sec, m, :, ls].astype(F32) * msk[m])
        accs = [jnp.zeros((GRID, CELL, LANE), F32) for _ in range(SIDE)]
        for a in range(3):
            for b in range(3):
                tap = 3 * a + b
                kg = jnp.zeros((CELL, LANE), F32)
                for wc in range(SIDE):
                    gs = moved[wc][2 - b][2 - a : 2 - a + GRID]
                    accs[wc] = accs[wc] + gs * taps[tap : tap + 1, :][None]
                    kg = kg + jnp.sum(gs * um[wc], axis=0)
                sgp[sec, tap, :, ls] += kg
        du = [(gh[wc] + mask[wc] * accs[wc]).reshape(HALF, LANE) for wc in range(SIDE)]
        out[m, :, ls] = jnp.concatenate(du, axis=0).astype(BF)
        return carry

    lax.fori_loop(0, D // LANE, back, 0)


def spread_heads(value, head_of_lane):
    parts = [jnp.where(head_of_lane == h, value, 0.0) for h in range(PACK)]
    return jnp.concatenate(parts, axis=0).astype(BF)


def gather_heads(value, rows, head_of_lane):
    out = jnp.zeros((rows, GROUP), F32)
    for h in range(PACK):
        out = jnp.where(head_of_lane == h, value[h * rows : (h + 1) * rows], out)
    return out


def unit_slices(unit):
    window, group = unit // NGROUP, lax.rem(unit, NGROUP)
    rows = pl.ds(pl.multiple_of(window * WROWS, 8), WROWS)
    cols = [pl.ds(pl.multiple_of(part * D + group * GROUP, LANE), GROUP) for part in range(3)]
    return rows, cols


def window_forward(m, qkv, pw, T):
    def unit(i, carry):
        rows, cols = unit_slices(i)
        head_of_lane = lax.broadcasted_iota(jnp.int32, (WROWS, GROUP), 1) // HEAD
        q = qkv[m, rows, cols[0]].astype(BF)
        kd = spread_heads(qkv[m, rows, cols[1]], head_of_lane)
        vd = spread_heads(qkv[m, rows, cols[2]], head_of_lane)
        s = dot(kd, q, 1, 1) * SCALE
        s = s.reshape(PACK, WROWS, WROWS)
        key = lax.broadcasted_iota(jnp.int32, s.shape, 1)
        s = jnp.where(lax.rem(key, CELL) == WIN, -1e30, s)
        p = jnp.exp(s - jnp.max(s, axis=1, keepdims=True))
        p = p * (1.0 / jnp.sum(p, axis=1, keepdims=True))
        p = p.reshape(PACK * WROWS, WROWS)
        pw[m, i] = p
        T[rows, cols[0]] = dot(p.astype(BF), vd, 0, 0)
        return carry

    lax.fori_loop(0, UNITS, unit, 0)


def window_backward(m, qkv, pw, T, Q):
    def unit(i, carry):
        rows, cols = unit_slices(i)
        head_of_lane = lax.broadcasted_iota(jnp.int32, (WROWS, GROUP), 1) // HEAD
        q = qkv[m, rows, cols[0]].astype(BF)
        kd = spread_heads(qkv[m, rows, cols[1]], head_of_lane)
        vd = spread_heads(qkv[m, rows, cols[2]], head_of_lane)
        g = T[rows, cols[0]].astype(BF)
        p = pw[m, i]
        dp = dot(vd, g, 1, 1).reshape(PACK, WROWS, WROWS)
        pf = p.reshape(PACK, WROWS, WROWS)
        ds = pf * (dp - jnp.sum(pf * dp, axis=1, keepdims=True))
        ds = ds.reshape(PACK * WROWS, WROWS).astype(BF)
        Q[rows, cols[0]] = dot(ds, kd, 0, 0) * SCALE
        Q[rows, cols[1]] = gather_heads(dot(ds, q), WROWS, head_of_lane) * SCALE
        Q[rows, cols[2]] = gather_heads(dot(p.astype(BF), g), WROWS, head_of_lane)
        return carry

    lax.fori_loop(0, UNITS, unit, 0)


def group_slices(group):
    return [pl.ds(pl.multiple_of(part * D + group * GROUP, LANE), GROUP) for part in range(3)]


def channel_forward(m, qkv, pc, T, msk):
    def unit(i, carry):
        cols = group_slices(i)
        mask = msk[m][:, :1]
        q = qkv[m, :, cols[0]].astype(BF)
        k = (qkv[m, :, cols[1]] * mask).astype(BF)
        v = qkv[m, :, cols[2]].astype(BF)
        s = dot(q, k, 0, 0) * SCALE
        same = (lax.broadcasted_iota(jnp.int32, s.shape, 0) // HEAD) == (lax.broadcasted_iota(jnp.int32, s.shape, 1) // HEAD)
        s = jnp.where(same, s, -1e30)
        p = jnp.exp(s - jnp.max(s, axis=1, keepdims=True))
        p = p * (1.0 / jnp.sum(p, axis=1, keepdims=True))
        pc[m, i] = p
        T[:, cols[0]] = dot(v, p.astype(BF), 1, 1)
        return carry

    lax.fori_loop(0, NGROUP, unit, 0)


def channel_backward(m, qkv, pc, T, Q, msk):
    def unit(i, carry):
        cols = group_slices(i)
        mask = msk[m][:, :1]
        q = qkv[m, :, cols[0]].astype(BF)
        k = (qkv[m, :, cols[1]] * mask).astype(BF)
        v = qkv[m, :, cols[2]].astype(BF)
        g = T[:, cols[0]].astype(BF)
        p = pc[m, i]
        dp = dot(g, v, 0, 0)
        ds = (p * (dp - jnp.sum(p * dp, axis=1, keepdims=True))).astype(BF)
        Q[:, cols[0]] = dot(k, ds, 1, 1) * SCALE
        Q[:, cols[1]] = dot(q, ds) * (SCALE * mask)
        Q[:, cols[2]] = dot(g, p.astype(BF))
        return carry

    lax.fori_loop(0, NGROUP, unit, 0)


def relay_kernel(
    img, cot, msk, prm, first, second,
    act, ing, fa, fb, fr, f2, fg, sg_own, sg_mate,
    wf, w2, pr, ubuf, gin, gatt, gout, uout, zb, xh, rs, qkv, ob, ab, db, hb, dqk, pw, pc, U, C, T, Q, sgp, sgs,
    wl, ws, wr, pl_, usem, gsem, hs, ls, ss, rsem, es, er, sgsem,
):
    s = lax.axis_index("section")
    dp = lax.axis_index("dp")
    stage, c = s // 2, lax.rem(s, 2)
    mate = (dp, stage * 2 + (1 - c))
    opposite = (dp, (1 - stage) * 2 + c)
    early = stage == 0

    barrier = pltpu.get_barrier_semaphore()
    for peer in (mate, opposite):
        pl.semaphore_signal(barrier, inc=1, device_id=peer, device_id_type=MESH)
    pl.semaphore_wait(barrier, 2)

    def remote(src, dst, send, recv, peer):
        return pltpu.make_async_remote_copy(
            src_ref=src, dst_ref=dst, send_sem=send, recv_sem=recv, device_id=peer, device_id_type=MESH
        )

    half = second.shape[0]

    def weight_parts(k):
        parts = []
        for i in range(4):
            parts.append((first.at[:, pl.ds(i * D, D)], wf.at[k, :, pl.ds(i * D, D)]))
        parts.append((second, w2.at[pl.ds(k * half, half), :]))
        parts.append((prm, pr.at[k]))
        return parts

    def weight_copies(k):
        local = [pltpu.make_async_copy(a, b, wl.at[i]) for i, (a, b) in enumerate(weight_parts(k))]
        sent = [remote(a, b, ws.at[i], wr.at[i], mate) for i, (a, b) in enumerate(weight_parts(k))]
        return local, sent

    order = (5, 0, 1, 2, 3, 4)
    for k in range(2):

        @pl.when(c == k)
        def _():
            local, sent = weight_copies(k)
            for i in order:
                local[i].start()
                sent[i].start()

    def wait_weight(k, i):
        @pl.when(c == k)
        def _():
            weight_copies(k)[0][i].wait()

        @pl.when(c != k)
        def _():
            weight_copies(k)[1][i].wait_recv()

    img_out = remote(img, ubuf.at[0, 1], pl_.at[0], usem.at[1], opposite)
    cot_out = remote(cot, gin.at[0], pl_.at[1], gsem.at[0], opposite)

    @pl.when(early)
    def _():
        cot_out.start()
        ubuf[0, 0] = img[...]

    @pl.when(jnp.logical_not(early))
    def _():
        img_out.start()
        gin[1] = cot[...]

    for wc in range(SIDE):
        U[wc, 0] = jnp.zeros((CELL, D), F32)
        U[wc, GRID + 1] = jnp.zeros((CELL, D), F32)
    sgp[...] = jnp.zeros(sgp.shape, F32)

    def u_hop(m):
        return remote(uout.at[m], ubuf.at[0, m], hs.at[m], usem.at[m], opposite)

    def g_hop(m):
        return remote(gout.at[m], gin.at[m], hs.at[m], gsem.at[m], opposite)

    def factor_copies(k, m, local):
        slot = m if local else 2 + m
        rows = pl.ds(pl.multiple_of(slot * ROWS, 16), ROWS)
        if k == 0:
            parts = [
                ("F", zb.at[0, m], fa.at[rows, :]),
                ("F", ob.at[m], fb.at[rows, :]),
                ("F", ab.at[m, :, pl.ds(0, FF // 2)], f2.at[rows, :]),
                ("M", gin.at[m], fg.at[rows, :]),
                ("G", gatt.at[m], fr.at[rows, pl.ds(3 * D, D)]),
                ("A", dqk.at[m], fr.at[rows, pl.ds(0, 3 * D)]),
            ]
        else:
            parts = [
                ("F", zb.at[1, m], fa.at[rows, :]),
                ("F", ab.at[m, :, pl.ds(FF // 2, FF // 2)], f2.at[rows, :]),
                ("M", gin.at[m], fg.at[rows, :]),
                ("M", hb.at[m], fr.at[rows, :]),
            ]
        made = []
        for i, (when, src, dst) in enumerate(parts):
            if local:
                made.append((when, pltpu.make_async_copy(src, dst, ls.at[m, i])))
            else:
                made.append((when, remote(src, dst, ss.at[m, i], rsem.at[m, i], mate)))
        return made

    def start_factors(m, which):
        for k in range(2):
            for local in (True, False):

                @pl.when((c == k) if local else (c != k))
                def _():
                    for when, copy in factor_copies(k, m, local):
                        if when == which:
                            copy.start()

    def forward(m, p):
        @pl.when(jnp.logical_not(early))
        def _():
            u_hop(m).wait_recv()

        @pl.when(early & (m == 1))
        def _():
            img_out.wait_recv()

        once = p == 0

        def first_time(k, i):
            @pl.when(once)
            def _():
                wait_weight(k, i)

        first_time(0, 5)
        front_forward(0, m, ubuf, msk, pr, U, C, zb, xh, rs)
        for i in range(3):
            first_time(0, i)
            qkv[m, :, pl.ds(i * D, D)] = dot(zb[0, m], wf[0, :, pl.ds(i * D, D)]).astype(BF).astype(F32)

        @pl.when(early)
        def _():
            window_forward(m, qkv, pw, T)

        @pl.when(jnp.logical_not(early))
        def _():
            channel_forward(m, qkv, pc, T, msk)

        first_time(0, 3)
        ob[m] = T[...].astype(BF)
        ubuf[1, m] = (C[...] + dot(ob[m], wf[0, :, pl.ds(3 * D, D)])).astype(BF)

        first_time(1, 5)
        front_forward(1, m, ubuf, msk, pr, U, C, zb, xh, rs)
        for i in range(4):
            first_time(1, i)
        first_time(0, 4)
        first_time(1, 4)

        def mlp(t, carry):
            cols = lanes(t, FTILE)
            h = dot(zb[1, m], wf[1, :, cols])
            a, d = gelu_parts(h)
            a = a.astype(BF)
            ab[m, :, cols] = a
            db[m, :, cols] = d.astype(BF)
            C[...] += dot(a, w2[cols, :])
            return carry

        lax.fori_loop(0, FF // FTILE, mlp, 0)

        @pl.when(early)
        def _():
            uout[m] = C[...].astype(BF)
            u_hop(m).start()

        @pl.when(jnp.logical_not(early))
        def _():
            for l in range(D // LANE):
                cols = pl.ds(l * LANE, LANE)
                uout[m, :, cols] = (C[:, cols].astype(BF).astype(F32) * msk[m]).astype(BF)

        @pl.when(jnp.logical_not(early) & (m == 0))
        def _():
            remote(uout.at[0], act, es.at[0], er.at[0], opposite).start()

        @pl.when(jnp.logical_not(early) & (m == 1))
        def _():
            pltpu.make_async_copy(uout.at[1], act, es.at[0]).start()

        start_factors(m, "F")

    def backward(m):
        @pl.when(early)
        def _():
            g_hop(m).wait_recv()

        @pl.when(jnp.logical_not(early))
        def _():
            @pl.when(m == 0)
            def _():
                cot_out.wait_recv()

            for l in range(D // LANE):
                cols = pl.ds(l * LANE, LANE)
                gin[m, :, cols] = (gin[m, :, cols].astype(F32) * msk[m]).astype(BF)

        def mlp(t, carry):
            cols = lanes(t, FTILE)
            da = dot(gin[m], w2[cols, :], 1, 1)
            h = (da * db[m, :, cols].astype(F32)).astype(BF)
            hb[m, :, cols] = h
            part = dot(h, wf[1, :, cols], 1, 1)

            @pl.when(t == 0)
            def _():
                T[...] = part

            @pl.when(t > 0)
            def _():
                T[...] += part

            return carry

        lax.fori_loop(0, FF // FTILE, mlp, 0)
        start_factors(m, "M")
        front_backward(1, m, ubuf, msk, pr, U, T, gin, xh, rs, sgp, gatt)
        start_factors(m, "G")
        T[...] = dot(gatt[m], wf[0, :, pl.ds(3 * D, D)], 1, 1)

        @pl.when(early)
        def _():
            window_backward(m, qkv, pw, T, Q)

        @pl.when(jnp.logical_not(early))
        def _():
            channel_backward(m, qkv, pc, T, Q, msk)

        for i in range(3):
            cols = pl.ds(i * D, D)
            dqk[m, :, cols] = Q[:, cols].astype(BF)
        start_factors(m, "A")
        for i in range(3):
            cols = pl.ds(i * D, D)
            part = dot(dqk[m, :, cols], wf[0, :, cols], 1, 1)
            if i == 0:
                T[...] = part
            else:
                T[...] += part
        front_backward(0, m, ubuf, msk, pr, U, T, gatt, xh, rs, sgp, gout)

        @pl.when(jnp.logical_not(early))
        def _():
            g_hop(m).start()

        @pl.when(early & (m == 0))
        def _():
            pltpu.make_async_copy(gout.at[0], ing, es.at[1]).start()

        @pl.when(early & (m == 1))
        def _():
            remote(gout.at[1], ing, es.at[1], er.at[1], opposite).start()

    def phase(p, carry):
        m = jnp.where(early, lax.rem(p, 2), p // 2)
        ahead = jnp.where(early, p < 2, lax.rem(p, 2) == 0)

        @pl.when(ahead)
        def _():
            forward(m, p)

        @pl.when(jnp.logical_not(ahead))
        def _():
            backward(m)

        return carry

    lax.fori_loop(0, 4, phase, 0)

    for sec in range(2):
        for j in range(12):
            sgs[sec, j : j + 1, :] = jnp.sum(sgp[sec, j], axis=0, keepdims=True)
        sgs[sec, 12:16, :] = jnp.zeros((4, D), F32)
    keep = pltpu.make_async_copy(sgs.at[c], sg_own, sgsem.at[0])
    give = remote(sgs.at[1 - c], sg_mate, sgsem.at[1], sgsem.at[2], mate)
    keep.start()
    give.start()

    for k in range(2):

        @pl.when(c == k)
        def _():
            for copy in weight_copies(k)[1]:
                copy.wait_send()
            for m in range(2):
                for _when, copy in factor_copies(k, m, True):
                    copy.wait()
                for _when, copy in factor_copies(1 - k, m, False):
                    copy.wait_send()
                for _when, copy in factor_copies(k, m, False):
                    copy.wait_recv()

    keep.wait()
    give.wait()

    @pl.when(early)
    def _():
        cot_out.wait_send()
        for m in range(2):
            u_hop(m).wait_send()
        pltpu.make_async_copy(gout.at[0], ing, es.at[1]).wait()
        remote(gout.at[1], ing, es.at[1], er.at[1], opposite).wait_send()
        remote(uout.at[0], act, es.at[0], er.at[0], opposite).wait_recv()

    @pl.when(jnp.logical_not(early))
    def _():
        img_out.wait_send()
        for m in range(2):
            g_hop(m).wait_send()
        remote(uout.at[0], act, es.at[0], er.at[0], opposite).wait_send()
        pltpu.make_async_copy(uout.at[1], act, es.at[0]).wait()
        remote(gout.at[1], ing, es.at[1], er.at[1], opposite).wait_recv()


def relay(img, cot, msk, prm, first, second):
    shape = jax.ShapeDtypeStruct
    vmem = pl.BlockSpec(memory_space=pltpu.VMEM)
    anywhere = pl.BlockSpec(memory_space=pl.ANY)
    dma = pltpu.SemaphoreType.DMA
    image = (ROWS, D)
    return pl.pallas_call(
        relay_kernel,
        out_shape=[
            shape(image, BF),
            shape(image, BF),
            shape((4 * ROWS, D), BF),
            shape((4 * ROWS, D), BF),
            shape((4 * ROWS, FF), BF),
            shape((4 * ROWS, FF // 2), BF),
            shape((4 * ROWS, D), BF),
            shape((16, D), F32),
            shape((16, D), F32),
        ],
        in_specs=[vmem, vmem, vmem, vmem, anywhere, anywhere],
        out_specs=[anywhere] * 9,
        scratch_shapes=[
            pltpu.VMEM((2, D, FF), BF),
            pltpu.VMEM((FF, D), BF),
            pltpu.VMEM((2, 16, D), F32),
            pltpu.VMEM((2, 2) + image, BF),
            pltpu.VMEM((2,) + image, BF),
            pltpu.VMEM((2,) + image, BF),
            pltpu.VMEM((2,) + image, BF),
            pltpu.VMEM((2,) + image, BF),
            pltpu.VMEM((2, 2) + image, BF),
            pltpu.VMEM((2, 2) + image, BF),
            pltpu.VMEM((2, 2, ROWS, LANE), F32),
            pltpu.VMEM((2, ROWS, 3 * D), F32),
            pltpu.VMEM((2,) + image, BF),
            pltpu.VMEM((2, ROWS, FF), BF),
            pltpu.VMEM((2, ROWS, FF), BF),
            pltpu.VMEM((2, ROWS, FF), BF),
            pltpu.VMEM((2, ROWS, 3 * D), BF),
            pltpu.VMEM((2, UNITS, PACK * WROWS, WROWS), F32),
            pltpu.VMEM((2, NGROUP, GROUP, GROUP), F32),
            pltpu.VMEM((SIDE, GRID + 2, CELL, D), F32),
            pltpu.VMEM(image, F32),
            pltpu.VMEM(image, F32),
            pltpu.VMEM((ROWS, 3 * D), F32),
            pltpu.VMEM((2, 12, CELL, D), F32),
            pltpu.VMEM((2, 16, D), F32),
            dma((6,)),
            dma((6,)),
            dma((6,)),
            dma((2,)),
            dma((2,)),
            dma((2,)),
            dma((2,)),
            dma((2, 6)),
            dma((2, 6)),
            dma((2, 6)),
            dma((2,)),
            dma((2,)),
            dma((3,)),
        ],
        name="relay",
        compiler_params=pltpu.CompilerParams(
            collective_id=1, has_side_effects=True, vmem_limit_bytes=60 * 2**20
        ),
    )(img, cot, msk, prm, first, second)


RING = 8
COLS = FF // RING
TAIL = FF // 2 // RING


def ring_kernel(
    n, fa, fb, fr, f2, fg, sg_own, sg_mate,
    out1, out2, outs,
    la, r1, a2, g2, lt, at, buf, ag, acc, got,
    lsem, ss, rs, os_, sms, smr,
):
    s = lax.axis_index("section")
    dp = lax.axis_index("dp")
    c = lax.rem(s, 2)
    tokens = la.shape[1]

    def place(pos):
        pos = lax.rem(pos + 2 * n, n)
        return jnp.where(pos < n // 2, 2 * pos, 2 * (n - 1 - pos) + 1)

    me = jnp.where(lax.rem(dp, 2) == 0, dp // 2, n - 1 - dp // 2)
    nexts = (place(me + 1), place(me - 1))
    rounds = n.bit_length() - 1
    partners = []
    for r in range(rounds):
        bit = 1 << r
        partners.append(jnp.where(lax.rem(dp // bit, 2) == 0, dp + bit, dp - bit))

    barrier = pltpu.get_barrier_semaphore()
    peers = list(nexts) + partners
    for peer in peers:
        pl.semaphore_signal(barrier, inc=1, device_id=(peer, s), device_id_type=MESH)

    loads = [
        pltpu.make_async_copy(fa, la.at[0], lsem.at[0]),
        pltpu.make_async_copy(fr, r1, lsem.at[1]),
        pltpu.make_async_copy(f2, a2, lsem.at[2]),
        pltpu.make_async_copy(fg, g2, lsem.at[3]),
        pltpu.make_async_copy(fb, la.at[1], lsem.at[4]),
    ]
    for copy in loads[:4]:
        copy.start()

    @pl.when(c == 0)
    def _():
        loads[4].start()

    def turn(src, dst, count):
        def body(i, carry):
            dst[lanes(i), :] = src[:, lanes(i)].T
            return carry

        lax.fori_loop(0, count, body, 0)

    def shard(k):
        return lax.rem(k + 2 * n, n)

    def tile1(h, j):
        sel = jnp.where((c == 0) & (j >= (3 * n) // 4), 1, 0)
        return dot(lt[sel, pl.ds(h * COLS, COLS), :], r1[:, lanes(j, COLS)])

    def tile2(h, j):
        rows = pl.ds(pl.multiple_of(j * TAIL, 16), TAIL)
        return dot(at[rows, :], g2[:, pl.ds(h * COLS, COLS)])

    parts = (pl.ds(0, COLS), pl.ds(COLS, TAIL))
    tiles = (tile1, tile2)

    def scatter(h, t, sub):
        return pltpu.make_async_remote_copy(
            src_ref=buf.at[h, t, parts[sub], :],
            dst_ref=buf.at[h, t + 1, parts[sub], :],
            send_sem=ss.at[h, t, sub],
            recv_sem=rs.at[h, t + 1, sub],
            device_id=(nexts[h], s),
            device_id_type=MESH,
        )

    def spread(h, t, sub, j):
        return pltpu.make_async_remote_copy(
            src_ref=ag.at[h, j, parts[sub], :],
            dst_ref=ag.at[h, j, parts[sub], :],
            send_sem=ss.at[h, n - 1 + t, sub],
            recv_sem=rs.at[h, n + t, sub],
            device_id=(nexts[h], s),
            device_id_type=MESH,
        )

    def write(h, j, sub):
        cols = lanes(j, COLS)
        if sub == 0:
            dst = out1.at[pl.ds(h * COLS, COLS), cols]
        else:
            dst = out2.at[pl.ds(pl.multiple_of(j * TAIL, 16), TAIL), pl.ds(h * COLS, COLS)]
        return pltpu.make_async_copy(ag.at[h, j, parts[sub], :], dst, os_.at[h, j, sub])

    def sign(h):
        return 1 if h == 0 else -1

    loads[0].wait()
    turn(la.at[0], lt.at[0], D // LANE)

    @pl.when(c == 0)
    def _():
        loads[4].wait()
        turn(la.at[1], lt.at[1], D // LANE)

    loads[1].wait()
    pl.semaphore_wait(barrier, len(peers))
    for h in range(2):
        buf[h, 0, parts[0], :] = tile1(h, me).astype(BF)
        scatter(h, 0, 0).start()
    loads[2].wait()
    loads[3].wait()
    turn(a2, at, FF // 2 // LANE)
    for h in range(2):
        buf[h, 0, parts[1], :] = tile2(h, me).astype(BF)
        scatter(h, 0, 1).start()

    acc[0] = sg_own[...] + sg_mate[...]

    def reduce_step(t, carry):
        for sub in range(2):
            for h in range(2):
                own = tiles[sub](h, shard(me - sign(h) * t))
                scatter(h, t - 1, sub).wait_recv()
                buf[h, t, parts[sub], :] = (own + buf[h, t, parts[sub], :].astype(F32)).astype(BF)
                scatter(h, t, sub).start()
        return carry

    lax.fori_loop(1, n - 1, reduce_step, 0)

    def home(h, t):
        return shard(me + sign(h) - sign(h) * t)

    for sub in range(2):
        for h in range(2):
            j = home(h, 0)
            own = tiles[sub](h, j)
            scatter(h, n - 2, sub).wait_recv()
            ag[h, j, parts[sub], :] = (own + buf[h, n - 1, parts[sub], :].astype(F32)).astype(BF)
            spread(h, 0, sub, j).start()
            write(h, j, sub).start()

    def small(r):
        return pltpu.make_async_remote_copy(
            src_ref=acc.at[r],
            dst_ref=got.at[r],
            send_sem=sms.at[r],
            recv_sem=smr.at[r],
            device_id=(partners[r], s),
            device_id_type=MESH,
        )

    small(0).start()
    for t in range(1, n):
        for sub in range(2):
            for h in range(2):
                j = home(h, t)
                spread(h, t - 1, sub, j).wait_recv()
                if t < n - 1:
                    spread(h, t, sub, j).start()
                write(h, j, sub).start()
        if t % 2 == 0 and t // 2 <= rounds:
            r = t // 2 - 1
            small(r).wait_recv()
            acc[r + 1] = acc[r] + got[r]
            if r + 1 < rounds:
                small(r + 1).start()
    outs[...] = acc[rounds]

    def drain(t, carry):
        for sub in range(2):
            for h in range(2):
                scatter(h, t, sub).wait_send()
        return carry

    lax.fori_loop(0, n - 1, drain, 0)
    for t in range(n - 1):
        for sub in range(2):
            for h in range(2):
                spread(h, t, sub, home(h, t)).wait_send()
    for j in range(n):
        for sub in range(2):
            for h in range(2):
                write(h, j, sub).wait()
    for r in range(rounds):
        small(r).wait_send()


def ring_reduce(n, fa, fb, fr, f2, fg, sg_own, sg_mate):
    shape = jax.ShapeDtypeStruct
    vmem = pl.BlockSpec(memory_space=pltpu.VMEM)
    anywhere = pl.BlockSpec(memory_space=pl.ANY)
    dma = pltpu.SemaphoreType.DMA
    tokens = fa.shape[0]
    rounds = n.bit_length() - 1
    block = (COLS + TAIL, COLS)
    return pl.pallas_call(
        partial(ring_kernel, n),
        out_shape=[shape((D, FF), BF), shape((FF // 2, D), BF), shape((16, D), F32)],
        in_specs=[anywhere] * 5 + [vmem] * 2,
        out_specs=[anywhere, anywhere, vmem],
        scratch_shapes=[
            pltpu.VMEM((2, tokens, D), BF),
            pltpu.VMEM((tokens, FF), BF),
            pltpu.VMEM((tokens, FF // 2), BF),
            pltpu.VMEM((tokens, D), BF),
            pltpu.VMEM((2, D, tokens), BF),
            pltpu.VMEM((FF // 2, tokens), BF),
            pltpu.VMEM((2, n) + block, BF),
            pltpu.VMEM((2, n) + block, BF),
            pltpu.VMEM((rounds + 1, 16, D), F32),
            pltpu.VMEM((rounds, 16, D), F32),
            dma((5,)),
            dma((2, 2 * n, 2)),
            dma((2, 2 * n, 2)),
            dma((2, n, 2)),
            dma((rounds,)),
            dma((rounds,)),
        ],
        name="ring",
        compiler_params=pltpu.CompilerParams(
            collective_id=2, has_side_effects=True, vmem_limit_bytes=60 * 2**20
        ),
    )(fa, fb, fr, f2, fg, sg_own, sg_mate)


def plain_reduce(fa, fb, fr, f2, fg, sg_own, sg_mate):
    even = lax.rem(lax.axis_index("section"), 2) == 0
    left = jnp.where(even, fb, fa)
    qkv = dot(fa, fr[:, : 3 * D], 0, 0)
    last = dot(left, fr[:, 3 * D :], 0, 0)
    out1 = jnp.concatenate([qkv, last], axis=1)
    out2 = dot(f2, fg, 0, 0)
    return lax.psum((out1.astype(BF), out2.astype(BF), sg_own + sg_mate), "dp")


def to_rows(images):
    shaped = images.reshape(GRID, SIDE, WIN, images.shape[-1]).transpose(1, 0, 2, 3)
    return jnp.pad(shaped, ((0, 0), (0, 0), (0, CELL - WIN), (0, 0))).reshape(ROWS, images.shape[-1])


def from_rows(rows):
    shaped = rows.reshape(SIDE, GRID, CELL, rows.shape[-1])[:, :, :WIN].transpose(1, 0, 2, 3)
    return shaped.reshape(1, GRID, GRID, rows.shape[-1])


def masks(window_rows, window_cols, c):
    places = jnp.stack([c, c + 2])
    height = (WIN * window_rows[places])[:, None]
    width = (WIN * window_cols[places])[:, None]
    index = jnp.arange(ROWS)[None, :]
    row = (index % HALF) // CELL
    cell = index % CELL
    column = (index // HALF) * WIN + cell
    inside = (row < height) & (column < width) & (cell < WIN)
    return jnp.broadcast_to(inside.astype(F32)[:, :, None], (2, ROWS, LANE))


def per_device(
    images, cotangent, window_rows, window_cols, pos_kernel, pos_bias, norm_gain, norm_shift, first_weight, second_weight
):
    s = lax.axis_index("section")
    prm = jnp.concatenate(
        [pos_kernel[0], pos_bias, norm_gain, norm_shift, jnp.zeros((4, D), pos_bias.dtype)], axis=0
    ).astype(F32)
    msk = masks(window_rows, window_cols, lax.rem(s, 2))
    act, ing, fa, fb, fr, f2, fg, sg_own, sg_mate = relay(
        to_rows(images), to_rows(cotangent), msk, prm, first_weight[0], second_weight
    )
    n = lax.axis_size("dp")
    reduce = partial(ring_reduce, n) if n == RING else plain_reduce
    out1, out2, outs = reduce(fa, fb, fr, f2, fg, sg_own, sg_mate)
    return (
        from_rows(act),
        from_rows(ing).astype(F32),
        out1.astype(F32)[None],
        out2.astype(F32),
        outs[None, :9],
        outs[9:10],
        outs[10:11],
        outs[11:12],
    )


def solution(mesh):
    in_specs = (
        P(("dp", "section"), None, None, None),
        P(("dp", "section"), None, None, None),
        P("dp"),
        P("dp"),
        P("section", None, None),
        P("section", None),
        P("section", None),
        P("section", None),
        P("section", None, None),
        P("section", None),
    )
    out_specs = (
        P(("dp", "section"), None, None, None),
        P(("dp", "section"), None, None, None),
        P("section", None, None),
        P("section", None),
        P("section", None, None),
        P("section", None),
        P("section", None),
        P("section", None),
    )
    return jax.shard_map(per_device, mesh=mesh, in_specs=in_specs, out_specs=out_specs, check_vma=False)
```

time: 2000 us -> 279 us (0.14)
  waiting for transfers between devices: 778 us -> 0 us
  local copies, waits for them, and re-layouts: 484 us -> 10.8 us
  Pallas kernels: 0 us -> 256 us
  matrix products: 216 us -> 0 us
  other arithmetic: 221 us -> 11 us
  loops' own time: 178 us -> 0 us
  starting transfers between devices: 41.1 us -> 0 us
  blocking collectives: 36 us -> 0 us
  between operations: 33.2 us -> 0.78 us
    psum x1 -> x0, waiting for transfers between devices: 530 us -> none  [per_device(): lax.psum((grad_first, grad_second, grad_kernel, grad_bias, grad_gain, gra...]
    pallas_call x0 -> x2, Pallas kernels: none -> 256 us  [the longest x1 147 us: ring_reduce(): pl.pallas_call(partial(ring_kernel, n), out_shape=[shape((D, FF), BF), sh...]
    ppermute x14 -> x0, waiting for transfers between devices: 230 us -> none  [shifted(): return lax.ppermute(block, axis, route)]
    dot_general x52 -> x0, matrix products: 165 us -> none  [the longest x8 31 us: outer(): lax.dot_general(former, latter, (((0, 1, 2), (0, 1, 2)), ((), ())), prefe...]
    another operation x18 -> x0, loops' own time: 145 us -> none  [the longest x4 64.7 us: backward_section(): lax.switch(section_id, backward_kinds, section_in, inside, normed_low, mi...]
    reshape x36 -> x0, local copies, waits for them, and re-layouts: 89.7 us -> none  [the longest x12 40 us: to_windows(): return shaped.reshape(number * SIDE * SIDE, WIN * WIN, channels)]
    slice x66 -> x1, local copies, waits for them, and re-layouts: 88.3 us -> 0.59 us  [per_device(): outs[11:12]]
    another operation x51 -> x0, local copies, waits for them, and re-layouts: 71.9 us -> none
  transfers between devices with their start and end apart: 19 -> 0, of which waited for: 9 -> 0; matrix products, arithmetic and copies ran while one was open for 5% -> 0% of each run, Pallas kernels for 0% -> 0%
where the time goes in v1:
time: 279 us
  Pallas kernels  256 us (92%)
  other arithmetic  11 us (4%)
  local copies, waits for them, and re-layouts  10.8 us (4%)
    pallas_call x1, Pallas kernels, ring_reduce(): pl.pallas_call(partial(ring_kernel, n), out_shape=[shape((D, FF), BF), sh...  147 us
    pallas_call x1, Pallas kernels, relay(): pl.pallas_call(relay_kernel, out_shape=[shape(image, BF), shape(image, BF...  109 us
    broadcast_in_dim x1, other arithmetic, per_device(): out1.astype(F32)[None]  7.52 us
    unnamed x26, local copies, waits for them, and re-layouts  5.87 us

profile of v1, /device:TPU:0, one launch (start us, length us, event | category | flops | bytes accessed | tf_op | source)
XLA Modules:
  0.0 278.7 jit_solution(2264718849027539169)
XLA Ops:
  0.6 0.0 copy-start
  0.6 0.0 copy-start.5
  0.7 0.0 copy-start.6
  0.7 0.0 copy-start.7
  0.7 0.0 copy-start.8
  0.7 0.1 fusion.3
  0.8 0.5 copy-done
  1.3 0.6 gather_fusion
  1.9 1.3 gather_fusion.1
  3.3 0.1 and_convert_fusion
  3.3 0.8 broadcast_in_dim.11.msk
  4.2 1.1 copy.23
  5.2 0.1 copy.34
  5.3 0.8 pad.7.clone
  6.1 1.1 copy.25
  7.2 0.1 copy.35
  7.3 0.8 pad.8.clone
  8.1 0.0 copy-done.5
  8.1 0.0 copy-done.6
  8.1 0.0 copy-done.7
  8.1 0.0 copy-done.8
  8.2 0.6 convert_element_type.35.prm
  8.8 109.1 %relay.1 = (bf16[224,768]{1,0:T(8,128)(2,1)}, bf16[224,768]{1,0:T(8,128)(2,1)}, bf16[896,768]{1,0:T(8,128)(2,1)}, bf16[896,768]{1,0:T(8,128)(2,1)}, bf16[896,307...) custom-call(bf16[224,768]{1,0:T(8,128)(2,1)} %bitcast.31, ...), custom_call_target="tpu_custom_call" | custom-call | tf_op jit(solution)/shard_map/relay/pallas_call | solution.py:591
  117.9 147.0 %ring.1 = (bf16[768,3072]{1,0:T(8,128)(2,1)}, bf16[1536,768]{1,0:T(8,128)(2,1)}, f32[16,768]{1,0:T(8,128)}) custom-call(bf16[896,768]{1,0:T(8,128)(2,1)} %get-tuple-element.22.fa, bf16[896,768]{1,0:T(8,128)(2,1)} %get-tuple-element.23.fb, bf16[896,3072]{1,0:T(8,128)(2,1)} %get-tuple-element.24.fr, bf16[896,1536]{1,0:T(8,128)(2,1)} %get-tuple-element.25.f2, ...), custom_call_target="tpu_custom_call" | custom-call | tf_op jit(solution)/shard_map/ring/pallas_call | solution.py:851
  264.9 0.0 copy-start.1
  264.9 7.5 %bitcast_convert_fusion = f32[1,768,3072]{2,1,0:T(8,128)} fusion(bf16[768,3072]{1,0:T(8,128)(2,1)} %get-tuple-element.29), kind=kLoop, calls=%fused_computation.2 | loop fusion | flops 2359296 | bytes 14155776 | tf_op jit(solution)/shard_map/broadcast_in_dim | solution.py:930
  272.4 0.0 copy-start.4
  272.4 0.0 copy-start.3
  272.4 0.0 copy-done.1
  272.4 0.0 copy-start.2
  272.4 2.5 convert_element_type.39
  275.0 0.0 copy-done.4
  275.0 0.6 copy.31
  275.6 0.6 fusion.4
  276.2 0.0 copy-done.3
  276.2 0.1 copy_convert_fusion
  276.3 1.4 copy.30
  277.8 0.0 copy-done.2
  277.8 0.1 copy.32
  277.8 0.8 copy.29
  (7 shorter events, 0.1 us)
Async XLA Ops:
  0.6 0.7 copy-start
  0.6 7.5 %copy-start.5 = (bf16[1,9,768]{2,1,0:T(8,128)(2,1)S(1)}, bf16[1,9,768]{2,1,0:T(8,128)(2,1)}, u32[]{:S(2)}) copy-start(bf16[1,9,768]{2,1,0:T(8,128)(2,1)} %param.14) | copy-start | bytes 41476
  0.7 7.5 %copy-start.6 = (bf16[1,768]{1,0:T(2,128)(2,1)S(1)}, bf16[1,768]{1,0:T(2,128)(2,1)}, u32[]{:S(2)}) copy-start(bf16[1,768]{1,0:T(2,128)(2,1)} %param.15) | copy-start | bytes 4612
  0.7 7.5 %copy-start.7 = (bf16[1,768]{1,0:T(2,128)(2,1)S(1)}, bf16[1,768]{1,0:T(2,128)(2,1)}, u32[]{:S(2)}) copy-start(bf16[1,768]{1,0:T(2,128)(2,1)} %param.16) | copy-start | bytes 4612
  0.7 7.5 %copy-start.8 = (bf16[1,768]{1,0:T(2,128)(2,1)S(1)}, bf16[1,768]{1,0:T(2,128)(2,1)}, u32[]{:S(2)}) copy-start(bf16[1,768]{1,0:T(2,128)(2,1)} %param.17) | copy-start | bytes 4612
  264.9 7.5 %copy-start.1 = (bf16[1536,768]{1,0:T(8,128)(2,1)S(1)}, bf16[1536,768]{1,0:T(8,128)(2,1)}, u32[]{:S(2)}) copy-start(bf16[1536,768]{1,0:T(8,128)(2,1)} %get-tuple-element.30) | copy-start | bytes 7077892
  272.4 2.6 copy-start.4
  272.4 3.8 %copy-start.3 = (bf16[224,768]{1,0:T(8,128)(2,1)S(1)}, bf16[224,768]{1,0:T(8,128)(2,1)}, u32[]{:S(2)}) copy-start(bf16[224,768]{1,0:T(8,128)(2,1)} %get-tuple-element.21) | copy-start | bytes 1032196
  272.4 5.3 %copy-start.2 = (bf16[224,768]{1,0:T(8,128)(2,1)S(1)}, bf16[224,768]{1,0:T(8,128)(2,1)}, u32[]{:S(2)}) copy-start(bf16[224,768]{1,0:T(8,128)(2,1)} %get-tuple-element.20) | copy-start | bytes 1032196

commit v2 on v1

--- a/solution.py
+++ b/solution.py
@@ -23,7 +23,7 @@
 NGROUP = D // GROUP
 UNITS = NGROUP * SIDE * SIDE
 LANE = 128
-FTILE = 512
+FTILE = 1024
 EPS = 1e-05
 SCALE = HEAD ** (-0.5)
 BF = jnp.bfloat16
@@ -168,52 +168,60 @@
 
 
 def unit_slices(unit):
-    window, group = unit // NGROUP, lax.rem(unit, NGROUP)
-    rows = pl.ds(pl.multiple_of(window * WROWS, 8), WROWS)
+    pair, group = unit // NGROUP, lax.rem(unit, NGROUP)
+    rows = [pl.ds(pl.multiple_of((2 * pair + w) * WROWS, 8), WROWS) for w in range(2)]
     cols = [pl.ds(pl.multiple_of(part * D + group * GROUP, LANE), GROUP) for part in range(3)]
     return rows, cols
 
 
+def window_parts(m, i, qkv):
+    rows, cols = unit_slices(i)
+    head_of_lane = lax.broadcasted_iota(jnp.int32, (WROWS, GROUP), 1) // HEAD
+    q = [qkv[m, r, cols[0]].astype(BF) for r in rows]
+    kd = [spread_heads(qkv[m, r, cols[1]], head_of_lane) for r in rows]
+    vd = [spread_heads(qkv[m, r, cols[2]], head_of_lane) for r in rows]
+    return rows, cols, head_of_lane, q, kd, vd
+
+
 def window_forward(m, qkv, pw, T):
     def unit(i, carry):
-        rows, cols = unit_slices(i)
-        head_of_lane = lax.broadcasted_iota(jnp.int32, (WROWS, GROUP), 1) // HEAD
-        q = qkv[m, rows, cols[0]].astype(BF)
-        kd = spread_heads(qkv[m, rows, cols[1]], head_of_lane)
-        vd = spread_heads(qkv[m, rows, cols[2]], head_of_lane)
-        s = dot(kd, q, 1, 1) * SCALE
-        s = s.reshape(PACK, WROWS, WROWS)
-        key = lax.broadcasted_iota(jnp.int32, s.shape, 1)
-        s = jnp.where(lax.rem(key, CELL) == WIN, -1e30, s)
-        p = jnp.exp(s - jnp.max(s, axis=1, keepdims=True))
-        p = p * (1.0 / jnp.sum(p, axis=1, keepdims=True))
-        p = p.reshape(PACK * WROWS, WROWS)
-        pw[m, i] = p
-        T[rows, cols[0]] = dot(p.astype(BF), vd, 0, 0)
+        rows, cols, head_of_lane, q, kd, vd = window_parts(m, i, qkv)
+        s = [(dot(b, a, 1, 1) * SCALE).reshape(PACK, WROWS, WROWS) for a, b in zip(q, kd)]
+        key = lax.broadcasted_iota(jnp.int32, s[0].shape, 1)
+        real = lax.rem(key, CELL) < WIN
+        s = [jnp.where(real, x, -1e30) for x in s]
+        p = [jnp.exp(x - jnp.max(x, axis=1, keepdims=True)) for x in s]
+        p = [x * (1.0 / jnp.sum(x, axis=1, keepdims=True)) for x in p]
+        p = [x.reshape(PACK * WROWS, WROWS) for x in p]
+        for w in range(2):
+            pw[m, 2 * i + w] = p[w]
+        out = [dot(x.astype(BF), v, 0, 0) for x, v in zip(p, vd)]
+        for w in range(2):
+            T[rows[w], cols[0]] = out[w]
         return carry
 
-    lax.fori_loop(0, UNITS, unit, 0)
+    lax.fori_loop(0, UNITS // 2, unit, 0)
 
 
 def window_backward(m, qkv, pw, T, Q):
     def unit(i, carry):
-        rows, cols = unit_slices(i)
-        head_of_lane = lax.broadcasted_iota(jnp.int32, (WROWS, GROUP), 1) // HEAD
-        q = qkv[m, rows, cols[0]].astype(BF)
-        kd = spread_heads(qkv[m, rows, cols[1]], head_of_lane)
-        vd = spread_heads(qkv[m, rows, cols[2]], head_of_lane)
-        g = T[rows, cols[0]].astype(BF)
-        p = pw[m, i]
-        dp = dot(vd, g, 1, 1).reshape(PACK, WROWS, WROWS)
-        pf = p.reshape(PACK, WROWS, WROWS)
-        ds = pf * (dp - jnp.sum(pf * dp, axis=1, keepdims=True))
-        ds = ds.reshape(PACK * WROWS, WROWS).astype(BF)
-        Q[rows, cols[0]] = dot(ds, kd, 0, 0) * SCALE
-        Q[rows, cols[1]] = gather_heads(dot(ds, q), WROWS, head_of_lane) * SCALE
-        Q[rows, cols[2]] = gather_heads(dot(p.astype(BF), g), WROWS, head_of_lane)
+        rows, cols, head_of_lane, q, kd, vd = window_parts(m, i, qkv)
+        g = [T[r, cols[0]].astype(BF) for r in rows]
+        p = [pw[m, 2 * i + w].reshape(PACK, WROWS, WROWS) for w in range(2)]
+        dp = [dot(v, x, 1, 1).reshape(PACK, WROWS, WROWS) for v, x in zip(vd, g)]
+        ds = [x * (y - jnp.sum(x * y, axis=1, keepdims=True)) for x, y in zip(p, dp)]
+        ds = [x.reshape(PACK * WROWS, WROWS).astype(BF) for x in ds]
+        pb = [x.reshape(PACK * WROWS, WROWS).astype(BF) for x in p]
+        dv = [gather_heads(dot(x, y), WROWS, head_of_lane) for x, y in zip(pb, g)]
+        dk = [gather_heads(dot(x, y), WROWS, head_of_lane) * SCALE for x, y in zip(ds, q)]
+        dq = [dot(x, y, 0, 0) * SCALE for x, y in zip(ds, kd)]
+        for w in range(2):
+            Q[rows[w], cols[0]] = dq[w]
+            Q[rows[w], cols[1]] = dk[w]
+            Q[rows[w], cols[2]] = dv[w]
         return carry
 
-    lax.fori_loop(0, UNITS, unit, 0)
+    lax.fori_loop(0, UNITS // 2, unit, 0)
 
 
 def group_slices(group):
@@ -236,7 +244,7 @@
         T[:, cols[0]] = dot(v, p.astype(BF), 1, 1)
         return carry
 
-    lax.fori_loop(0, NGROUP, unit, 0)
+    lax.fori_loop(0, NGROUP, unit, 0, unroll=True)
 
 
 def channel_backward(m, qkv, pc, T, Q, msk):
@@ -255,13 +263,13 @@
         Q[:, cols[2]] = dot(g, p.astype(BF))
         return carry
 
-    lax.fori_loop(0, NGROUP, unit, 0)
+    lax.fori_loop(0, NGROUP, unit, 0, unroll=True)
 
 
 def relay_kernel(
-    img, cot, msk, prm, first, second,
+    wrows, wcols, img, cot, kern, bias, gain, move, first, second,
     act, ing, fa, fb, fr, f2, fg, sg_own, sg_mate,
-    wf, w2, pr, ubuf, gin, gatt, gout, uout, zb, xh, rs, qkv, ob, ab, db, hb, dqk, pw, pc, U, C, T, Q, sgp, sgs,
+    wf, w2, pr, msk, raw, flat, ubuf, gin, gatt, gout, uout, zb, xh, rs, qkv, ob, ab, db, hb, dqk, pw, pc, U, C, T, Q, sgp, sgs,
     wl, ws, wr, pl_, usem, gsem, hs, ls, ss, rsem, es, er, sgsem,
 ):
     s = lax.axis_index("section")
@@ -288,7 +296,6 @@
         for i in range(4):
             parts.append((first.at[:, pl.ds(i * D, D)], wf.at[k, :, pl.ds(i * D, D)]))
         parts.append((second, w2.at[pl.ds(k * half, half), :]))
-        parts.append((prm, pr.at[k]))
         return parts
 
     def weight_copies(k):
@@ -296,37 +303,68 @@
         sent = [remote(a, b, ws.at[i], wr.at[i], mate) for i, (a, b) in enumerate(weight_parts(k))]
         return local, sent
 
-    order = (5, 0, 1, 2, 3, 4)
+    def params_copy(k):
+        return remote(pr.at[k], pr.at[k], ws.at[5], wr.at[5], mate)
+
+    pr[c, 0:9, :] = kern[...].astype(F32)
+    pr[c, 9:10, :] = bias[...].astype(F32)
+    pr[c, 10:11, :] = gain[...].astype(F32)
+    pr[c, 11:12, :] = move[...].astype(F32)
+    params_copy(c).start()
     for k in range(2):
 
         @pl.when(c == k)
         def _():
             local, sent = weight_copies(k)
-            for i in order:
+            for i in range(5):
                 local[i].start()
                 sent[i].start()
 
     def wait_weight(k, i):
-        @pl.when(c == k)
-        def _():
-            weight_copies(k)[0][i].wait()
+        if i < 5:
+
+            @pl.when(c == k)
+            def _():
+                weight_copies(k)[0][i].wait()
 
         @pl.when(c != k)
         def _():
-            weight_copies(k)[1][i].wait_recv()
-
-    img_out = remote(img, ubuf.at[0, 1], pl_.at[0], usem.at[1], opposite)
-    cot_out = remote(cot, gin.at[0], pl_.at[1], gsem.at[0], opposite)
+            (weight_copies(k)[1][i] if i < 5 else params_copy(k)).wait_recv()
+
+    img_out = remote(img, raw, pl_.at[0], pl_.at[1], opposite)
+    cot_out = remote(cot, raw, pl_.at[0], pl_.at[1], opposite)
+
+    def pad(src, dst):
+        blank = jnp.zeros((CELL - WIN, D), F32)
+        for r in range(GRID):
+            line = src[r].astype(F32)
+            for wc in range(SIDE):
+                cells = jnp.concatenate([line[wc * WIN : (wc + 1) * WIN], blank], axis=0)
+                C[pl.ds(wc * HALF + r * CELL, CELL), :] = cells
+        dst[...] = C[...].astype(BF)
+
+    def unpad(dst):
+        for r in range(GRID):
+            sides = [C[pl.ds(wc * HALF + r * CELL, CELL), :][:WIN] for wc in range(SIDE)]
+            dst[r] = jnp.concatenate(sides, axis=0).astype(BF)
 
     @pl.when(early)
     def _():
         cot_out.start()
-        ubuf[0, 0] = img[...]
+        pad(img, ubuf.at[0, 0])
 
     @pl.when(jnp.logical_not(early))
     def _():
         img_out.start()
-        gin[1] = cot[...]
+        pad(cot, gin.at[1])
+
+    index = lax.broadcasted_iota(jnp.int32, (ROWS, LANE), 0)
+    cell = lax.rem(index, CELL)
+    row = lax.rem(index, HALF) // CELL
+    column = (index // HALF) * WIN + cell
+    for m in range(2):
+        inside = (row < WIN * wrows[c + 2 * m]) & (column < WIN * wcols[c + 2 * m]) & (cell < WIN)
+        msk[m] = jnp.where(inside, 1.0, 0.0)
 
     for wc in range(SIDE):
         U[wc, 0] = jnp.zeros((CELL, D), F32)
@@ -384,6 +422,7 @@
         @pl.when(early & (m == 1))
         def _():
             img_out.wait_recv()
+            pad(raw, ubuf.at[0, 1])
 
         once = p == 0
 
@@ -417,36 +456,31 @@
         first_time(0, 4)
         first_time(1, 4)
 
-        def mlp(t, carry):
-            cols = lanes(t, FTILE)
-            h = dot(zb[1, m], wf[1, :, cols])
-            a, d = gelu_parts(h)
-            a = a.astype(BF)
-            ab[m, :, cols] = a
+        for t in range(FF // FTILE):
+            cols = pl.ds(t * FTILE, FTILE)
+            a, d = gelu_parts(dot(zb[1, m], wf[1, :, cols]))
+            ab[m, :, cols] = a.astype(BF)
             db[m, :, cols] = d.astype(BF)
-            C[...] += dot(a, w2[cols, :])
-            return carry
-
-        lax.fori_loop(0, FF // FTILE, mlp, 0)
+        uout[m] = (C[...] + dot(ab[m], w2[...])).astype(BF)
 
         @pl.when(early)
         def _():
-            uout[m] = C[...].astype(BF)
             u_hop(m).start()
 
         @pl.when(jnp.logical_not(early))
         def _():
             for l in range(D // LANE):
                 cols = pl.ds(l * LANE, LANE)
-                uout[m, :, cols] = (C[:, cols].astype(BF).astype(F32) * msk[m]).astype(BF)
+                C[:, cols] = uout[m, :, cols].astype(F32) * msk[m]
+            unpad(flat.at[m])
 
         @pl.when(jnp.logical_not(early) & (m == 0))
         def _():
-            remote(uout.at[0], act, es.at[0], er.at[0], opposite).start()
+            remote(flat.at[0], act, es.at[0], er.at[0], opposite).start()
 
         @pl.when(jnp.logical_not(early) & (m == 1))
         def _():
-            pltpu.make_async_copy(uout.at[1], act, es.at[0]).start()
+            pltpu.make_async_copy(flat.at[1], act, es.at[0]).start()
 
         start_factors(m, "F")
 
@@ -460,29 +494,17 @@
             @pl.when(m == 0)
             def _():
                 cot_out.wait_recv()
+                pad(raw, gin.at[0])
 
             for l in range(D // LANE):
                 cols = pl.ds(l * LANE, LANE)
                 gin[m, :, cols] = (gin[m, :, cols].astype(F32) * msk[m]).astype(BF)
 
-        def mlp(t, carry):
-            cols = lanes(t, FTILE)
+        for t in range(FF // FTILE):
+            cols = pl.ds(t * FTILE, FTILE)
             da = dot(gin[m], w2[cols, :], 1, 1)
-            h = (da * db[m, :, cols].astype(F32)).astype(BF)
-            hb[m, :, cols] = h
-            part = dot(h, wf[1, :, cols], 1, 1)
-
-            @pl.when(t == 0)
-            def _():
-                T[...] = part
-
-            @pl.when(t > 0)
-            def _():
-                T[...] += part
-
-            return carry
-
-        lax.fori_loop(0, FF // FTILE, mlp, 0)
+            hb[m, :, cols] = (da * db[m, :, cols].astype(F32)).astype(BF)
+        T[...] = dot(hb[m], wf[1], 1, 1)
         start_factors(m, "M")
         front_backward(1, m, ubuf, msk, pr, U, T, gin, xh, rs, sgp, gatt)
         start_factors(m, "G")
@@ -500,26 +522,25 @@
             cols = pl.ds(i * D, D)
             dqk[m, :, cols] = Q[:, cols].astype(BF)
         start_factors(m, "A")
-        for i in range(3):
-            cols = pl.ds(i * D, D)
-            part = dot(dqk[m, :, cols], wf[0, :, cols], 1, 1)
-            if i == 0:
-                T[...] = part
-            else:
-                T[...] += part
+        T[...] = dot(dqk[m], wf[0, :, pl.ds(0, 3 * D)], 1, 1)
         front_backward(0, m, ubuf, msk, pr, U, T, gatt, xh, rs, sgp, gout)
 
         @pl.when(jnp.logical_not(early))
         def _():
             g_hop(m).start()
 
+        @pl.when(early)
+        def _():
+            C[...] = gout[m].astype(F32)
+            unpad(flat.at[m])
+
         @pl.when(early & (m == 0))
         def _():
-            pltpu.make_async_copy(gout.at[0], ing, es.at[1]).start()
+            pltpu.make_async_copy(flat.at[0], ing, es.at[1]).start()
 
         @pl.when(early & (m == 1))
         def _():
-            remote(gout.at[1], ing, es.at[1], er.at[1], opposite).start()
+            remote(flat.at[1], ing, es.at[1], er.at[1], opposite).start()
 
     def phase(p, carry):
         m = jnp.where(early, lax.rem(p, 2), p // 2)
@@ -552,6 +573,7 @@
         def _():
             for copy in weight_copies(k)[1]:
                 copy.wait_send()
+            params_copy(k).wait_send()
             for m in range(2):
                 for _when, copy in factor_copies(k, m, True):
                     copy.wait()
@@ -568,31 +590,33 @@
         cot_out.wait_send()
         for m in range(2):
             u_hop(m).wait_send()
-        pltpu.make_async_copy(gout.at[0], ing, es.at[1]).wait()
-        remote(gout.at[1], ing, es.at[1], er.at[1], opposite).wait_send()
-        remote(uout.at[0], act, es.at[0], er.at[0], opposite).wait_recv()
+        pltpu.make_async_copy(flat.at[0], ing, es.at[1]).wait()
+        remote(flat.at[1], ing, es.at[1], er.at[1], opposite).wait_send()
+        remote(flat.at[0], act, es.at[0], er.at[0], opposite).wait_recv()
 
     @pl.when(jnp.logical_not(early))
     def _():
         img_out.wait_send()
         for m in range(2):
             g_hop(m).wait_send()
-        remote(uout.at[0], act, es.at[0], er.at[0], opposite).wait_send()
-        pltpu.make_async_copy(uout.at[1], act, es.at[0]).wait()
-        remote(gout.at[1], ing, es.at[1], er.at[1], opposite).wait_recv()
-
-
-def relay(img, cot, msk, prm, first, second):
+        remote(flat.at[0], act, es.at[0], er.at[0], opposite).wait_send()
+        pltpu.make_async_copy(flat.at[1], act, es.at[0]).wait()
+        remote(flat.at[1], ing, es.at[1], er.at[1], opposite).wait_recv()
+
+
+def relay(wrows, wcols, img, cot, kern, bias, gain, move, first, second):
     shape = jax.ShapeDtypeStruct
     vmem = pl.BlockSpec(memory_space=pltpu.VMEM)
     anywhere = pl.BlockSpec(memory_space=pl.ANY)
     dma = pltpu.SemaphoreType.DMA
+    smem = pl.BlockSpec(memory_space=pltpu.SMEM)
     image = (ROWS, D)
+    slot = img.shape
     return pl.pallas_call(
         relay_kernel,
         out_shape=[
-            shape(image, BF),
-            shape(image, BF),
+            shape(slot, BF),
+            shape(slot, BF),
             shape((4 * ROWS, D), BF),
             shape((4 * ROWS, D), BF),
             shape((4 * ROWS, FF), BF),
@@ -601,12 +625,15 @@
             shape((16, D), F32),
             shape((16, D), F32),
         ],
-        in_specs=[vmem, vmem, vmem, vmem, anywhere, anywhere],
+        in_specs=[smem] * 2 + [vmem] * 6 + [anywhere] * 2,
         out_specs=[anywhere] * 9,
         scratch_shapes=[
             pltpu.VMEM((2, D, FF), BF),
             pltpu.VMEM((FF, D), BF),
             pltpu.VMEM((2, 16, D), F32),
+            pltpu.VMEM((2, ROWS, LANE), F32),
+            pltpu.VMEM(slot, BF),
+            pltpu.VMEM((2,) + slot, BF),
             pltpu.VMEM((2, 2) + image, BF),
             pltpu.VMEM((2,) + image, BF),
             pltpu.VMEM((2,) + image, BF),
@@ -647,7 +674,7 @@
         compiler_params=pltpu.CompilerParams(
             collective_id=1, has_side_effects=True, vmem_limit_bytes=60 * 2**20
         ),
-    )(img, cot, msk, prm, first, second)
+    )(wrows, wcols, img, cot, kern, bias, gain, move, first, second)
 
 
 RING = 8
@@ -888,45 +915,19 @@
     return lax.psum((out1.astype(BF), out2.astype(BF), sg_own + sg_mate), "dp")
 
 
-def to_rows(images):
-    shaped = images.reshape(GRID, SIDE, WIN, images.shape[-1]).transpose(1, 0, 2, 3)
-    return jnp.pad(shaped, ((0, 0), (0, 0), (0, CELL - WIN), (0, 0))).reshape(ROWS, images.shape[-1])
-
-
-def from_rows(rows):
-    shaped = rows.reshape(SIDE, GRID, CELL, rows.shape[-1])[:, :, :WIN].transpose(1, 0, 2, 3)
-    return shaped.reshape(1, GRID, GRID, rows.shape[-1])
-
-
-def masks(window_rows, window_cols, c):
-    places = jnp.stack([c, c + 2])
-    height = (WIN * window_rows[places])[:, None]
-    width = (WIN * window_cols[places])[:, None]
-    index = jnp.arange(ROWS)[None, :]
-    row = (index % HALF) // CELL
-    cell = index % CELL
-    column = (index // HALF) * WIN + cell
-    inside = (row < height) & (column < width) & (cell < WIN)
-    return jnp.broadcast_to(inside.astype(F32)[:, :, None], (2, ROWS, LANE))
-
-
 def per_device(
     images, cotangent, window_rows, window_cols, pos_kernel, pos_bias, norm_gain, norm_shift, first_weight, second_weight
 ):
-    s = lax.axis_index("section")
-    prm = jnp.concatenate(
-        [pos_kernel[0], pos_bias, norm_gain, norm_shift, jnp.zeros((4, D), pos_bias.dtype)], axis=0
-    ).astype(F32)
-    msk = masks(window_rows, window_cols, lax.rem(s, 2))
     act, ing, fa, fb, fr, f2, fg, sg_own, sg_mate = relay(
-        to_rows(images), to_rows(cotangent), msk, prm, first_weight[0], second_weight
+        window_rows, window_cols, images[0], cotangent[0], pos_kernel[0], pos_bias, norm_gain, norm_shift,
+        first_weight[0], second_weight,
     )
     n = lax.axis_size("dp")
     reduce = partial(ring_reduce, n) if n == RING else plain_reduce
     out1, out2, outs = reduce(fa, fb, fr, f2, fg, sg_own, sg_mate)
     return (
-        from_rows(act),
-        from_rows(ing).astype(F32),
+        act[None],
+        ing.astype(F32)[None],
         out1.astype(F32)[None],
         out2.astype(F32),
         outs[None, :9],

time: 279 us -> 261 us (0.935)
  Pallas kernels: 256 us -> 246 us
  local copies, waits for them, and re-layouts: 10.8 us -> 3.42 us
    pallas_call x1, Pallas kernels: 109 us -> 101 us  [relay(): pl.pallas_call(relay_kernel, out_shape=[shape(slot, BF), shape(slot, BF),...]
    unnamed x26 -> x11, local copies, waits for them, and re-layouts: 5.87 us -> 2.82 us
where the time goes in v2:
time: 261 us; the launch traced here: 260 us
  Pallas kernels  246 us (94%)
  other arithmetic  10.1 us (4%)
  local copies, waits for them, and re-layouts  3.42 us (1%)
    pallas_call x1, Pallas kernels, ring_reduce(): pl.pallas_call(partial(ring_kernel, n), out_shape=[shape((D, FF), BF), sh...  145 us
    pallas_call x1, Pallas kernels, relay(): pl.pallas_call(relay_kernel, out_shape=[shape(slot, BF), shape(slot, BF),...  101 us
    broadcast_in_dim x1, other arithmetic, per_device(): out1.astype(F32)[None]  7.52 us

profile of v2, /device:TPU:0, one launch (start us, length us, event | category | flops | bytes accessed | tf_op | source)
XLA Modules:
  0.0 260.3 jit_solution(14221431114414240747)
XLA Ops:
  0.6 101.3 %relay.1 = (bf16[14,14,768]{2,1,0:T(8,128)(2,1)}, bf16[14,14,768]{2,1,0:T(8,128)(2,1)}, bf16[896,768]{1,0:T(8,128)(2,1)}, bf16[896,768]{1,0:T(8,128)(2,1)}, bf16...) custom-call(s32[4]{0:T(128)} %wrows.1, s32[4]{0:T(128)} %wcols.1, ...), custom_call_target="tpu_custom_call" | custom-call | tf_op jit(solution)/shard_map/relay/pallas_call | solution.py:615
  101.9 144.9 %ring.1 = (bf16[768,3072]{1,0:T(8,128)(2,1)}, bf16[1536,768]{1,0:T(8,128)(2,1)}, f32[16,768]{1,0:T(8,128)}) custom-call(bf16[896,768]{1,0:T(8,128)(2,1)} %get-tuple-element.22.fa, bf16[896,768]{1,0:T(8,128)(2,1)} %get-tuple-element.23.fb, bf16[896,3072]{1,0:T(8,128)(2,1)} %get-tuple-element.24.fr, bf16[896,1536]{1,0:T(8,128)(2,1)} %get-tuple-element.25.f2, ...), custom_call_target="tpu_custom_call" | custom-call | tf_op jit(solution)/shard_map/ring/pallas_call | solution.py:878
  246.8 0.0 copy-start
  246.8 7.5 %bitcast_convert_fusion = f32[1,768,3072]{2,1,0:T(8,128)} fusion(bf16[768,3072]{1,0:T(8,128)(2,1)} %get-tuple-element.29), kind=kLoop, calls=%fused_computation | loop fusion | flops 2359296 | bytes 14155776 | tf_op jit(solution)/shard_map/broadcast_in_dim | solution.py:931
  254.3 0.0 copy-start.3
  254.3 0.0 copy-start.2
  254.3 0.0 copy-done
  254.3 0.0 copy-start.1
  254.3 2.5 convert_element_type.2
  256.9 0.0 copy-done.3
  256.9 0.6 copy.19
  257.5 0.6 fusion
  258.1 0.0 copy-done.2
  258.1 0.1 bitcast_convert_fusion.1
  258.2 1.4 copy.18
  259.6 0.0 copy-done.1
  259.6 0.7 copy.21
  (1 shorter events, 0.0 us)
Async XLA Ops:
  246.8 7.5 %copy-start = (bf16[1536,768]{1,0:T(8,128)(2,1)S(1)}, bf16[1536,768]{1,0:T(8,128)(2,1)}, u32[]{:S(2)}) copy-start(bf16[1536,768]{1,0:T(8,128)(2,1)} %get-tuple-element.30) | copy-start | bytes 7077892
  254.3 2.6 copy-start.3
  254.3 3.8 %copy-start.2 = (bf16[14,14,768]{2,1,0:T(8,128)(2,1)S(1)}, bf16[14,14,768]{2,1,0:T(8,128)(2,1)}, u32[]{:S(2)}) copy-start(bf16[14,14,768]{2,1,0:T(8,128)(2,1)} %get-tuple-element.21) | copy-start | bytes 903172
  254.3 5.3 %copy-start.1 = (bf16[14,14,768]{2,1,0:T(8,128)(2,1)S(1)}, bf16[14,14,768]{2,1,0:T(8,128)(2,1)}, u32[]{:S(2)}) copy-start(bf16[14,14,768]{2,1,0:T(8,128)(2,1)} %get-tuple-element.20) | copy-start | bytes 903172

commit v3 on v2

--- a/solution.py
+++ b/solution.py
@@ -61,7 +61,7 @@
     return h * phi, phi + h * expo * 0.3989422804014327
 
 
-def front_forward(sec, m, ubuf, msk, pr, U, C, zb, xh, rs):
+def front_forward(sec, m, ubuf, msk, pr, U, C, zz, xh, rs):
     zero = jnp.zeros((ROWS, LANE), F32)
 
     def conv(i, total):
@@ -98,7 +98,7 @@
         ls = lanes(i)
         xhat = (C[:, ls] - mean) * rstd
         xh[sec, m, :, ls] = xhat.astype(BF)
-        zb[sec, m, :, ls] = (xhat * pr[sec, 10:11, ls] + pr[sec, 11:12, ls]).astype(BF)
+        zz[m, 2 * sec, :, ls] = (xhat * pr[sec, 10:11, ls] + pr[sec, 11:12, ls]).astype(BF)
         return carry
 
     lax.fori_loop(0, D // LANE, norm, 0)
@@ -129,7 +129,7 @@
         ls = lanes(i)
         xhat = xh[sec, m, :, ls].astype(F32)
         inner = T[:, ls] * pr[sec, 10:11, ls] - m1 - xhat * m2
-        gc = gfull[m, :, ls].astype(F32) + rs[sec, m] * inner
+        gc = gfull(i)[...].astype(F32) + rs[sec, m] * inner
         sgp[sec, 9, :, ls] += fold(gc)
         gh = halves(gc)
         U[0, 1 : GRID + 1, :, ls] = gh[0]
@@ -149,7 +149,7 @@
                     kg = kg + jnp.sum(gs * um[wc], axis=0)
                 sgp[sec, tap, :, ls] += kg
         du = [(gh[wc] + mask[wc] * accs[wc]).reshape(HALF, LANE) for wc in range(SIDE)]
-        out[m, :, ls] = jnp.concatenate(du, axis=0).astype(BF)
+        out(i)[...] = jnp.concatenate(du, axis=0).astype(BF)
         return carry
 
     lax.fori_loop(0, D // LANE, back, 0)
@@ -266,12 +266,20 @@
     lax.fori_loop(0, NGROUP, unit, 0, unroll=True)
 
 
+RING = 8
+COLS = FF // RING
+TAIL = FF // 2 // RING
+EARLY = 2
+
+
 def relay_kernel(
     wrows, wcols, img, cot, kern, bias, gain, move, first, second,
-    act, ing, fa, fb, fr, f2, fg, sg_own, sg_mate,
-    wf, w2, pr, msk, raw, flat, ubuf, gin, gatt, gout, uout, zb, xh, rs, qkv, ob, ab, db, hb, dqk, pw, pc, U, C, T, Q, sgp, sgs,
-    wl, ws, wr, pl_, usem, gsem, hs, ls, ss, rsem, es, er, sgsem,
+    act, ing, out1, out2, outs,
+    wf, w2, pr, msk, raw, flat, ubuf, gin, gout, uout, zz, xh, rs, qkv, ab, rr, pw, pc, U, C, T, Q, sgp, sgs, sgm,
+    rL, rR, rA, rG, buf, acc, got,
+    wl, ws, wr, pl_, usem, gsem, us, gs, ss, rsem, es, er, sgsem, ssem, rcem, osem, sms, smr, free,
 ):
+    n = RING
     s = lax.axis_index("section")
     dp = lax.axis_index("dp")
     stage, c = s // 2, lax.rem(s, 2)
@@ -279,10 +287,26 @@
     opposite = (dp, (1 - stage) * 2 + c)
     early = stage == 0
 
+    spot = lax.rem(dp, n)
+    base = dp - spot
+    me = jnp.where(lax.rem(spot, 2) == 0, spot // 2, n - 1 - spot // 2)
+
+    def place(pos):
+        pos = lax.rem(pos + 2 * n, n)
+        return (base + jnp.where(pos < n // 2, 2 * pos, 2 * (n - 1 - pos) + 1), s)
+
+    nexts = (place(me + 1), place(me - 1))
+    rounds = n.bit_length() - 1
+    partners = []
+    for r in range(rounds):
+        bit = 1 << r
+        partners.append((jnp.where(lax.rem(spot // bit, 2) == 0, dp + bit, dp - bit), s))
+
     barrier = pltpu.get_barrier_semaphore()
-    for peer in (mate, opposite):
+    peers = [mate, opposite, *nexts, *partners]
+    for peer in peers:
         pl.semaphore_signal(barrier, inc=1, device_id=peer, device_id_type=MESH)
-    pl.semaphore_wait(barrier, 2)
+    pl.semaphore_wait(barrier, len(peers))
 
     def remote(src, dst, send, recv, peer):
         return pltpu.make_async_remote_copy(
@@ -372,47 +396,153 @@
     sgp[...] = jnp.zeros(sgp.shape, F32)
 
     def u_hop(m):
-        return remote(uout.at[m], ubuf.at[0, m], hs.at[m], usem.at[m], opposite)
+        return remote(uout.at[m], ubuf.at[0, m], us.at[m], usem.at[m], opposite)
 
     def g_hop(m):
-        return remote(gout.at[m], gin.at[m], hs.at[m], gsem.at[m], opposite)
-
-    def factor_copies(k, m, local):
-        slot = m if local else 2 + m
-        rows = pl.ds(pl.multiple_of(slot * ROWS, 16), ROWS)
+        return remote(gout.at[m], gin.at[m], gs.at[m], gsem.at[m], opposite)
+
+    def factor_copies(k, m):
         if k == 0:
             parts = [
-                ("F", zb.at[0, m], fa.at[rows, :]),
-                ("F", ob.at[m], fb.at[rows, :]),
-                ("F", ab.at[m, :, pl.ds(0, FF // 2)], f2.at[rows, :]),
-                ("M", gin.at[m], fg.at[rows, :]),
-                ("G", gatt.at[m], fr.at[rows, pl.ds(3 * D, D)]),
-                ("A", dqk.at[m], fr.at[rows, pl.ds(0, 3 * D)]),
+                ("F", zz.at[m, 0], rL.at[m, 0]),
+                ("F", zz.at[m, 1], rL.at[m, 1]),
+                ("F", ab.at[m, :, pl.ds(0, FF // 2)], rA.at[m]),
+                ("M", gin.at[m], rG.at[m]),
+                ("G", rr.at[m, 0, :, pl.ds(3 * D, D)], rR.at[m, :, pl.ds(3 * D, D)]),
+                ("A", rr.at[m, 0, :, pl.ds(0, 3 * D)], rR.at[m, :, pl.ds(0, 3 * D)]),
             ]
         else:
             parts = [
-                ("F", zb.at[1, m], fa.at[rows, :]),
-                ("F", ab.at[m, :, pl.ds(FF // 2, FF // 2)], f2.at[rows, :]),
-                ("M", gin.at[m], fg.at[rows, :]),
-                ("M", hb.at[m], fr.at[rows, :]),
+                ("F", zz.at[m, 2], rL.at[m, 0]),
+                ("F", ab.at[m, :, pl.ds(FF // 2, FF // 2)], rA.at[m]),
+                ("M", gin.at[m], rG.at[m]),
+                ("M", rr.at[m, 1], rR.at[m]),
             ]
-        made = []
-        for i, (when, src, dst) in enumerate(parts):
-            if local:
-                made.append((when, pltpu.make_async_copy(src, dst, ls.at[m, i])))
-            else:
-                made.append((when, remote(src, dst, ss.at[m, i], rsem.at[m, i], mate)))
-        return made
+        return [(w, remote(a, b, ss.at[m, i], rsem.at[m, i], mate)) for i, (w, a, b) in enumerate(parts)]
 
     def start_factors(m, which):
         for k in range(2):
-            for local in (True, False):
-
-                @pl.when((c == k) if local else (c != k))
+
+            @pl.when(c != k)
+            def _():
+                for when, copy in factor_copies(k, m):
+                    if when == which:
+                        copy.start()
+
+    def wait_factors(which):
+        for k in range(2):
+
+            @pl.when(c == k)
+            def _():
+                for m in range(2):
+                    for when, copy in factor_copies(k, m):
+                        if when in which:
+                            copy.wait_recv()
+
+    def shard(k):
+        return lax.rem(k + 4 * n, n)
+
+    def sign(h):
+        return 1 if h == 0 else -1
+
+    def home(h, t):
+        return shard(me + sign(h) - sign(h) * t)
+
+    def tile(sub, h, j):
+        side = pl.ds(h * COLS, COLS)
+        if sub == 0:
+            last = jnp.where(j >= (3 * n) // 4, 1, 0)
+            own = jnp.where(c == 1, 2, last)
+            other = jnp.where(c == 1, 0, last)
+            cols = lanes(j, COLS)
+            terms = [(zz.at[m, own, :, side], rr.at[m, c, :, cols]) for m in range(2)]
+            terms += [(rL.at[m, other, :, side], rR.at[m, :, cols]) for m in range(2)]
+        else:
+            mine = pl.ds(pl.multiple_of(c * (FF // 2) + (j // 2) * 2 * TAIL, LANE), 2 * TAIL)
+            cols = lanes(j // 2, 2 * TAIL)
+            terms = [(ab.at[m, :, mine], gin.at[m, :, side]) for m in range(2)]
+            terms += [(rA.at[m, :, cols], rG.at[m, :, side]) for m in range(2)]
+        total = None
+        for a, b in terms:
+            part = dot(a[...], b[...], 0, 0)
+            total = part if total is None else total + part
+        if sub == 1:
+            total = jnp.where(lax.rem(j, 2) == 1, total[TAIL:], total[:TAIL])
+        return total
+
+    parts = (pl.ds(0, COLS), pl.ds(COLS, TAIL))
+
+    def gathered(sub, h, j):
+        if sub == 0:
+            return wf.at[0, pl.ds(h * COLS, COLS), lanes(j, COLS)]
+        return w2.at[pl.ds(pl.multiple_of(j * TAIL, 16), TAIL), pl.ds(h * COLS, COLS)]
+
+    def scatter(h, t, sub):
+        src, dst = buf.at[h, t, parts[sub], :], buf.at[h, t + 1, parts[sub], :]
+        return remote(src, dst, ssem.at[h, t, sub], rcem.at[h, t + 1, sub], nexts[h])
+
+    def spread(h, t, sub, j):
+        ref = gathered(sub, h, j)
+        return remote(ref, ref, ssem.at[h, n - 1 + t, sub], rcem.at[h, n + t, sub], nexts[h])
+
+    def write(h, j, sub):
+        if sub == 0:
+            dst = out1.at[pl.ds(h * COLS, COLS), lanes(j, COLS)]
+        else:
+            dst = out2.at[pl.ds(pl.multiple_of(j * TAIL, 16), TAIL), pl.ds(h * COLS, COLS)]
+        return pltpu.make_async_copy(gathered(sub, h, j), dst, osem.at[h, j, sub])
+
+    def reduce_event(sub, h, e):
+        total = tile(sub, h, shard(me - sign(h) * e))
+
+        @pl.when(e == 0)
+        def _():
+            buf[h, 0, parts[sub], :] = total.astype(BF)
+            scatter(h, 0, sub).start()
+
+        @pl.when((e > 0) & (e < n - 1))
+        def _():
+            scatter(h, e - 1, sub).wait_recv()
+            buf[h, e, parts[sub], :] = (total + buf[h, e, parts[sub], :].astype(F32)).astype(BF)
+            scatter(h, e, sub).start()
+
+        @pl.when(e == n - 1)
+        def _():
+            j = home(h, 0)
+            scatter(h, n - 2, sub).wait_recv()
+            gathered(sub, h, j)[...] = (total + buf[h, n - 1, parts[sub], :].astype(F32)).astype(BF)
+            pl.semaphore_wait(free.at[h, sub], 1)
+            spread(h, 0, sub, j).start()
+            write(h, j, sub).start()
+
+    def event(sub, e):
+        for h in range(2):
+
+            @pl.when(e < n)
+            def _():
+                reduce_event(sub, h, e)
+
+            @pl.when((e >= n) & (e < 2 * n - 1))
+            def _():
+                t = e - (n - 1)
+                j = home(h, t)
+                spread(h, t - 1, sub, j).wait_recv()
+
+                @pl.when(t < n - 1)
                 def _():
-                    for when, copy in factor_copies(k, m, local):
-                        if when == which:
-                            copy.start()
+                    spread(h, t, sub, j).start()
+
+                write(h, j, sub).start()
+
+    def early_event(e):
+        event(1, e)
+
+        @pl.when(c == 1)
+        def _():
+            event(0, e)
+
+    def small(r):
+        return remote(acc.at[r], got.at[r], sms.at[r], smr.at[r], partners[r])
 
     def forward(m, p):
         @pl.when(jnp.logical_not(early))
@@ -432,10 +562,10 @@
                 wait_weight(k, i)
 
         first_time(0, 5)
-        front_forward(0, m, ubuf, msk, pr, U, C, zb, xh, rs)
+        front_forward(0, m, ubuf, msk, pr, U, C, zz, xh, rs)
         for i in range(3):
             first_time(0, i)
-            qkv[m, :, pl.ds(i * D, D)] = dot(zb[0, m], wf[0, :, pl.ds(i * D, D)]).astype(BF).astype(F32)
+            qkv[m, :, pl.ds(i * D, D)] = dot(zz[m, 0], wf[0, :, pl.ds(i * D, D)]).astype(BF).astype(F32)
 
         @pl.when(early)
         def _():
@@ -446,11 +576,11 @@
             channel_forward(m, qkv, pc, T, msk)
 
         first_time(0, 3)
-        ob[m] = T[...].astype(BF)
-        ubuf[1, m] = (C[...] + dot(ob[m], wf[0, :, pl.ds(3 * D, D)])).astype(BF)
+        zz[m, 1] = T[...].astype(BF)
+        ubuf[1, m] = (C[...] + dot(zz[m, 1], wf[0, :, pl.ds(3 * D, D)])).astype(BF)
 
         first_time(1, 5)
-        front_forward(1, m, ubuf, msk, pr, U, C, zb, xh, rs)
+        front_forward(1, m, ubuf, msk, pr, U, C, zz, xh, rs)
         for i in range(4):
             first_time(1, i)
         first_time(0, 4)
@@ -458,9 +588,9 @@
 
         for t in range(FF // FTILE):
             cols = pl.ds(t * FTILE, FTILE)
-            a, d = gelu_parts(dot(zb[1, m], wf[1, :, cols]))
+            a, d = gelu_parts(dot(zz[m, 2], wf[1, :, cols]))
             ab[m, :, cols] = a.astype(BF)
-            db[m, :, cols] = d.astype(BF)
+            rr[m, 1, :, cols] = d.astype(BF)
         uout[m] = (C[...] + dot(ab[m], w2[...])).astype(BF)
 
         @pl.when(early)
@@ -503,12 +633,23 @@
         for t in range(FF // FTILE):
             cols = pl.ds(t * FTILE, FTILE)
             da = dot(gin[m], w2[cols, :], 1, 1)
-            hb[m, :, cols] = (da * db[m, :, cols].astype(F32)).astype(BF)
-        T[...] = dot(hb[m], wf[1], 1, 1)
+            rr[m, 1, :, cols] = (da * rr[m, 1, :, cols].astype(F32)).astype(BF)
+        T[...] = dot(rr[m, 1], wf[1], 1, 1)
         start_factors(m, "M")
-        front_backward(1, m, ubuf, msk, pr, U, T, gin, xh, rs, sgp, gatt)
+        last = pl.ds(3 * D, D)
+
+        def tail_lanes(i):
+            return rr.at[m, 0, :, pl.ds(pl.multiple_of(3 * D + i * LANE, LANE), LANE)]
+
+        front_backward(1, m, ubuf, msk, pr, U, T, lambda i: gin.at[m, :, lanes(i)], xh, rs, sgp, tail_lanes)
         start_factors(m, "G")
-        T[...] = dot(gatt[m], wf[0, :, pl.ds(3 * D, D)], 1, 1)
+
+        @pl.when(m == 1)
+        def _():
+            wait_factors("FM")
+            early_event(0)
+
+        T[...] = dot(rr[m, 0, :, last], wf[0, :, last], 1, 1)
 
         @pl.when(early)
         def _():
@@ -520,10 +661,16 @@
 
         for i in range(3):
             cols = pl.ds(i * D, D)
-            dqk[m, :, cols] = Q[:, cols].astype(BF)
+            rr[m, 0, :, cols] = Q[:, cols].astype(BF)
         start_factors(m, "A")
-        T[...] = dot(dqk[m], wf[0, :, pl.ds(0, 3 * D)], 1, 1)
-        front_backward(0, m, ubuf, msk, pr, U, T, gatt, xh, rs, sgp, gout)
+
+        @pl.when(m == 1)
+        def _():
+            for e in range(1, EARLY):
+                early_event(e)
+
+        T[...] = dot(rr[m, 0, :, pl.ds(0, 3 * D)], wf[0, :, pl.ds(0, 3 * D)], 1, 1)
+        front_backward(0, m, ubuf, msk, pr, U, T, tail_lanes, xh, rs, sgp, lambda i: gout.at[m, :, lanes(i)])
 
         @pl.when(jnp.logical_not(early))
         def _():
@@ -557,15 +704,39 @@
         return carry
 
     lax.fori_loop(0, 4, phase, 0)
+
+    for h in range(2):
+        for sub in range(2):
+            pl.semaphore_signal(free.at[h, sub], inc=1, device_id=nexts[1 - h], device_id_type=MESH)
 
     for sec in range(2):
         for j in range(12):
             sgs[sec, j : j + 1, :] = jnp.sum(sgp[sec, j], axis=0, keepdims=True)
         sgs[sec, 12:16, :] = jnp.zeros((4, D), F32)
-    keep = pltpu.make_async_copy(sgs.at[c], sg_own, sgsem.at[0])
-    give = remote(sgs.at[1 - c], sg_mate, sgsem.at[1], sgsem.at[2], mate)
-    keep.start()
+    give = remote(sgs.at[1 - c], sgm, sgsem.at[0], sgsem.at[1], mate)
     give.start()
+    wait_factors("GA")
+
+    def ring_step(t, carry):
+        event(1, t + EARLY)
+        event(0, t + jnp.where(c == 1, EARLY, 0))
+        for r in range(rounds + 1):
+
+            @pl.when(t == 1 + 3 * r)
+            def _():
+                if r == 0:
+                    give.wait_recv()
+                    acc[0] = sgs[c] + sgm[...]
+                else:
+                    small(r - 1).wait_recv()
+                    acc[r] = acc[r - 1] + got[r - 1]
+                if r < rounds:
+                    small(r).start()
+
+        return carry
+
+    lax.fori_loop(0, 2 * n - 1, ring_step, 0)
+    outs[...] = acc[rounds]
 
     for k in range(2):
 
@@ -575,15 +746,29 @@
                 copy.wait_send()
             params_copy(k).wait_send()
             for m in range(2):
-                for _when, copy in factor_copies(k, m, True):
-                    copy.wait()
-                for _when, copy in factor_copies(1 - k, m, False):
+                for _when, copy in factor_copies(1 - k, m):
                     copy.wait_send()
-                for _when, copy in factor_copies(k, m, False):
-                    copy.wait_recv()
-
-    keep.wait()
-    give.wait()
+
+    give.wait_send()
+    for r in range(rounds):
+        small(r).wait_send()
+
+    def drain(t, carry):
+        for sub in range(2):
+            for h in range(2):
+                scatter(h, t, sub).wait_send()
+                spread(h, t, sub, home(h, t)).wait_send()
+        return carry
+
+    lax.fori_loop(0, n - 1, drain, 0)
+
+    def written(j, carry):
+        for sub in range(2):
+            for h in range(2):
+                write(h, j, sub).wait()
+        return carry
+
+    lax.fori_loop(0, n, written, 0)
 
     @pl.when(early)
     def _():
@@ -612,21 +797,18 @@
     smem = pl.BlockSpec(memory_space=pltpu.SMEM)
     image = (ROWS, D)
     slot = img.shape
+    rounds = RING.bit_length() - 1
     return pl.pallas_call(
         relay_kernel,
         out_shape=[
             shape(slot, BF),
             shape(slot, BF),
-            shape((4 * ROWS, D), BF),
-            shape((4 * ROWS, D), BF),
-            shape((4 * ROWS, FF), BF),
-            shape((4 * ROWS, FF // 2), BF),
-            shape((4 * ROWS, D), BF),
-            shape((16, D), F32),
+            shape((D, FF), BF),
+            shape((FF // 2, D), BF),
             shape((16, D), F32),
         ],
         in_specs=[smem] * 2 + [vmem] * 6 + [anywhere] * 2,
-        out_specs=[anywhere] * 9,
+        out_specs=[anywhere] * 4 + [vmem],
         scratch_shapes=[
             pltpu.VMEM((2, D, FF), BF),
             pltpu.VMEM((FF, D), BF),
@@ -638,16 +820,12 @@
             pltpu.VMEM((2,) + image, BF),
             pltpu.VMEM((2,) + image, BF),
             pltpu.VMEM((2,) + image, BF),
-            pltpu.VMEM((2,) + image, BF),
-            pltpu.VMEM((2, 2) + image, BF),
+            pltpu.VMEM((2, 3) + image, BF),
             pltpu.VMEM((2, 2) + image, BF),
             pltpu.VMEM((2, 2, ROWS, LANE), F32),
             pltpu.VMEM((2, ROWS, 3 * D), F32),
-            pltpu.VMEM((2,) + image, BF),
             pltpu.VMEM((2, ROWS, FF), BF),
-            pltpu.VMEM((2, ROWS, FF), BF),
-            pltpu.VMEM((2, ROWS, FF), BF),
-            pltpu.VMEM((2, ROWS, 3 * D), BF),
+            pltpu.VMEM((2, 2, ROWS, FF), BF),
             pltpu.VMEM((2, UNITS, PACK * WROWS, WROWS), F32),
             pltpu.VMEM((2, NGROUP, GROUP, GROUP), F32),
             pltpu.VMEM((SIDE, GRID + 2, CELL, D), F32),
@@ -656,280 +834,56 @@
             pltpu.VMEM((ROWS, 3 * D), F32),
             pltpu.VMEM((2, 12, CELL, D), F32),
             pltpu.VMEM((2, 16, D), F32),
-            dma((6,)),
+            pltpu.VMEM((16, D), F32),
+            pltpu.VMEM((2, 2) + image, BF),
+            pltpu.VMEM((2, ROWS, FF), BF),
+            pltpu.VMEM((2, ROWS, FF // 2), BF),
+            pltpu.VMEM((2,) + image, BF),
+            pltpu.VMEM((2, RING, COLS + TAIL, COLS), BF),
+            pltpu.VMEM((rounds + 1, 16, D), F32),
+            pltpu.VMEM((rounds, 16, D), F32),
+            dma((5,)),
             dma((6,)),
             dma((6,)),
             dma((2,)),
             dma((2,)),
             dma((2,)),
             dma((2,)),
-            dma((2, 6)),
+            dma((2,)),
             dma((2, 6)),
             dma((2, 6)),
             dma((2,)),
             dma((2,)),
-            dma((3,)),
+            dma((2,)),
+            dma((2, 2 * RING, 2)),
+            dma((2, 2 * RING, 2)),
+            dma((2, RING, 2)),
+            dma((rounds,)),
+            dma((rounds,)),
+            pltpu.SemaphoreType.REGULAR((2, 2)),
         ],
         name="relay",
         compiler_params=pltpu.CompilerParams(
-            collective_id=1, has_side_effects=True, vmem_limit_bytes=60 * 2**20
+            collective_id=1, has_side_effects=True, vmem_limit_bytes=62 * 2**20
         ),
     )(wrows, wcols, img, cot, kern, bias, gain, move, first, second)
-
-
-RING = 8
-COLS = FF // RING
-TAIL = FF // 2 // RING
-
-
-def ring_kernel(
-    n, fa, fb, fr, f2, fg, sg_own, sg_mate,
-    out1, out2, outs,
-    la, r1, a2, g2, lt, at, buf, ag, acc, got,
-    lsem, ss, rs, os_, sms, smr,
-):
-    s = lax.axis_index("section")
-    dp = lax.axis_index("dp")
-    c = lax.rem(s, 2)
-    tokens = la.shape[1]
-
-    def place(pos):
-        pos = lax.rem(pos + 2 * n, n)
-        return jnp.where(pos < n // 2, 2 * pos, 2 * (n - 1 - pos) + 1)
-
-    me = jnp.where(lax.rem(dp, 2) == 0, dp // 2, n - 1 - dp // 2)
-    nexts = (place(me + 1), place(me - 1))
-    rounds = n.bit_length() - 1
-    partners = []
-    for r in range(rounds):
-        bit = 1 << r
-        partners.append(jnp.where(lax.rem(dp // bit, 2) == 0, dp + bit, dp - bit))
-
-    barrier = pltpu.get_barrier_semaphore()
-    peers = list(nexts) + partners
-    for peer in peers:
-        pl.semaphore_signal(barrier, inc=1, device_id=(peer, s), device_id_type=MESH)
-
-    loads = [
-        pltpu.make_async_copy(fa, la.at[0], lsem.at[0]),
-        pltpu.make_async_copy(fr, r1, lsem.at[1]),
-        pltpu.make_async_copy(f2, a2, lsem.at[2]),
-        pltpu.make_async_copy(fg, g2, lsem.at[3]),
-        pltpu.make_async_copy(fb, la.at[1], lsem.at[4]),
-    ]
-    for copy in loads[:4]:
-        copy.start()
-
-    @pl.when(c == 0)
-    def _():
-        loads[4].start()
-
-    def turn(src, dst, count):
-        def body(i, carry):
-            dst[lanes(i), :] = src[:, lanes(i)].T
-            return carry
-
-        lax.fori_loop(0, count, body, 0)
-
-    def shard(k):
-        return lax.rem(k + 2 * n, n)
-
-    def tile1(h, j):
-        sel = jnp.where((c == 0) & (j >= (3 * n) // 4), 1, 0)
-        return dot(lt[sel, pl.ds(h * COLS, COLS), :], r1[:, lanes(j, COLS)])
-
-    def tile2(h, j):
-        rows = pl.ds(pl.multiple_of(j * TAIL, 16), TAIL)
-        return dot(at[rows, :], g2[:, pl.ds(h * COLS, COLS)])
-
-    parts = (pl.ds(0, COLS), pl.ds(COLS, TAIL))
-    tiles = (tile1, tile2)
-
-    def scatter(h, t, sub):
-        return pltpu.make_async_remote_copy(
-            src_ref=buf.at[h, t, parts[sub], :],
-            dst_ref=buf.at[h, t + 1, parts[sub], :],
-            send_sem=ss.at[h, t, sub],
-            recv_sem=rs.at[h, t + 1, sub],
-            device_id=(nexts[h], s),
-            device_id_type=MESH,
-        )
-
-    def spread(h, t, sub, j):
-        return pltpu.make_async_remote_copy(
-            src_ref=ag.at[h, j, parts[sub], :],
-            dst_ref=ag.at[h, j, parts[sub], :],
-            send_sem=ss.at[h, n - 1 + t, sub],
-            recv_sem=rs.at[h, n + t, sub],
-            device_id=(nexts[h], s),
-            device_id_type=MESH,
-        )
-
-    def write(h, j, sub):
-        cols = lanes(j, COLS)
-        if sub == 0:
-            dst = out1.at[pl.ds(h * COLS, COLS), cols]
-        else:
-            dst = out2.at[pl.ds(pl.multiple_of(j * TAIL, 16), TAIL), pl.ds(h * COLS, COLS)]
-        return pltpu.make_async_copy(ag.at[h, j, parts[sub], :], dst, os_.at[h, j, sub])
-
-    def sign(h):
-        return 1 if h == 0 else -1
-
-    loads[0].wait()
-    turn(la.at[0], lt.at[0], D // LANE)
-
-    @pl.when(c == 0)
-    def _():
-        loads[4].wait()
-        turn(la.at[1], lt.at[1], D // LANE)
-
-    loads[1].wait()
-    pl.semaphore_wait(barrier, len(peers))
-    for h in range(2):
-        buf[h, 0, parts[0], :] = tile1(h, me).astype(BF)
-        scatter(h, 0, 0).start()
-    loads[2].wait()
-    loads[3].wait()
-    turn(a2, at, FF // 2 // LANE)
-    for h in range(2):
-        buf[h, 0, parts[1], :] = tile2(h, me).astype(BF)
-        scatter(h, 0, 1).start()
-
-    acc[0] = sg_own[...] + sg_mate[...]
-
-    def reduce_step(t, carry):
-        for sub in range(2):
-            for h in range(2):
-                own = tiles[sub](h, shard(me - sign(h) * t))
-                scatter(h, t - 1, sub).wait_recv()
-                buf[h, t, parts[sub], :] = (own + buf[h, t, parts[sub], :].astype(F32)).astype(BF)
-                scatter(h, t, sub).start()
-        return carry
-
-    lax.fori_loop(1, n - 1, reduce_step, 0)
-
-    def home(h, t):
-        return shard(me + sign(h) - sign(h) * t)
-
-    for sub in range(2):
-        for h in range(2):
-            j = home(h, 0)
-            own = tiles[sub](h, j)
-            scatter(h, n - 2, sub).wait_recv()
-            ag[h, j, parts[sub], :] = (own + buf[h, n - 1, parts[sub], :].astype(F32)).astype(BF)
-            spread(h, 0, sub, j).start()
-            write(h, j, sub).start()
-
-    def small(r):
-        return pltpu.make_async_remote_copy(
-            src_ref=acc.at[r],
-            dst_ref=got.at[r],
-            send_sem=sms.at[r],
-            recv_sem=smr.at[r],
-            device_id=(partners[r], s),
-            device_id_type=MESH,
-        )
-
-    small(0).start()
-    for t in range(1, n):
-        for sub in range(2):
-            for h in range(2):
-                j = home(h, t)
-                spread(h, t - 1, sub, j).wait_recv()
-                if t < n - 1:
-                    spread(h, t, sub, j).start()
-                write(h, j, sub).start()
-        if t % 2 == 0 and t // 2 <= rounds:
-            r = t // 2 - 1
-            small(r).wait_recv()
-            acc[r + 1] = acc[r] + got[r]
-            if r + 1 < rounds:
-                small(r + 1).start()
-    outs[...] = acc[rounds]
-
-    def drain(t, carry):
-        for sub in range(2):
-            for h in range(2):
-                scatter(h, t, sub).wait_send()
-        return carry
-
-    lax.fori_loop(0, n - 1, drain, 0)
-    for t in range(n - 1):
-        for sub in range(2):
-            for h in range(2):
-                spread(h, t, sub, home(h, t)).wait_send()
-    for j in range(n):
-        for sub in range(2):
-            for h in range(2):
-                write(h, j, sub).wait()
-    for r in range(rounds):
-        small(r).wait_send()
-
-
-def ring_reduce(n, fa, fb, fr, f2, fg, sg_own, sg_mate):
-    shape = jax.ShapeDtypeStruct
-    vmem = pl.BlockSpec(memory_space=pltpu.VMEM)
-    anywhere = pl.BlockSpec(memory_space=pl.ANY)
-    dma = pltpu.SemaphoreType.DMA
-    tokens = fa.shape[0]
-    rounds = n.bit_length() - 1
-    block = (COLS + TAIL, COLS)
-    return pl.pallas_call(
-        partial(ring_kernel, n),
-        out_shape=[shape((D, FF), BF), shape((FF // 2, D), BF), shape((16, D), F32)],
-        in_specs=[anywhere] * 5 + [vmem] * 2,
-        out_specs=[anywhere, anywhere, vmem],
-        scratch_shapes=[
-            pltpu.VMEM((2, tokens, D), BF),
-            pltpu.VMEM((tokens, FF), BF),
-            pltpu.VMEM((tokens, FF // 2), BF),
-            pltpu.VMEM((tokens, D), BF),
-            pltpu.VMEM((2, D, tokens), BF),
-            pltpu.VMEM((FF // 2, tokens), BF),
-            pltpu.VMEM((2, n) + block, BF),
-            pltpu.VMEM((2, n) + block, BF),
-            pltpu.VMEM((rounds + 1, 16, D), F32),
-            pltpu.VMEM((rounds, 16, D), F32),
-            dma((5,)),
-            dma((2, 2 * n, 2)),
-            dma((2, 2 * n, 2)),
-            dma((2, n, 2)),
-            dma((rounds,)),
-            dma((rounds,)),
-        ],
-        name="ring",
-        compiler_params=pltpu.CompilerParams(
-            collective_id=2, has_side_effects=True, vmem_limit_bytes=60 * 2**20
-        ),
-    )(fa, fb, fr, f2, fg, sg_own, sg_mate)
-
-
-def plain_reduce(fa, fb, fr, f2, fg, sg_own, sg_mate):
-    even = lax.rem(lax.axis_index("section"), 2) == 0
-    left = jnp.where(even, fb, fa)
-    qkv = dot(fa, fr[:, : 3 * D], 0, 0)
-    last = dot(left, fr[:, 3 * D :], 0, 0)
-    out1 = jnp.concatenate([qkv, last], axis=1)
-    out2 = dot(f2, fg, 0, 0)
-    return lax.psum((out1.astype(BF), out2.astype(BF), sg_own + sg_mate), "dp")
 
 
 def per_device(
     images, cotangent, window_rows, window_cols, pos_kernel, pos_bias, norm_gain, norm_shift, first_weight, second_weight
 ):
-    act, ing, fa, fb, fr, f2, fg, sg_own, sg_mate = relay(
+    act, ing, out1, out2, outs = relay(
         window_rows, window_cols, images[0], cotangent[0], pos_kernel[0], pos_bias, norm_gain, norm_shift,
         first_weight[0], second_weight,
     )
-    n = lax.axis_size("dp")
-    reduce = partial(ring_reduce, n) if n == RING else plain_reduce
-    out1, out2, outs = reduce(fa, fb, fr, f2, fg, sg_own, sg_mate)
+    out1, out2 = out1.astype(F32), out2.astype(F32)
+    if lax.axis_size("dp") > RING:
+        out1, out2, outs = lax.psum((out1 / RING, out2 / RING, outs / RING), "dp")
     return (
         act[None],
         ing.astype(F32)[None],
-        out1.astype(F32)[None],
-        out2.astype(F32),
+        out1[None],
+        out2,
         outs[None, :9],
         outs[9:10],
         outs[10:11],

time: 261 us -> 252 us (0.966)
  Pallas kernels: 246 us -> 236 us
    pallas_call x1 -> x0, Pallas kernels: 145 us -> none  [ring_reduce(): pl.pallas_call(partial(ring_kernel, n), out_shape=[shape((D, FF), BF), sh...]
    pallas_call x1, Pallas kernels: 101 us -> 236 us  [relay(): pl.pallas_call(relay_kernel, out_shape=[shape(slot, BF), shape(slot, BF),...]
where the time goes in v3:
time: 252 us
  Pallas kernels  236 us (94%)
  other arithmetic  10.1 us (4%)
  local copies, waits for them, and re-layouts  5.06 us (2%)
    pallas_call x1, Pallas kernels, relay(): pl.pallas_call(relay_kernel, out_shape=[shape(slot, BF), shape(slot, BF),...  236 us
    broadcast_in_dim x1, other arithmetic, per_device(): out1[None]  7.52 us

profile of v3, /device:TPU:0, one launch (start us, length us, event | category | flops | bytes accessed | tf_op | source)
XLA Modules:
  0.0 251.9 jit_solution(2506611198608933801)
XLA Ops:
  0.6 236.0 %relay.1 = (bf16[14,14,768]{2,1,0:T(8,128)(2,1)}, bf16[14,14,768]{2,1,0:T(8,128)(2,1)}, bf16[768,3072]{1,0:T(8,128)(2,1)}, bf16[1536,768]{1,0:T(8,128)(2,1)}, f32[16,768]{1,0:T(8,128)}) custom-call(s32[4]{0:T(128)} %wrows.1, s32[4]{0:T(128)} %wcols.1, bf16[14,14,768]{2,1,0:T(8,128)(2,1)} %bitcast.14, bf16[14,14,768]{2,1,0:T(8,128)(2,1)} %bitcast.15, ...), custom_call_target="tpu_custom_call" | custom-call | tf_op jit(solution)/shard_map/relay/pallas_call | solution.py:801
  236.7 1.4 fusion
  238.1 0.8 slice_bitcast_fusion
  238.9 0.6 copy.19
  239.6 0.0 copy-start
  239.6 7.5 %bitcast_convert_fusion = f32[1,768,3072]{2,1,0:T(8,128)} fusion(bf16[768,3072]{1,0:T(8,128)(2,1)} %get-tuple-element.15), kind=kLoop, calls=%fused_computation | loop fusion | flops 2359296 | bytes 14155776 | tf_op jit(solution)/shard_map/broadcast_in_dim | solution.py:885
  247.1 0.0 copy-start.2
  247.1 0.0 copy-start.1
  247.1 0.0 copy-done
  247.1 2.5 %convert_element_type.2 = f32[1536,768]{1,0:T(8,128)} convert(bf16[1536,768]{1,0:T(8,128)(2,1)S(1)} %copy-done) | non-fusion elementwise | flops 1179648 | bytes 7077888 | tf_op jit(solution)/shard_map/convert_element_type | solution.py:879
  249.6 0.0 copy-done.2
  249.6 0.1 bitcast_convert_fusion.1
  249.7 1.4 copy.18
  251.1 0.0 copy-done.1
  251.1 0.7 copy.21
Async XLA Ops:
  239.6 7.5 %copy-start = (bf16[1536,768]{1,0:T(8,128)(2,1)S(1)}, bf16[1536,768]{1,0:T(8,128)(2,1)}, u32[]{:S(2)}) copy-start(bf16[1536,768]{1,0:T(8,128)(2,1)} %get-tuple-element.16) | copy-start | bytes 7077892
  247.1 2.6 %copy-start.2 = (bf16[14,14,768]{2,1,0:T(8,128)(2,1)S(1)}, bf16[14,14,768]{2,1,0:T(8,128)(2,1)}, u32[]{:S(2)}) copy-start(bf16[14,14,768]{2,1,0:T(8,128)(2,1)} %get-tuple-element.14) | copy-start | bytes 903172
  247.1 4.1 %copy-start.1 = (bf16[14,14,768]{2,1,0:T(8,128)(2,1)S(1)}, bf16[14,14,768]{2,1,0:T(8,128)(2,1)}, u32[]{:S(2)}) copy-start(bf16[14,14,768]{2,1,0:T(8,128)(2,1)} %get-tuple-element.13) | copy-start | bytes 903172

commit v4 on v3

--- a/solution.py
+++ b/solution.py
@@ -203,7 +203,7 @@
     lax.fori_loop(0, UNITS // 2, unit, 0)
 
 
-def window_backward(m, qkv, pw, T, Q):
+def window_backward(m, qkv, pw, T):
     def unit(i, carry):
         rows, cols, head_of_lane, q, kd, vd = window_parts(m, i, qkv)
         g = [T[r, cols[0]].astype(BF) for r in rows]
@@ -216,9 +216,9 @@
         dk = [gather_heads(dot(x, y), WROWS, head_of_lane) * SCALE for x, y in zip(ds, q)]
         dq = [dot(x, y, 0, 0) * SCALE for x, y in zip(ds, kd)]
         for w in range(2):
-            Q[rows[w], cols[0]] = dq[w]
-            Q[rows[w], cols[1]] = dk[w]
-            Q[rows[w], cols[2]] = dv[w]
+            qkv[m, rows[w], cols[0]] = dq[w]
+            qkv[m, rows[w], cols[1]] = dk[w]
+            qkv[m, rows[w], cols[2]] = dv[w]
         return carry
 
     lax.fori_loop(0, UNITS // 2, unit, 0)
@@ -247,7 +247,7 @@
     lax.fori_loop(0, NGROUP, unit, 0, unroll=True)
 
 
-def channel_backward(m, qkv, pc, T, Q, msk):
+def channel_backward(m, qkv, pc, T, msk):
     def unit(i, carry):
         cols = group_slices(i)
         mask = msk[m][:, :1]
@@ -258,9 +258,9 @@
         p = pc[m, i]
         dp = dot(g, v, 0, 0)
         ds = (p * (dp - jnp.sum(p * dp, axis=1, keepdims=True))).astype(BF)
-        Q[:, cols[0]] = dot(k, ds, 1, 1) * SCALE
-        Q[:, cols[1]] = dot(q, ds) * (SCALE * mask)
-        Q[:, cols[2]] = dot(g, p.astype(BF))
+        qkv[m, :, cols[0]] = dot(k, ds, 1, 1) * SCALE
+        qkv[m, :, cols[1]] = dot(q, ds) * (SCALE * mask)
+        qkv[m, :, cols[2]] = dot(g, p.astype(BF))
         return carry
 
     lax.fori_loop(0, NGROUP, unit, 0, unroll=True)
@@ -268,16 +268,18 @@
 
 RING = 8
 COLS = FF // RING
-TAIL = FF // 2 // RING
+TAIL = FF // 3 // RING
+REST = FF // 6 // RING
+LATER = FF // 3
 EARLY = 2
 
 
 def relay_kernel(
     wrows, wcols, img, cot, kern, bias, gain, move, first, second,
     act, ing, out1, out2, outs,
-    wf, w2, pr, msk, raw, flat, ubuf, gin, gout, uout, zz, xh, rs, qkv, ab, rr, pw, pc, U, C, T, Q, sgp, sgs, sgm,
-    rL, rR, rA, rG, buf, acc, got,
-    wl, ws, wr, pl_, usem, gsem, us, gs, ss, rsem, es, er, sgsem, ssem, rcem, osem, sms, smr, free,
+    wf, w2, pr, msk, raw, flat, ubuf, gin, gout, zz, xh, rs, qkv, ab, rr, pw, pc, U, C, T, sgp, sgs, sgm,
+    rL, rR, rA, rG, xA, xG, buf, acc, got,
+    wl, ws, wr, pl_, usem, gsem, us, gs, ss, rsem, es, er, sgsem, ssem, rcem, osem, sms, smr, xs, xr, ys, yr, bs, br, free,
 ):
     n = RING
     s = lax.axis_index("section")
@@ -396,7 +398,7 @@
     sgp[...] = jnp.zeros(sgp.shape, F32)
 
     def u_hop(m):
-        return remote(uout.at[m], ubuf.at[0, m], us.at[m], usem.at[m], opposite)
+        return remote(gout.at[m], ubuf.at[0, m], us.at[m], usem.at[m], opposite)
 
     def g_hop(m):
         return remote(gout.at[m], gin.at[m], gs.at[m], gsem.at[m], opposite)
@@ -448,6 +450,16 @@
     def home(h, t):
         return shard(me + sign(h) - sign(h) * t)
 
+    def products(terms):
+        total = None
+        for a, b in terms:
+            part = dot(a[...], b[...], 0, 0)
+            total = part if total is None else total + part
+        return total
+
+    def pick(total, j):
+        return jnp.where(lax.rem(j, 2) == 1, total[REST:], total[:REST])
+
     def tile(sub, h, j):
         side = pl.ds(h * COLS, COLS)
         if sub == 0:
@@ -457,25 +469,31 @@
             cols = lanes(j, COLS)
             terms = [(zz.at[m, own, :, side], rr.at[m, c, :, cols]) for m in range(2)]
             terms += [(rL.at[m, other, :, side], rR.at[m, :, cols]) for m in range(2)]
-        else:
-            mine = pl.ds(pl.multiple_of(c * (FF // 2) + (j // 2) * 2 * TAIL, LANE), 2 * TAIL)
-            cols = lanes(j // 2, 2 * TAIL)
+        elif sub == 1:
+            mine = pl.ds(pl.multiple_of(c * (FF // 2) + j * TAIL, LANE), TAIL)
+            cols = lanes(j, TAIL)
             terms = [(ab.at[m, :, mine], gin.at[m, :, side]) for m in range(2)]
             terms += [(rA.at[m, :, cols], rG.at[m, :, side]) for m in range(2)]
-        total = None
-        for a, b in terms:
-            part = dot(a[...], b[...], 0, 0)
-            total = part if total is None else total + part
-        if sub == 1:
-            total = jnp.where(lax.rem(j, 2) == 1, total[TAIL:], total[:TAIL])
-        return total
-
-    parts = (pl.ds(0, COLS), pl.ds(COLS, TAIL))
+        else:
+            block = j // 2 * 2 * REST
+            mine = pl.ds(pl.multiple_of(c * (FF // 2) + LATER + block, LANE), 2 * REST)
+            cols = pl.ds(pl.multiple_of(LATER + block, LANE), 2 * REST)
+            sent = pl.ds(pl.multiple_of(block, LANE), 2 * REST)
+            terms = [(ab.at[m, :, mine], gin.at[m, :, side]) for m in range(2)]
+            terms += [(rA.at[m, :, cols], rG.at[m, :, side]) for m in range(2)]
+            own = pick(products(terms), j)
+            terms = [(xA.at[m, :, sent], gout.at[m, :, side]) for m in range(2)]
+            terms += [(xA.at[2 + m, :, sent], xG.at[m, :, side]) for m in range(2)]
+            return jnp.concatenate([own, pick(products(terms), j)], axis=0)
+        return products(terms)
+
+    parts = (pl.ds(0, COLS), pl.ds(COLS, TAIL), pl.ds(COLS + TAIL, 2 * REST))
 
     def gathered(sub, h, j):
         if sub == 0:
             return wf.at[0, pl.ds(h * COLS, COLS), lanes(j, COLS)]
-        return w2.at[pl.ds(pl.multiple_of(j * TAIL, 16), TAIL), pl.ds(h * COLS, COLS)]
+        start = j * TAIL if sub == 1 else 2 * LATER + j * 2 * REST
+        return w2.at[pl.ds(pl.multiple_of(start, 16), TAIL if sub == 1 else 2 * REST), pl.ds(h * COLS, COLS)]
 
     def scatter(h, t, sub):
         src, dst = buf.at[h, t, parts[sub], :], buf.at[h, t + 1, parts[sub], :]
@@ -488,9 +506,33 @@
     def write(h, j, sub):
         if sub == 0:
             dst = out1.at[pl.ds(h * COLS, COLS), lanes(j, COLS)]
+        elif sub == 1:
+            dst = out2.at[pl.ds(pl.multiple_of(j * TAIL, 16), TAIL), pl.ds(h * COLS, COLS)]
         else:
-            dst = out2.at[pl.ds(pl.multiple_of(j * TAIL, 16), TAIL), pl.ds(h * COLS, COLS)]
+            dst = out2.at[pl.ds(pl.multiple_of(LATER + j * REST, 16), REST), pl.ds(h * COLS, COLS)]
+            return pltpu.make_async_copy(gathered(sub, h, j).at[pl.ds(0, REST), :], dst, osem.at[h, j, sub])
         return pltpu.make_async_copy(gathered(sub, h, j), dst, osem.at[h, j, sub])
+
+    def give_back(h, j):
+        src = w2.at[pl.ds(pl.multiple_of(2 * LATER + j * 2 * REST + REST, 16), REST), pl.ds(h * COLS, COLS)]
+        dst = out2.at[pl.ds(pl.multiple_of(LATER + j * REST, 16), REST), pl.ds(h * COLS, COLS)]
+        return remote(src, dst, bs.at[h, j], br.at[h, j], opposite)
+
+    def deliver(h, j, sub):
+        write(h, j, sub).start()
+        if sub == 2:
+            give_back(h, j).start()
+
+    def lend(m):
+        own = ab.at[m, :, pl.ds(pl.multiple_of(c * (FF // 2) + LATER, LANE), FF // 2 - LATER)]
+        other = rA.at[m, :, pl.ds(LATER, FF // 2 - LATER)]
+        return (
+            remote(own, xA.at[m], xs.at[m], xr.at[m], opposite),
+            remote(other, xA.at[2 + m], xs.at[2 + m], xr.at[2 + m], opposite),
+        )
+
+    def share(m):
+        return remote(gout.at[m], xG.at[m], ys.at[m], yr.at[m], mate)
 
     def reduce_event(sub, h, e):
         total = tile(sub, h, shard(me - sign(h) * e))
@@ -513,7 +555,7 @@
             gathered(sub, h, j)[...] = (total + buf[h, n - 1, parts[sub], :].astype(F32)).astype(BF)
             pl.semaphore_wait(free.at[h, sub], 1)
             spread(h, 0, sub, j).start()
-            write(h, j, sub).start()
+            deliver(h, j, sub)
 
     def event(sub, e):
         for h in range(2):
@@ -532,7 +574,7 @@
                 def _():
                     spread(h, t, sub, j).start()
 
-                write(h, j, sub).start()
+                deliver(h, j, sub)
 
     def early_event(e):
         event(1, e)
@@ -591,7 +633,7 @@
             a, d = gelu_parts(dot(zz[m, 2], wf[1, :, cols]))
             ab[m, :, cols] = a.astype(BF)
             rr[m, 1, :, cols] = d.astype(BF)
-        uout[m] = (C[...] + dot(ab[m], w2[...])).astype(BF)
+        gout[m] = (C[...] + dot(ab[m], w2[...])).astype(BF)
 
         @pl.when(early)
         def _():
@@ -601,7 +643,7 @@
         def _():
             for l in range(D // LANE):
                 cols = pl.ds(l * LANE, LANE)
-                C[:, cols] = uout[m, :, cols].astype(F32) * msk[m]
+                C[:, cols] = gout[m, :, cols].astype(F32) * msk[m]
             unpad(flat.at[m])
 
         @pl.when(jnp.logical_not(early) & (m == 0))
@@ -613,6 +655,13 @@
             pltpu.make_async_copy(flat.at[1], act, es.at[0]).start()
 
         start_factors(m, "F")
+
+        @pl.when(early & (m == 1))
+        def _():
+            wait_factors("F")
+            for i in range(2):
+                for copy in lend(i):
+                    copy.start()
 
     def backward(m):
         @pl.when(early)
@@ -638,6 +687,10 @@
         start_factors(m, "M")
         last = pl.ds(3 * D, D)
 
+        @pl.when(early)
+        def _():
+            u_hop(m).wait_send()
+
         def tail_lanes(i):
             return rr.at[m, 0, :, pl.ds(pl.multiple_of(3 * D + i * LANE, LANE), LANE)]
 
@@ -646,22 +699,26 @@
 
         @pl.when(m == 1)
         def _():
-            wait_factors("FM")
+            @pl.when(jnp.logical_not(early))
+            def _():
+                wait_factors("F")
+
+            wait_factors("M")
             early_event(0)
 
         T[...] = dot(rr[m, 0, :, last], wf[0, :, last], 1, 1)
 
         @pl.when(early)
         def _():
-            window_backward(m, qkv, pw, T, Q)
+            window_backward(m, qkv, pw, T)
 
         @pl.when(jnp.logical_not(early))
         def _():
-            channel_backward(m, qkv, pc, T, Q, msk)
+            channel_backward(m, qkv, pc, T, msk)
 
         for i in range(3):
             cols = pl.ds(i * D, D)
-            rr[m, 0, :, cols] = Q[:, cols].astype(BF)
+            rr[m, 0, :, cols] = qkv[m, :, cols].astype(BF)
         start_factors(m, "A")
 
         @pl.when(m == 1)
@@ -675,6 +732,7 @@
         @pl.when(jnp.logical_not(early))
         def _():
             g_hop(m).start()
+            share(m).start()
 
         @pl.when(early)
         def _():
@@ -708,6 +766,10 @@
     for h in range(2):
         for sub in range(2):
             pl.semaphore_signal(free.at[h, sub], inc=1, device_id=nexts[1 - h], device_id_type=MESH)
+
+        @pl.when(jnp.logical_not(early))
+        def _():
+            pl.semaphore_signal(free.at[h, 2], inc=1, device_id=nexts[1 - h], device_id_type=MESH)
 
     for sec in range(2):
         for j in range(12):
@@ -717,8 +779,20 @@
     give.start()
     wait_factors("GA")
 
+    @pl.when(jnp.logical_not(early))
+    def _():
+        for m in range(2):
+            for copy in lend(m):
+                copy.wait_recv()
+            share(m).wait_recv()
+
     def ring_step(t, carry):
         event(1, t + EARLY)
+
+        @pl.when(jnp.logical_not(early))
+        def _():
+            event(2, t)
+
         event(0, t + jnp.where(c == 1, EARLY, 0))
         for r in range(rounds + 1):
 
@@ -754,18 +828,34 @@
         small(r).wait_send()
 
     def drain(t, carry):
-        for sub in range(2):
-            for h in range(2):
+        for h in range(2):
+            for sub in range(2):
                 scatter(h, t, sub).wait_send()
                 spread(h, t, sub, home(h, t)).wait_send()
+
+            @pl.when(jnp.logical_not(early))
+            def _():
+                scatter(h, t, 2).wait_send()
+                spread(h, t, 2, home(h, t)).wait_send()
+
         return carry
 
     lax.fori_loop(0, n - 1, drain, 0)
 
     def written(j, carry):
-        for sub in range(2):
-            for h in range(2):
+        for h in range(2):
+            for sub in range(2):
                 write(h, j, sub).wait()
+
+            @pl.when(early)
+            def _():
+                give_back(h, j).wait_recv()
+
+            @pl.when(jnp.logical_not(early))
+            def _():
+                write(h, j, 2).wait()
+                give_back(h, j).wait_send()
+
         return carry
 
     lax.fori_loop(0, n, written, 0)
@@ -774,7 +864,8 @@
     def _():
         cot_out.wait_send()
         for m in range(2):
-            u_hop(m).wait_send()
+            for copy in lend(m):
+                copy.wait_send()
         pltpu.make_async_copy(flat.at[0], ing, es.at[1]).wait()
         remote(flat.at[1], ing, es.at[1], er.at[1], opposite).wait_send()
         remote(flat.at[0], act, es.at[0], er.at[0], opposite).wait_recv()
@@ -784,6 +875,7 @@
         img_out.wait_send()
         for m in range(2):
             g_hop(m).wait_send()
+            share(m).wait_send()
         remote(flat.at[0], act, es.at[0], er.at[0], opposite).wait_send()
         pltpu.make_async_copy(flat.at[1], act, es.at[0]).wait()
         remote(flat.at[1], ing, es.at[1], er.at[1], opposite).wait_recv()
@@ -819,7 +911,6 @@
             pltpu.VMEM((2, 2) + image, BF),
             pltpu.VMEM((2,) + image, BF),
             pltpu.VMEM((2,) + image, BF),
-            pltpu.VMEM((2,) + image, BF),
             pltpu.VMEM((2, 3) + image, BF),
             pltpu.VMEM((2, 2) + image, BF),
             pltpu.VMEM((2, 2, ROWS, LANE), F32),
@@ -831,7 +922,6 @@
             pltpu.VMEM((SIDE, GRID + 2, CELL, D), F32),
             pltpu.VMEM(image, F32),
             pltpu.VMEM(image, F32),
-            pltpu.VMEM((ROWS, 3 * D), F32),
             pltpu.VMEM((2, 12, CELL, D), F32),
             pltpu.VMEM((2, 16, D), F32),
             pltpu.VMEM((16, D), F32),
@@ -839,7 +929,9 @@
             pltpu.VMEM((2, ROWS, FF), BF),
             pltpu.VMEM((2, ROWS, FF // 2), BF),
             pltpu.VMEM((2,) + image, BF),
-            pltpu.VMEM((2, RING, COLS + TAIL, COLS), BF),
+            pltpu.VMEM((4, ROWS, FF // 2 - LATER), BF),
+            pltpu.VMEM((2,) + image, BF),
+            pltpu.VMEM((2, RING, COLS + TAIL + 2 * REST, COLS), BF),
             pltpu.VMEM((rounds + 1, 16, D), F32),
             pltpu.VMEM((rounds, 16, D), F32),
             dma((5,)),
@@ -855,12 +947,18 @@
             dma((2,)),
             dma((2,)),
             dma((2,)),
-            dma((2, 2 * RING, 2)),
-            dma((2, 2 * RING, 2)),
-            dma((2, RING, 2)),
+            dma((2, 2 * RING, 3)),
+            dma((2, 2 * RING, 3)),
+            dma((2, RING, 3)),
             dma((rounds,)),
             dma((rounds,)),
-            pltpu.SemaphoreType.REGULAR((2, 2)),
+            dma((4,)),
+            dma((4,)),
+            dma((2,)),
+            dma((2,)),
+            dma((2, RING)),
+            dma((2, RING)),
+            pltpu.SemaphoreType.REGULAR((2, 3)),
         ],
         name="relay",
         compiler_params=pltpu.CompilerParams(

time: 252 us -> 242 us (0.960)
  Pallas kernels: 236 us -> 225 us
    pallas_call x1, Pallas kernels: 236 us -> 225 us  [relay(): pl.pallas_call(relay_kernel, out_shape=[shape(slot, BF), shape(slot, BF),...]
where the time goes in v4:
time: 242 us; the launch traced here: 241 us
  Pallas kernels  225 us (93%)
  other arithmetic  10.1 us (4%)
  local copies, waits for them, and re-layouts  5.06 us (2%)
    pallas_call x1, Pallas kernels, relay(): pl.pallas_call(relay_kernel, out_shape=[shape(slot, BF), shape(slot, BF),...  225 us
    broadcast_in_dim x1, other arithmetic, per_device(): out1[None]  7.52 us

profile of v4, /device:TPU:0, one launch (start us, length us, event | category | flops | bytes accessed | tf_op | source)
XLA Modules:
  0.0 241.1 jit_solution(5641845879698713161)
XLA Ops:
  0.6 225.2 %relay.1 = (bf16[14,14,768]{2,1,0:T(8,128)(2,1)}, bf16[14,14,768]{2,1,0:T(8,128)(2,1)}, bf16[768,3072]{1,0:T(8,128)(2,1)}, bf16[1536,768]{1,0:T(8,128)(2,1)}, f32[16,768]{1,0:T(8,128)}) custom-call(s32[4]{0:T(128)} %wrows.1, s32[4]{0:T(128)} %wcols.1, bf16[14,14,768]{2,1,0:T(8,128)(2,1)} %bitcast.14, bf16[14,14,768]{2,1,0:T(8,128)(2,1)} %bitcast.15, ...), custom_call_target="tpu_custom_call" | custom-call | tf_op jit(solution)/shard_map/relay/pallas_call | solution.py:893
  225.9 1.4 fusion
  227.3 0.8 slice_bitcast_fusion
  228.1 0.6 copy.19
  228.8 0.0 copy-start
  228.8 7.5 %bitcast_convert_fusion = f32[1,768,3072]{2,1,0:T(8,128)} fusion(bf16[768,3072]{1,0:T(8,128)(2,1)} %get-tuple-element.15), kind=kLoop, calls=%fused_computation | loop fusion | flops 2359296 | bytes 14155776 | tf_op jit(solution)/shard_map/broadcast_in_dim | solution.py:983
  236.3 0.0 copy-start.2
  236.3 0.0 copy-start.1
  236.3 0.0 copy-done
  236.3 2.5 %convert_element_type.2 = f32[1536,768]{1,0:T(8,128)} convert(bf16[1536,768]{1,0:T(8,128)(2,1)S(1)} %copy-done) | non-fusion elementwise | flops 1179648 | bytes 7077888 | tf_op jit(solution)/shard_map/convert_element_type | solution.py:977
  238.8 0.0 copy-done.2
  238.9 0.1 bitcast_convert_fusion.1
  238.9 1.4 copy.18
  240.4 0.0 copy-done.1
  240.4 0.7 copy.21
Async XLA Ops:
  228.8 7.5 %copy-start = (bf16[1536,768]{1,0:T(8,128)(2,1)S(1)}, bf16[1536,768]{1,0:T(8,128)(2,1)}, u32[]{:S(2)}) copy-start(bf16[1536,768]{1,0:T(8,128)(2,1)} %get-tuple-element.16) | copy-start | bytes 7077892
  236.3 2.6 %copy-start.2 = (bf16[14,14,768]{2,1,0:T(8,128)(2,1)S(1)}, bf16[14,14,768]{2,1,0:T(8,128)(2,1)}, u32[]{:S(2)}) copy-start(bf16[14,14,768]{2,1,0:T(8,128)(2,1)} %get-tuple-element.14) | copy-start | bytes 903172
  236.3 4.1 %copy-start.1 = (bf16[14,14,768]{2,1,0:T(8,128)(2,1)S(1)}, bf16[14,14,768]{2,1,0:T(8,128)(2,1)}, u32[]{:S(2)}) copy-start(bf16[14,14,768]{2,1,0:T(8,128)(2,1)} %get-tuple-element.13) | copy-start | bytes 903172

commit v5 on v4

--- a/solution.py
+++ b/solution.py
@@ -287,6 +287,8 @@
     stage, c = s // 2, lax.rem(s, 2)
     mate = (dp, stage * 2 + (1 - c))
     opposite = (dp, (1 - stage) * 2 + c)
+    diagonal = (dp, 3 - s)
+    lender, helper = s == 0, s == 3
     early = stage == 0
 
     spot = lax.rem(dp, n)
@@ -305,7 +307,7 @@
         partners.append((jnp.where(lax.rem(spot // bit, 2) == 0, dp + bit, dp - bit), s))
 
     barrier = pltpu.get_barrier_semaphore()
-    peers = [mate, opposite, *nexts, *partners]
+    peers = [mate, opposite, diagonal, *nexts, *partners]
     for peer in peers:
         pl.semaphore_signal(barrier, inc=1, device_id=peer, device_id_type=MESH)
     pl.semaphore_wait(barrier, len(peers))
@@ -474,26 +476,35 @@
             cols = lanes(j, TAIL)
             terms = [(ab.at[m, :, mine], gin.at[m, :, side]) for m in range(2)]
             terms += [(rA.at[m, :, cols], rG.at[m, :, side]) for m in range(2)]
-        else:
+        elif sub == 2:
             block = j // 2 * 2 * REST
             mine = pl.ds(pl.multiple_of(c * (FF // 2) + LATER + block, LANE), 2 * REST)
             cols = pl.ds(pl.multiple_of(LATER + block, LANE), 2 * REST)
-            sent = pl.ds(pl.multiple_of(block, LANE), 2 * REST)
             terms = [(ab.at[m, :, mine], gin.at[m, :, side]) for m in range(2)]
             terms += [(rA.at[m, :, cols], rG.at[m, :, side]) for m in range(2)]
-            own = pick(products(terms), j)
-            terms = [(xA.at[m, :, sent], gout.at[m, :, side]) for m in range(2)]
-            terms += [(xA.at[2 + m, :, sent], xG.at[m, :, side]) for m in range(2)]
-            return jnp.concatenate([own, pick(products(terms), j)], axis=0)
+            return pick(products(terms), j)
+        else:
+            cols = lanes(j // 2, 2 * REST)
+            terms = [(xA.at[m, :, cols], xG.at[m, :, side]) for m in range(2)]
+            terms += [(xA.at[2 + m, :, cols], gout.at[m, :, side]) for m in range(2)]
+            return pick(products(terms), j)
         return products(terms)
 
-    parts = (pl.ds(0, COLS), pl.ds(COLS, TAIL), pl.ds(COLS + TAIL, 2 * REST))
+    parts = (pl.ds(0, COLS), pl.ds(COLS, TAIL), pl.ds(COLS + TAIL, REST), pl.ds(COLS + TAIL + REST, REST))
+    active = (None, None, jnp.logical_not(lender), helper)
+
+    def where_active(sub, run):
+        if active[sub] is None:
+            run()
+        else:
+            pl.when(active[sub])(run)
+
 
     def gathered(sub, h, j):
         if sub == 0:
             return wf.at[0, pl.ds(h * COLS, COLS), lanes(j, COLS)]
-        start = j * TAIL if sub == 1 else 2 * LATER + j * 2 * REST
-        return w2.at[pl.ds(pl.multiple_of(start, 16), TAIL if sub == 1 else 2 * REST), pl.ds(h * COLS, COLS)]
+        first_row, count = ((0, TAIL), (LATER, REST), (2 * LATER, REST))[sub - 1]
+        return w2.at[pl.ds(pl.multiple_of(first_row + j * count, 16), count), pl.ds(h * COLS, COLS)]
 
     def scatter(h, t, sub):
         src, dst = buf.at[h, t, parts[sub], :], buf.at[h, t + 1, parts[sub], :]
@@ -506,29 +517,19 @@
     def write(h, j, sub):
         if sub == 0:
             dst = out1.at[pl.ds(h * COLS, COLS), lanes(j, COLS)]
-        elif sub == 1:
-            dst = out2.at[pl.ds(pl.multiple_of(j * TAIL, 16), TAIL), pl.ds(h * COLS, COLS)]
         else:
-            dst = out2.at[pl.ds(pl.multiple_of(LATER + j * REST, 16), REST), pl.ds(h * COLS, COLS)]
-            return pltpu.make_async_copy(gathered(sub, h, j).at[pl.ds(0, REST), :], dst, osem.at[h, j, sub])
+            first_row, count = ((0, TAIL), (LATER, REST), (LATER, REST))[sub - 1]
+            dst = out2.at[pl.ds(pl.multiple_of(first_row + j * count, 16), count), pl.ds(h * COLS, COLS)]
+        if sub == 3:
+            return remote(gathered(sub, h, j), dst, bs.at[h, j], br.at[h, j], diagonal)
         return pltpu.make_async_copy(gathered(sub, h, j), dst, osem.at[h, j, sub])
 
-    def give_back(h, j):
-        src = w2.at[pl.ds(pl.multiple_of(2 * LATER + j * 2 * REST + REST, 16), REST), pl.ds(h * COLS, COLS)]
-        dst = out2.at[pl.ds(pl.multiple_of(LATER + j * REST, 16), REST), pl.ds(h * COLS, COLS)]
-        return remote(src, dst, bs.at[h, j], br.at[h, j], opposite)
-
-    def deliver(h, j, sub):
-        write(h, j, sub).start()
-        if sub == 2:
-            give_back(h, j).start()
-
     def lend(m):
-        own = ab.at[m, :, pl.ds(pl.multiple_of(c * (FF // 2) + LATER, LANE), FF // 2 - LATER)]
+        own = ab.at[m, :, pl.ds(LATER, FF // 2 - LATER)]
         other = rA.at[m, :, pl.ds(LATER, FF // 2 - LATER)]
         return (
-            remote(own, xA.at[m], xs.at[m], xr.at[m], opposite),
-            remote(other, xA.at[2 + m], xs.at[2 + m], xr.at[2 + m], opposite),
+            remote(own, xA.at[m], xs.at[m], xr.at[m], diagonal),
+            remote(other, xA.at[2 + m], xs.at[2 + m], xr.at[2 + m], diagonal),
         )
 
     def share(m):
@@ -555,7 +556,7 @@
             gathered(sub, h, j)[...] = (total + buf[h, n - 1, parts[sub], :].astype(F32)).astype(BF)
             pl.semaphore_wait(free.at[h, sub], 1)
             spread(h, 0, sub, j).start()
-            deliver(h, j, sub)
+            write(h, j, sub).start()
 
     def event(sub, e):
         for h in range(2):
@@ -574,10 +575,11 @@
                 def _():
                     spread(h, t, sub, j).start()
 
-                deliver(h, j, sub)
+                write(h, j, sub).start()
 
     def early_event(e):
         event(1, e)
+        where_active(2, lambda: event(2, e))
 
         @pl.when(c == 1)
         def _():
@@ -659,6 +661,9 @@
         @pl.when(early & (m == 1))
         def _():
             wait_factors("F")
+
+        @pl.when(lender & (m == 1))
+        def _():
             for i in range(2):
                 for copy in lend(i):
                     copy.start()
@@ -732,6 +737,9 @@
         @pl.when(jnp.logical_not(early))
         def _():
             g_hop(m).start()
+
+        @pl.when(s == 2)
+        def _():
             share(m).start()
 
         @pl.when(early)
@@ -764,12 +772,12 @@
     lax.fori_loop(0, 4, phase, 0)
 
     for h in range(2):
-        for sub in range(2):
-            pl.semaphore_signal(free.at[h, sub], inc=1, device_id=nexts[1 - h], device_id_type=MESH)
-
-        @pl.when(jnp.logical_not(early))
-        def _():
-            pl.semaphore_signal(free.at[h, 2], inc=1, device_id=nexts[1 - h], device_id_type=MESH)
+        for sub in range(4):
+
+            def ready():
+                pl.semaphore_signal(free.at[h, sub], inc=1, device_id=nexts[1 - h], device_id_type=MESH)
+
+            where_active(sub, ready)
 
     for sec in range(2):
         for j in range(12):
@@ -779,7 +787,7 @@
     give.start()
     wait_factors("GA")
 
-    @pl.when(jnp.logical_not(early))
+    @pl.when(helper)
     def _():
         for m in range(2):
             for copy in lend(m):
@@ -788,11 +796,8 @@
 
     def ring_step(t, carry):
         event(1, t + EARLY)
-
-        @pl.when(jnp.logical_not(early))
-        def _():
-            event(2, t)
-
+        where_active(2, lambda: event(2, t + EARLY))
+        where_active(3, lambda: event(3, t))
         event(0, t + jnp.where(c == 1, EARLY, 0))
         for r in range(rounds + 1):
 
@@ -829,14 +834,13 @@
 
     def drain(t, carry):
         for h in range(2):
-            for sub in range(2):
-                scatter(h, t, sub).wait_send()
-                spread(h, t, sub, home(h, t)).wait_send()
-
-            @pl.when(jnp.logical_not(early))
-            def _():
-                scatter(h, t, 2).wait_send()
-                spread(h, t, 2, home(h, t)).wait_send()
+            for sub in range(4):
+
+                def sent():
+                    scatter(h, t, sub).wait_send()
+                    spread(h, t, sub, home(h, t)).wait_send()
+
+                where_active(sub, sent)
 
         return carry
 
@@ -844,28 +848,35 @@
 
     def written(j, carry):
         for h in range(2):
-            for sub in range(2):
-                write(h, j, sub).wait()
-
-            @pl.when(early)
+            for sub in range(3):
+                where_active(sub, lambda: write(h, j, sub).wait())
+
+            @pl.when(helper)
             def _():
-                give_back(h, j).wait_recv()
-
-            @pl.when(jnp.logical_not(early))
+                write(h, j, 3).wait_send()
+
+            @pl.when(lender)
             def _():
-                write(h, j, 2).wait()
-                give_back(h, j).wait_send()
+                write(h, j, 3).wait_recv()
 
         return carry
 
     lax.fori_loop(0, n, written, 0)
+
+    @pl.when(lender)
+    def _():
+        for m in range(2):
+            for copy in lend(m):
+                copy.wait_send()
+
+    @pl.when(s == 2)
+    def _():
+        for m in range(2):
+            share(m).wait_send()
 
     @pl.when(early)
     def _():
         cot_out.wait_send()
-        for m in range(2):
-            for copy in lend(m):
-                copy.wait_send()
         pltpu.make_async_copy(flat.at[0], ing, es.at[1]).wait()
         remote(flat.at[1], ing, es.at[1], er.at[1], opposite).wait_send()
         remote(flat.at[0], act, es.at[0], er.at[0], opposite).wait_recv()
@@ -875,7 +886,6 @@
         img_out.wait_send()
         for m in range(2):
             g_hop(m).wait_send()
-            share(m).wait_send()
         remote(flat.at[0], act, es.at[0], er.at[0], opposite).wait_send()
         pltpu.make_async_copy(flat.at[1], act, es.at[0]).wait()
         remote(flat.at[1], ing, es.at[1], er.at[1], opposite).wait_recv()
@@ -947,8 +957,8 @@
             dma((2,)),
             dma((2,)),
             dma((2,)),
-            dma((2, 2 * RING, 3)),
-            dma((2, 2 * RING, 3)),
+            dma((2, 2 * RING, 4)),
+            dma((2, 2 * RING, 4)),
             dma((2, RING, 3)),
             dma((rounds,)),
             dma((rounds,)),
@@ -958,13 +968,74 @@
             dma((2,)),
             dma((2, RING)),
             dma((2, RING)),
-            pltpu.SemaphoreType.REGULAR((2, 3)),
+            pltpu.SemaphoreType.REGULAR((2, 4)),
         ],
         name="relay",
         compiler_params=pltpu.CompilerParams(
             collective_id=1, has_side_effects=True, vmem_limit_bytes=62 * 2**20
         ),
     )(wrows, wcols, img, cot, kern, bias, gain, move, first, second)
+
+
+STEPS = 8
+
+
+def finish_kernel(out1, out2, act, ing, outs, first, second, acts, ings, kern, bias, gain, move, sem):
+    first[...] = out1[...].astype(F32)
+    second[...] = out2[...].astype(F32)
+    step = pl.program_id(0)
+    copy = pltpu.make_async_copy(act, acts, sem.at[0])
+
+    @pl.when(step == 0)
+    def _():
+        copy.start()
+        for k in range(9):
+            kern[k] = outs[k : k + 1, :]
+        bias[...] = outs[9:10, :]
+        gain[...] = outs[10:11, :]
+        move[...] = outs[11:12, :]
+        for r in range(GRID):
+            line = ing[r].astype(F32)
+            for k in range(GRID):
+                ings[r, k] = line[k : k + 1, :]
+
+    @pl.when(step == STEPS - 1)
+    def _():
+        copy.wait()
+
+
+def finish(out1, out2, act, ing, outs):
+    shape = jax.ShapeDtypeStruct
+    slot = act.shape
+
+    def split(like):
+        return pl.BlockSpec((like.shape[0] // STEPS,) + like.shape[1:], lambda i: (i, 0))
+
+    def whole(dims):
+        return pl.BlockSpec(dims, lambda i: (0,) * len(dims))
+
+    anywhere = pl.BlockSpec(memory_space=pl.ANY)
+    line = (1, D)
+    spread = slot[:2] + line
+    return pl.pallas_call(
+        finish_kernel,
+        grid=(STEPS,),
+        out_shape=[
+            shape(out1.shape, F32),
+            shape(out2.shape, F32),
+            shape(slot, BF),
+            shape(spread, F32),
+            shape((9,) + line, F32),
+            shape(line, F32),
+            shape(line, F32),
+            shape(line, F32),
+        ],
+        in_specs=[split(out1), split(out2), anywhere, whole(slot), whole(outs.shape)],
+        out_specs=[split(out1), split(out2), anywhere, whole(spread), whole((9,) + line)] + [whole(line)] * 3,
+        scratch_shapes=[pltpu.SemaphoreType.DMA((1,))],
+        name="finish",
+        compiler_params=pltpu.CompilerParams(vmem_limit_bytes=60 * 2**20),
+    )(out1, out2, act, ing, outs)
 
 
 def per_device(
@@ -974,18 +1045,18 @@
         window_rows, window_cols, images[0], cotangent[0], pos_kernel[0], pos_bias, norm_gain, norm_shift,
         first_weight[0], second_weight,
     )
-    out1, out2 = out1.astype(F32), out2.astype(F32)
     if lax.axis_size("dp") > RING:
-        out1, out2, outs = lax.psum((out1 / RING, out2 / RING, outs / RING), "dp")
+        out1, out2, outs = lax.psum((out1.astype(F32) / RING, out2.astype(F32) / RING, outs / RING), "dp")
+    out1, out2, act, ing, kern, bias, gain, move = finish(out1, out2, act, ing, outs)
     return (
         act[None],
-        ing.astype(F32)[None],
+        ing.transpose(2, 0, 1, 3),
         out1[None],
         out2,
-        outs[None, :9],
-        outs[9:10],
-        outs[10:11],
-        outs[11:12],
+        kern.transpose(1, 0, 2),
+        bias,
+        gain,
+        move,
     )
 
 

time: 242 us -> 246 us (1.017)
  Pallas kernels: 225 us -> 244 us
  other arithmetic: 10.1 us -> 0 us
  local copies, waits for them, and re-layouts: 5.06 us -> 0 us
    pallas_call x0 -> x1, Pallas kernels: none -> 14.4 us  [finish(): pl.pallas_call(finish_kernel, grid=(STEPS,), out_shape=[shape(out1.shape,...]
    broadcast_in_dim x2 -> x0, other arithmetic: 7.58 us -> none  [the longest x1 7.52 us: per_device(): out1[None]]
    pallas_call x1, Pallas kernels: 225 us -> 230 us  [relay(): pl.pallas_call(relay_kernel, out_shape=[shape(slot, BF), shape(slot, BF),...]
    unnamed x9 -> x0, local copies, waits for them, and re-layouts: 2.82 us -> none
    convert_element_type x1 -> x0, other arithmetic: 2.54 us -> none  [per_device(): out1, out2 = (out1.astype(F32), out2.astype(F32))]
where the time goes in v5:
time: 246 us; the launch traced here: 245 us
  Pallas kernels  244 us (99%)
    pallas_call x1, Pallas kernels, relay(): pl.pallas_call(relay_kernel, out_shape=[shape(slot, BF), shape(slot, BF),...  230 us
    pallas_call x1, Pallas kernels, finish(): pl.pallas_call(finish_kernel, grid=(STEPS,), out_shape=[shape(out1.shape,...  14.4 us

profile of v5, /device:TPU:0, one launch (start us, length us, event | category | flops | bytes accessed | tf_op | source)
XLA Modules:
  0.0 245.3 jit_solution(15565884879808755987)
XLA Ops:
  0.6 230.1 %relay.1 = (bf16[14,14,768]{2,1,0:T(8,128)(2,1)}, bf16[14,14,768]{2,1,0:T(8,128)(2,1)}, bf16[768,3072]{1,0:T(8,128)(2,1)}, bf16[1536,768]{1,0:T(8,128)(2,1)}, f32[16,768]{1,0:T(8,128)}) custom-call(s32[4]{0:T(128)} %wrows.1, s32[4]{0:T(128)} %wcols.1, bf16[14,14,768]{2,1,0:T(8,128)(2,1)} %bitcast.9, bf16[14,14,768]{2,1,0:T(8,128)(2,1)} %bitcast.10, ...), custom_call_target="tpu_custom_call" | custom-call | tf_op jit(solution)/shard_map/relay/pallas_call | solution.py:903
  230.8 14.4 %finish.1 = (f32[768,3072]{1,0:T(8,128)}, f32[1536,768]{1,0:T(8,128)}, bf16[14,14,768]{2,1,0:T(8,128)(2,1)}, f32[14,14,1,768]{3,2,1,0:T(1,128)}, f32[9,1,768]{2,...) custom-call(bf16[768,3072]{1,0:T(8,128)(2,1)} %get-tuple-element.21.out1, ...), custom_call_target="tpu_custom_call" | custom-call | tf_op jit(solution)/shard_map/finish/pallas_call | solution.py:1020

commit v6 on v5

--- a/solution.py
+++ b/solution.py
@@ -194,7 +194,7 @@
         p = [x * (1.0 / jnp.sum(x, axis=1, keepdims=True)) for x in p]
         p = [x.reshape(PACK * WROWS, WROWS) for x in p]
         for w in range(2):
-            pw[m, 2 * i + w] = p[w]
+            pw[m, 2 * i + w, :, 0:WROWS] = p[w]
         out = [dot(x.astype(BF), v, 0, 0) for x, v in zip(p, vd)]
         for w in range(2):
             T[rows[w], cols[0]] = out[w]
@@ -207,7 +207,7 @@
     def unit(i, carry):
         rows, cols, head_of_lane, q, kd, vd = window_parts(m, i, qkv)
         g = [T[r, cols[0]].astype(BF) for r in rows]
-        p = [pw[m, 2 * i + w].reshape(PACK, WROWS, WROWS) for w in range(2)]
+        p = [pw[m, 2 * i + w, :, 0:WROWS].reshape(PACK, WROWS, WROWS) for w in range(2)]
         dp = [dot(v, x, 1, 1).reshape(PACK, WROWS, WROWS) for v, x in zip(vd, g)]
         ds = [x * (y - jnp.sum(x * y, axis=1, keepdims=True)) for x, y in zip(p, dp)]
         ds = [x.reshape(PACK * WROWS, WROWS).astype(BF) for x in ds]
@@ -228,7 +228,7 @@
     return [pl.ds(pl.multiple_of(part * D + group * GROUP, LANE), GROUP) for part in range(3)]
 
 
-def channel_forward(m, qkv, pc, T, msk):
+def channel_forward(m, qkv, pw, T, msk):
     def unit(i, carry):
         cols = group_slices(i)
         mask = msk[m][:, :1]
@@ -240,14 +240,15 @@
         s = jnp.where(same, s, -1e30)
         p = jnp.exp(s - jnp.max(s, axis=1, keepdims=True))
         p = p * (1.0 / jnp.sum(p, axis=1, keepdims=True))
-        pc[m, i] = p
+        for k in range(GROUP // LANE):
+            pw[m, 2 * i + k, 0:GROUP, :] = p[:, k * LANE : (k + 1) * LANE]
         T[:, cols[0]] = dot(v, p.astype(BF), 1, 1)
         return carry
 
     lax.fori_loop(0, NGROUP, unit, 0, unroll=True)
 
 
-def channel_backward(m, qkv, pc, T, msk):
+def channel_backward(m, qkv, pw, T, msk):
     def unit(i, carry):
         cols = group_slices(i)
         mask = msk[m][:, :1]
@@ -255,7 +256,7 @@
         k = (qkv[m, :, cols[1]] * mask).astype(BF)
         v = qkv[m, :, cols[2]].astype(BF)
         g = T[:, cols[0]].astype(BF)
-        p = pc[m, i]
+        p = jnp.concatenate([pw[m, 2 * i + k, 0:GROUP, :] for k in range(GROUP // LANE)], axis=1)
         dp = dot(g, v, 0, 0)
         ds = (p * (dp - jnp.sum(p * dp, axis=1, keepdims=True))).astype(BF)
         qkv[m, :, cols[0]] = dot(k, ds, 1, 1) * SCALE
@@ -268,18 +269,18 @@
 
 RING = 8
 COLS = FF // RING
-TAIL = FF // 3 // RING
+WIDE = FF // 12 * 8 // RING
 REST = FF // 6 // RING
-LATER = FF // 3
+FIFTH, SIXTH = FF // 6 * 4, FF // 6 * 5
 EARLY = 2
 
 
 def relay_kernel(
     wrows, wcols, img, cot, kern, bias, gain, move, first, second,
     act, ing, out1, out2, outs,
-    wf, w2, pr, msk, raw, flat, ubuf, gin, gout, zz, xh, rs, qkv, ab, rr, pw, pc, U, C, T, sgp, sgs, sgm,
+    wf, w2, pr, msk, flat, ubuf, gin, gout, zz, xh, rs, qkv, ab, rr, pw, U, C, T, sgp, sgs, sgm,
     rL, rR, rA, rG, xA, xG, buf, acc, got,
-    wl, ws, wr, pl_, usem, gsem, us, gs, ss, rsem, es, er, sgsem, ssem, rcem, osem, sms, smr, xs, xr, ys, yr, bs, br, free,
+    wl, ws, wr, pl_, usem, gsem, us, gs, ss, rsem, es, er, sgsem, ssem, rcem, osem, sms, smr, xs, xr, ys, yr, bs, br, hs, hr, free,
 ):
     n = RING
     s = lax.axis_index("section")
@@ -287,8 +288,7 @@
     stage, c = s // 2, lax.rem(s, 2)
     mate = (dp, stage * 2 + (1 - c))
     opposite = (dp, (1 - stage) * 2 + c)
-    diagonal = (dp, 3 - s)
-    lender, helper = s == 0, s == 3
+    lender, helper = s == 1, s == 3
     early = stage == 0
 
     spot = lax.rem(dp, n)
@@ -307,7 +307,7 @@
         partners.append((jnp.where(lax.rem(spot // bit, 2) == 0, dp + bit, dp - bit), s))
 
     barrier = pltpu.get_barrier_semaphore()
-    peers = [mate, opposite, diagonal, *nexts, *partners]
+    peers = [mate, opposite, *nexts, *partners]
     for peer in peers:
         pl.semaphore_signal(barrier, inc=1, device_id=peer, device_id_type=MESH)
     pl.semaphore_wait(barrier, len(peers))
@@ -359,6 +359,7 @@
         def _():
             (weight_copies(k)[1][i] if i < 5 else params_copy(k)).wait_recv()
 
+    raw = flat.at[0]
     img_out = remote(img, raw, pl_.at[0], pl_.at[1], opposite)
     cot_out = remote(cot, raw, pl_.at[0], pl_.at[1], opposite)
 
@@ -394,6 +395,15 @@
         inside = (row < WIN * wrows[c + 2 * m]) & (column < WIN * wcols[c + 2 * m]) & (cell < WIN)
         msk[m] = jnp.where(inside, 1.0, 0.0)
 
+    @pl.when(jnp.logical_not(early))
+    def _():
+        cot_out.wait_recv()
+        pad(raw, gin.at[0])
+        for m in range(2):
+            for l in range(D // LANE):
+                cols = pl.ds(l * LANE, LANE)
+                gin[m, :, cols] = (gin[m, :, cols].astype(F32) * msk[m]).astype(BF)
+
     for wc in range(SIDE):
         U[wc, 0] = jnp.zeros((CELL, D), F32)
         U[wc, GRID + 1] = jnp.zeros((CELL, D), F32)
@@ -410,15 +420,13 @@
             parts = [
                 ("F", zz.at[m, 0], rL.at[m, 0]),
                 ("F", zz.at[m, 1], rL.at[m, 1]),
-                ("F", ab.at[m, :, pl.ds(0, FF // 2)], rA.at[m]),
-                ("M", gin.at[m], rG.at[m]),
                 ("G", rr.at[m, 0, :, pl.ds(3 * D, D)], rR.at[m, :, pl.ds(3 * D, D)]),
                 ("A", rr.at[m, 0, :, pl.ds(0, 3 * D)], rR.at[m, :, pl.ds(0, 3 * D)]),
             ]
         else:
             parts = [
                 ("F", zz.at[m, 2], rL.at[m, 0]),
-                ("F", ab.at[m, :, pl.ds(FF // 2, FF // 2)], rA.at[m]),
+                ("F", ab.at[m], rA.at[m]),
                 ("M", gin.at[m], rG.at[m]),
                 ("M", rr.at[m, 1], rR.at[m]),
             ]
@@ -472,26 +480,27 @@
             terms = [(zz.at[m, own, :, side], rr.at[m, c, :, cols]) for m in range(2)]
             terms += [(rL.at[m, other, :, side], rR.at[m, :, cols]) for m in range(2)]
         elif sub == 1:
-            mine = pl.ds(pl.multiple_of(c * (FF // 2) + j * TAIL, LANE), TAIL)
-            cols = lanes(j, TAIL)
-            terms = [(ab.at[m, :, mine], gin.at[m, :, side]) for m in range(2)]
+            cols = lanes(j, WIDE)
+            terms = [(ab.at[m, :, cols], gin.at[m, :, side]) for m in range(2)]
             terms += [(rA.at[m, :, cols], rG.at[m, :, side]) for m in range(2)]
-        elif sub == 2:
-            block = j // 2 * 2 * REST
-            mine = pl.ds(pl.multiple_of(c * (FF // 2) + LATER + block, LANE), 2 * REST)
-            cols = pl.ds(pl.multiple_of(LATER + block, LANE), 2 * REST)
-            terms = [(ab.at[m, :, mine], gin.at[m, :, side]) for m in range(2)]
+        else:
+            start = (FIFTH if sub == 2 else SIXTH) + j // 2 * 2 * REST
+            cols = pl.ds(pl.multiple_of(start, LANE), 2 * REST)
+            terms = [(ab.at[m, :, cols], gin.at[m, :, side]) for m in range(2)]
             terms += [(rA.at[m, :, cols], rG.at[m, :, side]) for m in range(2)]
-            return pick(products(terms), j)
-        else:
+            own = pick(products(terms), j)
+            if sub == 2:
+                return own
             cols = lanes(j // 2, 2 * REST)
-            terms = [(xA.at[m, :, cols], xG.at[m, :, side]) for m in range(2)]
-            terms += [(xA.at[2 + m, :, cols], gout.at[m, :, side]) for m in range(2)]
-            return pick(products(terms), j)
+            terms = [(xA.at[m, :, cols], gout.at[m, :, side]) for m in range(2)]
+            terms += [(xA.at[2 + m, :, cols], xG.at[m, :, side]) for m in range(2)]
+            return jnp.concatenate([own, pick(products(terms), j)], axis=0)
         return products(terms)
 
-    parts = (pl.ds(0, COLS), pl.ds(COLS, TAIL), pl.ds(COLS + TAIL, REST), pl.ds(COLS + TAIL + REST, REST))
-    active = (None, None, jnp.logical_not(lender), helper)
+    sizes = (COLS, WIDE, REST, 2 * REST)
+    parts = [pl.ds(sum(sizes[:i]), size) for i, size in enumerate(sizes)]
+    odd = c == 1
+    active = (None, odd, odd, helper)
 
     def where_active(sub, run):
         if active[sub] is None:
@@ -503,8 +512,11 @@
     def gathered(sub, h, j):
         if sub == 0:
             return wf.at[0, pl.ds(h * COLS, COLS), lanes(j, COLS)]
-        first_row, count = ((0, TAIL), (LATER, REST), (2 * LATER, REST))[sub - 1]
-        return w2.at[pl.ds(pl.multiple_of(first_row + j * count, 16), count), pl.ds(h * COLS, COLS)]
+        if sub == 3:
+            rows = pl.ds(pl.multiple_of(lax.rem(j, n // 2) * sizes[3], 16), sizes[3])
+            return wf.at[1, rows, lanes(2 * (j // (n // 2)) + h, COLS)]
+        first_row = 0 if sub == 1 else FIFTH
+        return w2.at[pl.ds(pl.multiple_of(first_row + j * sizes[sub], 16), sizes[sub]), pl.ds(h * COLS, COLS)]
 
     def scatter(h, t, sub):
         src, dst = buf.at[h, t, parts[sub], :], buf.at[h, t + 1, parts[sub], :]
@@ -514,22 +526,47 @@
         ref = gathered(sub, h, j)
         return remote(ref, ref, ssem.at[h, n - 1 + t, sub], rcem.at[h, n + t, sub], nexts[h])
 
-    def write(h, j, sub):
+    half_shards = n * 3 // 4
+
+    def write(h, j, sub, part=0):
+        src, side = gathered(sub, h, j), pl.ds(h * COLS, COLS)
         if sub == 0:
-            dst = out1.at[pl.ds(h * COLS, COLS), lanes(j, COLS)]
+            dst = out1.at[side, lanes(j, COLS)]
+        elif sub == 1:
+            dst = out2.at[pl.ds(pl.multiple_of((j - half_shards) * WIDE, 16), WIDE), side]
         else:
-            first_row, count = ((0, TAIL), (LATER, REST), (LATER, REST))[sub - 1]
-            dst = out2.at[pl.ds(pl.multiple_of(first_row + j * count, 16), count), pl.ds(h * COLS, COLS)]
-        if sub == 3:
-            return remote(gathered(sub, h, j), dst, bs.at[h, j], br.at[h, j], diagonal)
-        return pltpu.make_async_copy(gathered(sub, h, j), dst, osem.at[h, j, sub])
+            first_row = (FIFTH if sub == 2 else SIXTH) - FF // 2
+            dst = out2.at[pl.ds(pl.multiple_of(first_row + j * REST, 16), REST), side]
+            src = src.at[pl.ds(part * REST, REST), :]
+        if part == 1:
+            return remote(src, dst, bs.at[h, j], br.at[h, j], opposite)
+        return pltpu.make_async_copy(src, dst, osem.at[h, j, sub])
+
+    def hand_over(h, j):
+        dst = out2.at[pl.ds(pl.multiple_of(j * WIDE, 16), WIDE), pl.ds(h * COLS, COLS)]
+        return remote(gathered(1, h, j), dst, hs.at[h, j], hr.at[h, j], mate)
+
+    def deliver(h, j, sub):
+        if sub == 1:
+
+            @pl.when(j < half_shards)
+            def _():
+                hand_over(h, j).start()
+
+            @pl.when(j >= half_shards)
+            def _():
+                write(h, j, sub).start()
+
+        else:
+            write(h, j, sub).start()
+            if sub == 3:
+                write(h, j, sub, 1).start()
 
     def lend(m):
-        own = ab.at[m, :, pl.ds(LATER, FF // 2 - LATER)]
-        other = rA.at[m, :, pl.ds(LATER, FF // 2 - LATER)]
+        cols = pl.ds(SIXTH, FF - SIXTH)
         return (
-            remote(own, xA.at[m], xs.at[m], xr.at[m], diagonal),
-            remote(other, xA.at[2 + m], xs.at[2 + m], xr.at[2 + m], diagonal),
+            remote(ab.at[m, :, cols], xA.at[m], xs.at[m], xr.at[m], opposite),
+            remote(rA.at[m, :, cols], xA.at[2 + m], xs.at[2 + m], xr.at[2 + m], opposite),
         )
 
     def share(m):
@@ -556,7 +593,7 @@
             gathered(sub, h, j)[...] = (total + buf[h, n - 1, parts[sub], :].astype(F32)).astype(BF)
             pl.semaphore_wait(free.at[h, sub], 1)
             spread(h, 0, sub, j).start()
-            write(h, j, sub).start()
+            deliver(h, j, sub)
 
     def event(sub, e):
         for h in range(2):
@@ -575,15 +612,13 @@
                 def _():
                     spread(h, t, sub, j).start()
 
-                write(h, j, sub).start()
+                deliver(h, j, sub)
 
     def early_event(e):
-        event(1, e)
-        where_active(2, lambda: event(2, e))
-
-        @pl.when(c == 1)
-        def _():
-            event(0, e)
+        @pl.when(odd)
+        def _():
+            for sub in range(3):
+                event(sub, e)
 
     def small(r):
         return remote(acc.at[r], got.at[r], sms.at[r], smr.at[r], partners[r])
@@ -617,7 +652,7 @@
 
         @pl.when(jnp.logical_not(early))
         def _():
-            channel_forward(m, qkv, pc, T, msk)
+            channel_forward(m, qkv, pw, T, msk)
 
         first_time(0, 3)
         zz[m, 1] = T[...].astype(BF)
@@ -672,17 +707,6 @@
         @pl.when(early)
         def _():
             g_hop(m).wait_recv()
-
-        @pl.when(jnp.logical_not(early))
-        def _():
-            @pl.when(m == 0)
-            def _():
-                cot_out.wait_recv()
-                pad(raw, gin.at[0])
-
-            for l in range(D // LANE):
-                cols = pl.ds(l * LANE, LANE)
-                gin[m, :, cols] = (gin[m, :, cols].astype(F32) * msk[m]).astype(BF)
 
         for t in range(FF // FTILE):
             cols = pl.ds(t * FTILE, FTILE)
@@ -719,7 +743,7 @@
 
         @pl.when(jnp.logical_not(early))
         def _():
-            channel_backward(m, qkv, pc, T, msk)
+            channel_backward(m, qkv, pw, T, msk)
 
         for i in range(3):
             cols = pl.ds(i * D, D)
@@ -795,10 +819,10 @@
             share(m).wait_recv()
 
     def ring_step(t, carry):
-        event(1, t + EARLY)
+        event(0, t + jnp.where(odd, EARLY, 0))
+        where_active(1, lambda: event(1, t + EARLY))
         where_active(2, lambda: event(2, t + EARLY))
         where_active(3, lambda: event(3, t))
-        event(0, t + jnp.where(c == 1, EARLY, 0))
         for r in range(rounds + 1):
 
             @pl.when(t == 1 + 3 * r)
@@ -848,16 +872,32 @@
 
     def written(j, carry):
         for h in range(2):
-            for sub in range(3):
-                where_active(sub, lambda: write(h, j, sub).wait())
+            write(h, j, 0).wait()
+
+            @pl.when(odd)
+            def _():
+                write(h, j, 2).wait()
+
+                @pl.when(j < half_shards)
+                def _():
+                    hand_over(h, j).wait_send()
+
+                @pl.when(j >= half_shards)
+                def _():
+                    write(h, j, 1).wait()
+
+            @pl.when(jnp.logical_not(odd) & (j < half_shards))
+            def _():
+                hand_over(h, j).wait_recv()
 
             @pl.when(helper)
             def _():
-                write(h, j, 3).wait_send()
+                write(h, j, 3).wait()
+                write(h, j, 3, 1).wait_send()
 
             @pl.when(lender)
             def _():
-                write(h, j, 3).wait_recv()
+                write(h, j, 3, 1).wait_recv()
 
         return carry
 
@@ -916,7 +956,6 @@
             pltpu.VMEM((FF, D), BF),
             pltpu.VMEM((2, 16, D), F32),
             pltpu.VMEM((2, ROWS, LANE), F32),
-            pltpu.VMEM(slot, BF),
             pltpu.VMEM((2,) + slot, BF),
             pltpu.VMEM((2, 2) + image, BF),
             pltpu.VMEM((2,) + image, BF),
@@ -927,8 +966,7 @@
             pltpu.VMEM((2, ROWS, 3 * D), F32),
             pltpu.VMEM((2, ROWS, FF), BF),
             pltpu.VMEM((2, 2, ROWS, FF), BF),
-            pltpu.VMEM((2, UNITS, PACK * WROWS, WROWS), F32),
-            pltpu.VMEM((2, NGROUP, GROUP, GROUP), F32),
+            pltpu.VMEM((2, UNITS, PACK * WROWS, LANE), F32),
             pltpu.VMEM((SIDE, GRID + 2, CELL, D), F32),
             pltpu.VMEM(image, F32),
             pltpu.VMEM(image, F32),
@@ -937,11 +975,11 @@
             pltpu.VMEM((16, D), F32),
             pltpu.VMEM((2, 2) + image, BF),
             pltpu.VMEM((2, ROWS, FF), BF),
-            pltpu.VMEM((2, ROWS, FF // 2), BF),
+            pltpu.VMEM((2, ROWS, FF), BF),
             pltpu.VMEM((2,) + image, BF),
-            pltpu.VMEM((4, ROWS, FF // 2 - LATER), BF),
+            pltpu.VMEM((4, ROWS, FF - SIXTH), BF),
             pltpu.VMEM((2,) + image, BF),
-            pltpu.VMEM((2, RING, COLS + TAIL + 2 * REST, COLS), BF),
+            pltpu.VMEM((2, RING, COLS + WIDE + 3 * REST, COLS), BF),
             pltpu.VMEM((rounds + 1, 16, D), F32),
             pltpu.VMEM((rounds, 16, D), F32),
             dma((5,)),
@@ -959,7 +997,7 @@
             dma((2,)),
             dma((2, 2 * RING, 4)),
             dma((2, 2 * RING, 4)),
-            dma((2, RING, 3)),
+            dma((2, RING, 4)),
             dma((rounds,)),
             dma((rounds,)),
             dma((4,)),
@@ -968,58 +1006,74 @@
             dma((2,)),
             dma((2, RING)),
             dma((2, RING)),
+            dma((2, RING)),
+            dma((2, RING)),
             pltpu.SemaphoreType.REGULAR((2, 4)),
         ],
         name="relay",
         compiler_params=pltpu.CompilerParams(
-            collective_id=1, has_side_effects=True, vmem_limit_bytes=62 * 2**20
+            collective_id=1, has_side_effects=True, vmem_limit_bytes=63 * 2**20
         ),
     )(wrows, wcols, img, cot, kern, bias, gain, move, first, second)
 
 
-STEPS = 8
-
-
-def finish_kernel(out1, out2, act, ing, outs, first, second, acts, ings, kern, bias, gain, move, sem):
-    first[...] = out1[...].astype(F32)
-    second[...] = out2[...].astype(F32)
-    step = pl.program_id(0)
-    copy = pltpu.make_async_copy(act, acts, sem.at[0])
-
-    @pl.when(step == 0)
-    def _():
+def finish_kernel(
+    out1, out2, act, ing, outs, first, second, acts, ings, kern, bias, gain, move,
+    raw1, raw2, full1, full2, acted, graded, wide, small, kernels, rsem, wsem,
+):
+    steps = rsem.shape[0] - 3
+
+    loads = [
+        pltpu.make_async_copy(act, acted, rsem.at[steps]),
+        pltpu.make_async_copy(ing, graded, rsem.at[steps + 1]),
+        pltpu.make_async_copy(outs, small, rsem.at[steps + 2]),
+    ]
+    for copy in loads:
         copy.start()
-        for k in range(9):
-            kern[k] = outs[k : k + 1, :]
-        bias[...] = outs[9:10, :]
-        gain[...] = outs[10:11, :]
-        move[...] = outs[11:12, :]
-        for r in range(GRID):
-            line = ing[r].astype(F32)
-            for k in range(GRID):
-                ings[r, k] = line[k : k + 1, :]
-
-    @pl.when(step == STEPS - 1)
-    def _():
+    reads, writes = [], []
+    for i in range(steps):
+        pair = ((out1, raw1, full1, first), (out2, raw2, full2, second))[i % 2]
+        src, raw, full, dst = pair
+        half = steps // 2
+        rows = pl.ds(i // 2 * (src.shape[0] // half), src.shape[0] // half)
+        reads.append((pltpu.make_async_copy(src.at[rows, :], raw.at[rows, :], rsem.at[i]), raw, full, rows))
+        writes.append(pltpu.make_async_copy(full.at[rows, :], dst.at[rows, :], wsem.at[i]))
+    for copy, *_ in reads:
+        copy.start()
+    for (copy, raw, full, rows), back in zip(reads, writes):
+        copy.wait()
+        full[rows, :] = raw[rows, :].astype(F32)
+        back.start()
+    for copy in loads:
+        copy.wait()
+    for k in range(9):
+        kernels[k] = small[k : k + 1, :]
+    for r in range(GRID):
+        line = graded[r].astype(F32)
+        for k in range(GRID):
+            wide[r, k] = line[k : k + 1, :]
+    last = [
+        pltpu.make_async_copy(acted, acts, wsem.at[steps]),
+        pltpu.make_async_copy(wide, ings, wsem.at[steps + 1]),
+        pltpu.make_async_copy(kernels, kern, wsem.at[steps + 2]),
+    ]
+    for i, dst in enumerate((bias, gain, move)):
+        last.append(pltpu.make_async_copy(small.at[pl.ds(9 + i, 1), :], dst, wsem.at[steps + 3 + i]))
+    for copy in last:
+        copy.start()
+    for copy in writes + last:
         copy.wait()
 
 
 def finish(out1, out2, act, ing, outs):
     shape = jax.ShapeDtypeStruct
     slot = act.shape
-
-    def split(like):
-        return pl.BlockSpec((like.shape[0] // STEPS,) + like.shape[1:], lambda i: (i, 0))
-
-    def whole(dims):
-        return pl.BlockSpec(dims, lambda i: (0,) * len(dims))
-
     anywhere = pl.BlockSpec(memory_space=pl.ANY)
     line = (1, D)
     spread = slot[:2] + line
+    steps = 16
     return pl.pallas_call(
         finish_kernel,
-        grid=(STEPS,),
         out_shape=[
             shape(out1.shape, F32),
             shape(out2.shape, F32),
@@ -1030,9 +1084,21 @@
             shape(line, F32),
             shape(line, F32),
         ],
-        in_specs=[split(out1), split(out2), anywhere, whole(slot), whole(outs.shape)],
-        out_specs=[split(out1), split(out2), anywhere, whole(spread), whole((9,) + line)] + [whole(line)] * 3,
-        scratch_shapes=[pltpu.SemaphoreType.DMA((1,))],
+        in_specs=[anywhere] * 5,
+        out_specs=[anywhere] * 8,
+        scratch_shapes=[
+            pltpu.VMEM(out1.shape, out1.dtype),
+            pltpu.VMEM(out2.shape, out2.dtype),
+            pltpu.VMEM(out1.shape, F32),
+            pltpu.VMEM(out2.shape, F32),
+            pltpu.VMEM(slot, BF),
+            pltpu.VMEM(slot, BF),
+            pltpu.VMEM(spread, F32),
+            pltpu.VMEM(outs.shape, F32),
+            pltpu.VMEM((9,) + line, F32),
+            pltpu.SemaphoreType.DMA((steps + 3,)),
+            pltpu.SemaphoreType.DMA((steps + 6,)),
+        ],
         name="finish",
         compiler_params=pltpu.CompilerParams(vmem_limit_bytes=60 * 2**20),
     )(out1, out2, act, ing, outs)

time: 246 us -> 236 us (0.959)
  Pallas kernels: 244 us -> 235 us
    pallas_call x1, Pallas kernels: 14.4 us -> 7.58 us  [finish(): pl.pallas_call(finish_kernel, out_shape=[shape(out1.shape, F32), shape(ou...]
    pallas_call x1, Pallas kernels: 230 us -> 228 us  [relay(): pl.pallas_call(relay_kernel, out_shape=[shape(slot, BF), shape(slot, BF),...]
where the time goes in v6:
time: 236 us
  Pallas kernels  235 us (100%)
    pallas_call x1, Pallas kernels, relay(): pl.pallas_call(relay_kernel, out_shape=[shape(slot, BF), shape(slot, BF),...  228 us
    pallas_call x1, Pallas kernels, finish(): pl.pallas_call(finish_kernel, out_shape=[shape(out1.shape, F32), shape(ou...  7.58 us

profile of v6, /device:TPU:0, one launch (start us, length us, event | category | flops | bytes accessed | tf_op | source)
XLA Modules:
  0.0 236.0 jit_solution(1043918698883140450)
XLA Ops:
  0.6 227.7 %relay.1 = (bf16[14,14,768]{2,1,0:T(8,128)(2,1)}, bf16[14,14,768]{2,1,0:T(8,128)(2,1)}, bf16[768,3072]{1,0:T(8,128)(2,1)}, bf16[1536,768]{1,0:T(8,128)(2,1)}, f32[16,768]{1,0:T(8,128)}) custom-call(s32[4]{0:T(128)} %wrows.1, s32[4]{0:T(128)} %wcols.1, bf16[14,14,768]{2,1,0:T(8,128)(2,1)} %bitcast.9, bf16[14,14,768]{2,1,0:T(8,128)(2,1)} %bitcast.10, ...), custom_call_target="tpu_custom_call" | custom-call | tf_op jit(solution)/shard_map/relay/pallas_call | solution.py:943
  228.3 7.6 %finish.1 = (f32[768,3072]{1,0:T(8,128)}, f32[1536,768]{1,0:T(8,128)}, bf16[14,14,768]{2,1,0:T(8,128)(2,1)}, f32[14,14,1,768]{3,2,1,0:T(1,128)}, f32[9,1,768]{2,...) custom-call(bf16[768,3072]{1,0:T(8,128)(2,1)} %get-tuple-element.21.out1, ...), custom_call_target="tpu_custom_call" | custom-call | tf_op jit(solution)/shard_map/finish/pallas_call | solution.py:1075

commit v7 on v6

--- a/solution.py
+++ b/solution.py
@@ -23,7 +23,7 @@
 NGROUP = D // GROUP
 UNITS = NGROUP * SIDE * SIDE
 LANE = 128
-FTILE = 1024
+FTILE = 512
 EPS = 1e-05
 SCALE = HEAD ** (-0.5)
 BF = jnp.bfloat16
@@ -104,11 +104,12 @@
     lax.fori_loop(0, D // LANE, norm, 0)
 
 
-def front_backward(sec, m, ubuf, msk, pr, U, T, gfull, xh, rs, sgp, out):
+def fold(value):
+    return jnp.sum(value.reshape(ROWS // CELL, CELL, LANE), axis=0)
+
+
+def front_backward(sec, m, msk, pr, U, T, gfull, xh, rs, sgp, out, sent):
     zero = jnp.zeros((ROWS, LANE), F32)
-
-    def fold(value):
-        return jnp.sum(value.reshape(ROWS // CELL, CELL, LANE), axis=0)
 
     def sums(i, carry):
         s1, s2 = carry
@@ -130,29 +131,49 @@
         xhat = xh[sec, m, :, ls].astype(F32)
         inner = T[:, ls] * pr[sec, 10:11, ls] - m1 - xhat * m2
         gc = gfull(i)[...].astype(F32) + rs[sec, m] * inner
-        sgp[sec, 9, :, ls] += fold(gc)
+        xh[sec, m, :, ls] = gc.astype(BF)
         gh = halves(gc)
         U[0, 1 : GRID + 1, :, ls] = gh[0]
         U[1, 1 : GRID + 1, :, ls] = gh[1]
         moved = shifts(U[0, :, :, ls], U[1, :, :, ls])
         taps = pr[sec, :, ls]
         mask = halves(msk[m])
+        du = []
+        for wc in range(SIDE):
+            acc = jnp.zeros((GRID, CELL, LANE), F32)
+            for a in range(3):
+                for b in range(3):
+                    tap = 3 * a + b
+                    acc = acc + moved[wc][2 - b][2 - a : 2 - a + GRID] * taps[tap : tap + 1, :][None]
+            du.append((gh[wc] + mask[wc] * acc).reshape(HALF, LANE))
+        out(i)[...] = jnp.concatenate(du, axis=0).astype(BF)
+        return carry
+
+    lax.fori_loop(0, D // LANE // 2, back, 0)
+    sent(0)
+    lax.fori_loop(D // LANE // 2, D // LANE, back, 0)
+    sent(1)
+
+
+def front_sums(sec, m, ubuf, msk, U, xh, sgp):
+    def part(i, carry):
+        ls = lanes(i)
+        gc = xh[sec, m, :, ls].astype(F32)
+        sgp[sec, 9, :, ls] += fold(gc)
+        gh = halves(gc)
+        U[0, 1 : GRID + 1, :, ls] = gh[0]
+        U[1, 1 : GRID + 1, :, ls] = gh[1]
+        moved = shifts(U[0, :, :, ls], U[1, :, :, ls])
         um = halves(ubuf[sec, m, :, ls].astype(F32) * msk[m])
-        accs = [jnp.zeros((GRID, CELL, LANE), F32) for _ in range(SIDE)]
         for a in range(3):
             for b in range(3):
-                tap = 3 * a + b
                 kg = jnp.zeros((CELL, LANE), F32)
                 for wc in range(SIDE):
-                    gs = moved[wc][2 - b][2 - a : 2 - a + GRID]
-                    accs[wc] = accs[wc] + gs * taps[tap : tap + 1, :][None]
-                    kg = kg + jnp.sum(gs * um[wc], axis=0)
-                sgp[sec, tap, :, ls] += kg
-        du = [(gh[wc] + mask[wc] * accs[wc]).reshape(HALF, LANE) for wc in range(SIDE)]
-        out(i)[...] = jnp.concatenate(du, axis=0).astype(BF)
+                    kg = kg + jnp.sum(moved[wc][2 - b][2 - a : 2 - a + GRID] * um[wc], axis=0)
+                sgp[sec, 3 * a + b, :, ls] += kg
         return carry
 
-    lax.fori_loop(0, D // LANE, back, 0)
+    lax.fori_loop(0, D // LANE, part, 0)
 
 
 def spread_heads(value, head_of_lane):
@@ -228,7 +249,7 @@
     return [pl.ds(pl.multiple_of(part * D + group * GROUP, LANE), GROUP) for part in range(3)]
 
 
-def channel_forward(m, qkv, pw, T, msk):
+def channel_forward(m, qkv, pw, zz, msk):
     def unit(i, carry):
         cols = group_slices(i)
         mask = msk[m][:, :1]
@@ -242,13 +263,13 @@
         p = p * (1.0 / jnp.sum(p, axis=1, keepdims=True))
         for k in range(GROUP // LANE):
             pw[m, 2 * i + k, 0:GROUP, :] = p[:, k * LANE : (k + 1) * LANE]
-        T[:, cols[0]] = dot(v, p.astype(BF), 1, 1)
+        zz[m, 1, :, cols[0]] = dot(v, p.astype(BF), 1, 1).astype(BF)
         return carry
 
     lax.fori_loop(0, NGROUP, unit, 0, unroll=True)
 
 
-def channel_backward(m, qkv, pw, T, msk):
+def channel_backward(m, qkv, pw, T, rr, msk):
     def unit(i, carry):
         cols = group_slices(i)
         mask = msk[m][:, :1]
@@ -259,9 +280,9 @@
         p = jnp.concatenate([pw[m, 2 * i + k, 0:GROUP, :] for k in range(GROUP // LANE)], axis=1)
         dp = dot(g, v, 0, 0)
         ds = (p * (dp - jnp.sum(p * dp, axis=1, keepdims=True))).astype(BF)
-        qkv[m, :, cols[0]] = dot(k, ds, 1, 1) * SCALE
-        qkv[m, :, cols[1]] = dot(q, ds) * (SCALE * mask)
-        qkv[m, :, cols[2]] = dot(g, p.astype(BF))
+        rr[m, 0, :, cols[0]] = (dot(k, ds, 1, 1) * SCALE).astype(BF)
+        rr[m, 0, :, cols[1]] = (dot(q, ds) * (SCALE * mask)).astype(BF)
+        rr[m, 0, :, cols[2]] = (dot(g, p.astype(BF))).astype(BF)
         return carry
 
     lax.fori_loop(0, NGROUP, unit, 0, unroll=True)
@@ -409,11 +430,18 @@
         U[wc, GRID + 1] = jnp.zeros((CELL, D), F32)
     sgp[...] = jnp.zeros(sgp.shape, F32)
 
+    def hop(m, dst, send, recv):
+        sides = [pl.ds(i * D // 2, D // 2) for i in range(2)]
+        return [
+            remote(gout.at[m, :, cols], dst.at[:, cols], send.at[m, i], recv.at[m, i], opposite)
+            for i, cols in enumerate(sides)
+        ]
+
     def u_hop(m):
-        return remote(gout.at[m], ubuf.at[0, m], us.at[m], usem.at[m], opposite)
+        return hop(m, ubuf.at[0, m], us, usem)
 
     def g_hop(m):
-        return remote(gout.at[m], gin.at[m], gs.at[m], gsem.at[m], opposite)
+        return hop(m, gin.at[m], gs, gsem)
 
     def factor_copies(k, m):
         if k == 0:
@@ -428,8 +456,10 @@
                 ("F", zz.at[m, 2], rL.at[m, 0]),
                 ("F", ab.at[m], rA.at[m]),
                 ("M", gin.at[m], rG.at[m]),
-                ("M", rr.at[m, 1], rR.at[m]),
             ]
+            for i in range(3):
+                cols = pl.ds(i * (FF // 3), FF // 3)
+                parts.append((f"M{i}", rr.at[m, 1, :, cols], rR.at[m, :, cols]))
         return [(w, remote(a, b, ss.at[m, i], rsem.at[m, i], mate)) for i, (w, a, b) in enumerate(parts)]
 
     def start_factors(m, which):
@@ -448,7 +478,7 @@
             def _():
                 for m in range(2):
                     for when, copy in factor_copies(k, m):
-                        if when in which:
+                        if when[0] in which:
                             copy.wait_recv()
 
     def shard(k):
@@ -626,7 +656,8 @@
     def forward(m, p):
         @pl.when(jnp.logical_not(early))
         def _():
-            u_hop(m).wait_recv()
+            for copy in u_hop(m):
+                copy.wait_recv()
 
         @pl.when(early & (m == 1))
         def _():
@@ -644,18 +675,18 @@
         front_forward(0, m, ubuf, msk, pr, U, C, zz, xh, rs)
         for i in range(3):
             first_time(0, i)
-            qkv[m, :, pl.ds(i * D, D)] = dot(zz[m, 0], wf[0, :, pl.ds(i * D, D)]).astype(BF).astype(F32)
+            qkv[m, :, pl.ds(i * D, D)] = dot(zz[m, 0], wf[0, :, pl.ds(i * D, D)])
 
         @pl.when(early)
         def _():
             window_forward(m, qkv, pw, T)
+            zz[m, 1] = T[...].astype(BF)
 
         @pl.when(jnp.logical_not(early))
         def _():
-            channel_forward(m, qkv, pw, T, msk)
+            channel_forward(m, qkv, pw, zz, msk)
 
         first_time(0, 3)
-        zz[m, 1] = T[...].astype(BF)
         ubuf[1, m] = (C[...] + dot(zz[m, 1], wf[0, :, pl.ds(3 * D, D)])).astype(BF)
 
         first_time(1, 5)
@@ -665,16 +696,25 @@
         first_time(0, 4)
         first_time(1, 4)
 
+        total, before = C[...], None
         for t in range(FF // FTILE):
             cols = pl.ds(t * FTILE, FTILE)
-            a, d = gelu_parts(dot(zz[m, 2], wf[1, :, cols]))
-            ab[m, :, cols] = a.astype(BF)
+            h = dot(zz[m, 2], wf[1, :, cols])
+            if t > 0:
+                total = total + dot(before, w2[pl.ds((t - 1) * FTILE, FTILE), :])
+            a, d = gelu_parts(h)
+            before = a.astype(BF)
+            ab[m, :, cols] = before
             rr[m, 1, :, cols] = d.astype(BF)
-        gout[m] = (C[...] + dot(ab[m], w2[...])).astype(BF)
-
-        @pl.when(early)
-        def _():
-            u_hop(m).start()
+        for i in range(2):
+            cols = pl.ds(i * D // 2, D // 2)
+            part = total[:, i * D // 2 : (i + 1) * D // 2]
+            gout[m, :, cols] = (part + dot(before, w2[pl.ds(FF - FTILE, FTILE), cols])).astype(BF)
+
+            @pl.when(early)
+            def _():
+                u_hop(m)[i].start()
+
 
         @pl.when(jnp.logical_not(early))
         def _():
@@ -706,24 +746,31 @@
     def backward(m):
         @pl.when(early)
         def _():
-            g_hop(m).wait_recv()
-
+            for copy in g_hop(m):
+                copy.wait_recv()
+
+        start_factors(m, "M")
         for t in range(FF // FTILE):
             cols = pl.ds(t * FTILE, FTILE)
             da = dot(gin[m], w2[cols, :], 1, 1)
             rr[m, 1, :, cols] = (da * rr[m, 1, :, cols].astype(F32)).astype(BF)
+            if t % 2 == 1:
+                start_factors(m, f"M{t // 2}")
         T[...] = dot(rr[m, 1], wf[1], 1, 1)
-        start_factors(m, "M")
         last = pl.ds(3 * D, D)
 
         @pl.when(early)
         def _():
-            u_hop(m).wait_send()
+            for copy in u_hop(m):
+                copy.wait_send()
 
         def tail_lanes(i):
             return rr.at[m, 0, :, pl.ds(pl.multiple_of(3 * D + i * LANE, LANE), LANE)]
 
-        front_backward(1, m, ubuf, msk, pr, U, T, lambda i: gin.at[m, :, lanes(i)], xh, rs, sgp, tail_lanes)
+        def nothing(half):
+            pass
+
+        front_backward(1, m, msk, pr, U, T, lambda i: gin.at[m, :, lanes(i)], xh, rs, sgp, tail_lanes, nothing)
         start_factors(m, "G")
 
         @pl.when(m == 1)
@@ -740,14 +787,14 @@
         @pl.when(early)
         def _():
             window_backward(m, qkv, pw, T)
+            for i in range(3):
+                cols = pl.ds(i * D, D)
+                rr[m, 0, :, cols] = qkv[m, :, cols].astype(BF)
 
         @pl.when(jnp.logical_not(early))
         def _():
-            channel_backward(m, qkv, pw, T, msk)
-
-        for i in range(3):
-            cols = pl.ds(i * D, D)
-            rr[m, 0, :, cols] = qkv[m, :, cols].astype(BF)
+            channel_backward(m, qkv, pw, T, rr, msk)
+
         start_factors(m, "A")
 
         @pl.when(m == 1)
@@ -756,11 +803,14 @@
                 early_event(e)
 
         T[...] = dot(rr[m, 0, :, pl.ds(0, 3 * D)], wf[0, :, pl.ds(0, 3 * D)], 1, 1)
-        front_backward(0, m, ubuf, msk, pr, U, T, tail_lanes, xh, rs, sgp, lambda i: gout.at[m, :, lanes(i)])
-
-        @pl.when(jnp.logical_not(early))
-        def _():
-            g_hop(m).start()
+        def send_half(half):
+            @pl.when(jnp.logical_not(early))
+            def _():
+                g_hop(m)[half].start()
+
+        front_backward(
+            0, m, msk, pr, U, T, tail_lanes, xh, rs, sgp, lambda i: gout.at[m, :, lanes(i)], send_half
+        )
 
         @pl.when(s == 2)
         def _():
@@ -803,12 +853,15 @@
 
             where_active(sub, ready)
 
-    for sec in range(2):
-        for j in range(12):
-            sgs[sec, j : j + 1, :] = jnp.sum(sgp[sec, j], axis=0, keepdims=True)
-        sgs[sec, 12:16, :] = jnp.zeros((4, D), F32)
     give = remote(sgs.at[1 - c], sgm, sgsem.at[0], sgsem.at[1], mate)
-    give.start()
+
+    def small_sums():
+        for sec in range(2):
+            for j in range(12):
+                sgs[sec, j : j + 1, :] = jnp.sum(sgp[sec, j], axis=0, keepdims=True)
+            sgs[sec, 12:16, :] = jnp.zeros((4, D), F32)
+        give.start()
+
     wait_factors("GA")
 
     @pl.when(helper)
@@ -823,9 +876,14 @@
         where_active(1, lambda: event(1, t + EARLY))
         where_active(2, lambda: event(2, t + EARLY))
         where_active(3, lambda: event(3, t))
+        @pl.when((t >= 1) & (t < 5))
+        def _():
+            front_sums((t - 1) // 2, lax.rem(t - 1, 2), ubuf, msk, U, xh, sgp)
+
+        pl.when(t == 5)(small_sums)
         for r in range(rounds + 1):
 
-            @pl.when(t == 1 + 3 * r)
+            @pl.when(t == 6 + 2 * r)
             def _():
                 if r == 0:
                     give.wait_recv()
@@ -925,7 +983,8 @@
     def _():
         img_out.wait_send()
         for m in range(2):
-            g_hop(m).wait_send()
+            for copy in g_hop(m):
+                copy.wait_send()
         remote(flat.at[0], act, es.at[0], er.at[0], opposite).wait_send()
         pltpu.make_async_copy(flat.at[1], act, es.at[0]).wait()
         remote(flat.at[1], ing, es.at[1], er.at[1], opposite).wait_recv()
@@ -986,10 +1045,10 @@
             dma((6,)),
             dma((6,)),
             dma((2,)),
-            dma((2,)),
-            dma((2,)),
-            dma((2,)),
-            dma((2,)),
+            dma((2, 2)),
+            dma((2, 2)),
+            dma((2, 2)),
+            dma((2, 2)),
             dma((2, 6)),
             dma((2, 6)),
             dma((2,)),

time: 236 us -> 235 us (level)
  no operation moved by 1% of the time
where the time goes in v7:
time: 235 us
  Pallas kernels  234 us (100%)
    pallas_call x1, Pallas kernels, relay(): pl.pallas_call(relay_kernel, out_shape=[shape(slot, BF), shape(slot, BF),...  226 us
    pallas_call x1, Pallas kernels, finish(): pl.pallas_call(finish_kernel, out_shape=[shape(out1.shape, F32), shape(ou...  7.58 us

profile of v7, /device:TPU:0, one launch (start us, length us, event | category | flops | bytes accessed | tf_op | source)
XLA Modules:
  0.0 234.7 jit_solution(6557518850696517492)
XLA Ops:
  0.6 226.3 %relay.1 = (bf16[14,14,768]{2,1,0:T(8,128)(2,1)}, bf16[14,14,768]{2,1,0:T(8,128)(2,1)}, bf16[768,3072]{1,0:T(8,128)(2,1)}, bf16[1536,768]{1,0:T(8,128)(2,1)}, f32[16,768]{1,0:T(8,128)}) custom-call(s32[4]{0:T(128)} %wrows.1, s32[4]{0:T(128)} %wcols.1, bf16[14,14,768]{2,1,0:T(8,128)(2,1)} %bitcast.9, bf16[14,14,768]{2,1,0:T(8,128)(2,1)} %bitcast.10, ...), custom_call_target="tpu_custom_call" | custom-call | tf_op jit(solution)/shard_map/relay/pallas_call | solution.py:1002
  226.9 7.6 %finish.1 = (f32[768,3072]{1,0:T(8,128)}, f32[1536,768]{1,0:T(8,128)}, bf16[14,14,768]{2,1,0:T(8,128)(2,1)}, f32[14,14,1,768]{3,2,1,0:T(1,128)}, f32[9,1,768]{2,...) custom-call(bf16[768,3072]{1,0:T(8,128)(2,1)} %get-tuple-element.21.out1, ...), custom_call_target="tpu_custom_call" | custom-call | tf_op jit(solution)/shard_map/finish/pallas_call | solution.py:1134

commit v8 on v7

--- a/solution.py
+++ b/solution.py
@@ -459,7 +459,7 @@
             ]
             for i in range(3):
                 cols = pl.ds(i * (FF // 3), FF // 3)
-                parts.append((f"M{i}", rr.at[m, 1, :, cols], rR.at[m, :, cols]))
+                parts.append((f"H{i}", rr.at[m, 1, :, cols], rR.at[m, :, cols]))
         return [(w, remote(a, b, ss.at[m, i], rsem.at[m, i], mate)) for i, (w, a, b) in enumerate(parts)]
 
     def start_factors(m, which):
@@ -502,13 +502,14 @@
 
     def tile(sub, h, j):
         side = pl.ds(h * COLS, COLS)
-        if sub == 0:
+        if sub in (0, 4):
+            rows = first_rows(sub, h)
             last = jnp.where(j >= (3 * n) // 4, 1, 0)
             own = jnp.where(c == 1, 2, last)
             other = jnp.where(c == 1, 0, last)
             cols = lanes(j, COLS)
-            terms = [(zz.at[m, own, :, side], rr.at[m, c, :, cols]) for m in range(2)]
-            terms += [(rL.at[m, other, :, side], rR.at[m, :, cols]) for m in range(2)]
+            terms = [(zz.at[m, own, :, rows], rr.at[m, c, :, cols]) for m in range(2)]
+            terms += [(rL.at[m, other, :, rows], rR.at[m, :, cols]) for m in range(2)]
         elif sub == 1:
             cols = lanes(j, WIDE)
             terms = [(ab.at[m, :, cols], gin.at[m, :, side]) for m in range(2)]
@@ -527,10 +528,14 @@
             return jnp.concatenate([own, pick(products(terms), j)], axis=0)
         return products(terms)
 
-    sizes = (COLS, WIDE, REST, 2 * REST)
+    sizes = (COLS // 3 * 2, WIDE, REST, 2 * REST, COLS // 3)
     parts = [pl.ds(sum(sizes[:i]), size) for i, size in enumerate(sizes)]
+    subs = range(len(sizes))
     odd = c == 1
-    active = (None, odd, odd, helper)
+    active = (None, odd, odd, helper, None)
+
+    def first_rows(sub, h):
+        return pl.ds(h * COLS + (0 if sub == 0 else sizes[0]), sizes[sub])
 
     def where_active(sub, run):
         if active[sub] is None:
@@ -540,8 +545,8 @@
 
 
     def gathered(sub, h, j):
-        if sub == 0:
-            return wf.at[0, pl.ds(h * COLS, COLS), lanes(j, COLS)]
+        if sub in (0, 4):
+            return wf.at[0, first_rows(sub, h), lanes(j, COLS)]
         if sub == 3:
             rows = pl.ds(pl.multiple_of(lax.rem(j, n // 2) * sizes[3], 16), sizes[3])
             return wf.at[1, rows, lanes(2 * (j // (n // 2)) + h, COLS)]
@@ -560,8 +565,8 @@
 
     def write(h, j, sub, part=0):
         src, side = gathered(sub, h, j), pl.ds(h * COLS, COLS)
-        if sub == 0:
-            dst = out1.at[side, lanes(j, COLS)]
+        if sub in (0, 4):
+            dst = out1.at[first_rows(sub, h), lanes(j, COLS)]
         elif sub == 1:
             dst = out2.at[pl.ds(pl.multiple_of((j - half_shards) * WIDE, 16), WIDE), side]
         else:
@@ -644,10 +649,10 @@
 
                 deliver(h, j, sub)
 
-    def early_event(e):
+    def early_event(e, which):
         @pl.when(odd)
         def _():
-            for sub in range(3):
+            for sub in which:
                 event(sub, e)
 
     def small(r):
@@ -755,8 +760,24 @@
             da = dot(gin[m], w2[cols, :], 1, 1)
             rr[m, 1, :, cols] = (da * rr[m, 1, :, cols].astype(F32)).astype(BF)
             if t % 2 == 1:
-                start_factors(m, f"M{t // 2}")
+                start_factors(m, f"H{t // 2}")
+
+        @pl.when(m == 1)
+        def _():
+            @pl.when(jnp.logical_not(early))
+            def _():
+                wait_factors("F")
+
+            wait_factors("M")
+            early_event(0, (1, 2))
+
         T[...] = dot(rr[m, 1], wf[1], 1, 1)
+
+        @pl.when(m == 1)
+        def _():
+            wait_factors("H")
+            early_event(0, (0, 4))
+
         last = pl.ds(3 * D, D)
 
         @pl.when(early)
@@ -772,15 +793,6 @@
 
         front_backward(1, m, msk, pr, U, T, lambda i: gin.at[m, :, lanes(i)], xh, rs, sgp, tail_lanes, nothing)
         start_factors(m, "G")
-
-        @pl.when(m == 1)
-        def _():
-            @pl.when(jnp.logical_not(early))
-            def _():
-                wait_factors("F")
-
-            wait_factors("M")
-            early_event(0)
 
         T[...] = dot(rr[m, 0, :, last], wf[0, :, last], 1, 1)
 
@@ -800,7 +812,7 @@
         @pl.when(m == 1)
         def _():
             for e in range(1, EARLY):
-                early_event(e)
+                early_event(e, (1, 2, 0, 4))
 
         T[...] = dot(rr[m, 0, :, pl.ds(0, 3 * D)], wf[0, :, pl.ds(0, 3 * D)], 1, 1)
         def send_half(half):
@@ -846,7 +858,7 @@
     lax.fori_loop(0, 4, phase, 0)
 
     for h in range(2):
-        for sub in range(4):
+        for sub in subs:
 
             def ready():
                 pl.semaphore_signal(free.at[h, sub], inc=1, device_id=nexts[1 - h], device_id_type=MESH)
@@ -872,7 +884,8 @@
             share(m).wait_recv()
 
     def ring_step(t, carry):
-        event(0, t + jnp.where(odd, EARLY, 0))
+        for sub in (0, 4):
+            event(sub, t + jnp.where(odd, EARLY, 0))
         where_active(1, lambda: event(1, t + EARLY))
         where_active(2, lambda: event(2, t + EARLY))
         where_active(3, lambda: event(3, t))
@@ -916,7 +929,7 @@
 
     def drain(t, carry):
         for h in range(2):
-            for sub in range(4):
+            for sub in subs:
 
                 def sent():
                     scatter(h, t, sub).wait_send()
@@ -931,6 +944,7 @@
     def written(j, carry):
         for h in range(2):
             write(h, j, 0).wait()
+            write(h, j, 4).wait()
 
             @pl.when(odd)
             def _():
@@ -1054,9 +1068,9 @@
             dma((2,)),
             dma((2,)),
             dma((2,)),
-            dma((2, 2 * RING, 4)),
-            dma((2, 2 * RING, 4)),
-            dma((2, RING, 4)),
+            dma((2, 2 * RING, 5)),
+            dma((2, 2 * RING, 5)),
+            dma((2, RING, 5)),
             dma((rounds,)),
             dma((rounds,)),
             dma((4,)),
@@ -1067,7 +1081,7 @@
             dma((2, RING)),
             dma((2, RING)),
             dma((2, RING)),
-            pltpu.SemaphoreType.REGULAR((2, 4)),
+            pltpu.SemaphoreType.REGULAR((2, 5)),
         ],
         name="relay",
         compiler_params=pltpu.CompilerParams(

time: 235 us -> 233 us (level)
  Pallas kernels: 234 us -> 231 us
    pallas_call x1, Pallas kernels: 226 us -> 223 us  [relay(): pl.pallas_call(relay_kernel, out_shape=[shape(slot, BF), shape(slot, BF),...]
where the time goes in v8:
time: 233 us; the launch traced here: 232 us
  Pallas kernels  231 us (99%)
    pallas_call x1, Pallas kernels, relay(): pl.pallas_call(relay_kernel, out_shape=[shape(slot, BF), shape(slot, BF),...  223 us
    pallas_call x1, Pallas kernels, finish(): pl.pallas_call(finish_kernel, out_shape=[shape(out1.shape, F32), shape(ou...  7.58 us

profile of v8, /device:TPU:0, one launch (start us, length us, event | category | flops | bytes accessed | tf_op | source)
XLA Modules:
  0.0 231.7 jit_solution(14633389271749775912)
XLA Ops:
  0.6 223.4 %relay.1 = (bf16[14,14,768]{2,1,0:T(8,128)(2,1)}, bf16[14,14,768]{2,1,0:T(8,128)(2,1)}, bf16[768,3072]{1,0:T(8,128)(2,1)}, bf16[1536,768]{1,0:T(8,128)(2,1)}, f32[16,768]{1,0:T(8,128)}) custom-call(s32[4]{0:T(128)} %wrows.1, s32[4]{0:T(128)} %wcols.1, bf16[14,14,768]{2,1,0:T(8,128)(2,1)} %bitcast.9, bf16[14,14,768]{2,1,0:T(8,128)(2,1)} %bitcast.10, ...), custom_call_target="tpu_custom_call" | custom-call | tf_op jit(solution)/shard_map/relay/pallas_call | solution.py:1016
  224.0 7.6 %finish.1 = (f32[768,3072]{1,0:T(8,128)}, f32[1536,768]{1,0:T(8,128)}, bf16[14,14,768]{2,1,0:T(8,128)(2,1)}, f32[14,14,1,768]{3,2,1,0:T(1,128)}, f32[9,1,768]{2,...) custom-call(bf16[768,3072]{1,0:T(8,128)(2,1)} %get-tuple-element.21.out1, ...), custom_call_target="tpu_custom_call" | custom-call | tf_op jit(solution)/shard_map/finish/pallas_call | solution.py:1148

commit v9 on v8

--- a/solution.py
+++ b/solution.py
@@ -291,8 +291,8 @@
 RING = 8
 COLS = FF // RING
 WIDE = FF // 12 * 8 // RING
-REST = FF // 6 // RING
-FIFTH, SIXTH = FF // 6 * 4, FF // 6 * 5
+REST = FF // 3 // RING
+THIRD = FF // 3 * 2
 EARLY = 2
 
 
@@ -309,7 +309,8 @@
     stage, c = s // 2, lax.rem(s, 2)
     mate = (dp, stage * 2 + (1 - c))
     opposite = (dp, (1 - stage) * 2 + c)
-    lender, helper = s == 1, s == 3
+    diagonal = (dp, 3 - s)
+    lender, helper = s == 1, s == 2
     early = stage == 0
 
     spot = lax.rem(dp, n)
@@ -328,7 +329,7 @@
         partners.append((jnp.where(lax.rem(spot // bit, 2) == 0, dp + bit, dp - bit), s))
 
     barrier = pltpu.get_barrier_semaphore()
-    peers = [mate, opposite, *nexts, *partners]
+    peers = [mate, opposite, diagonal, *nexts, *partners]
     for peer in peers:
         pl.semaphore_signal(barrier, inc=1, device_id=peer, device_id_type=MESH)
     pl.semaphore_wait(barrier, len(peers))
@@ -497,9 +498,6 @@
             total = part if total is None else total + part
         return total
 
-    def pick(total, j):
-        return jnp.where(lax.rem(j, 2) == 1, total[REST:], total[:REST])
-
     def tile(sub, h, j):
         side = pl.ds(h * COLS, COLS)
         if sub in (0, 4):
@@ -510,29 +508,22 @@
             cols = lanes(j, COLS)
             terms = [(zz.at[m, own, :, rows], rr.at[m, c, :, cols]) for m in range(2)]
             terms += [(rL.at[m, other, :, rows], rR.at[m, :, cols]) for m in range(2)]
-        elif sub == 1:
-            cols = lanes(j, WIDE)
+        elif sub == 3:
+            cols = lanes(j, REST)
+            terms = [(xA.at[m, :, cols], xG.at[m, :, side]) for m in range(2)]
+            terms += [(xA.at[2 + m, :, cols], gout.at[m, :, side]) for m in range(2)]
+        else:
+            cols = lanes(j, WIDE) if sub == 1 else pl.ds(pl.multiple_of(THIRD + j * REST, LANE), REST)
             terms = [(ab.at[m, :, cols], gin.at[m, :, side]) for m in range(2)]
             terms += [(rA.at[m, :, cols], rG.at[m, :, side]) for m in range(2)]
-        else:
-            start = (FIFTH if sub == 2 else SIXTH) + j // 2 * 2 * REST
-            cols = pl.ds(pl.multiple_of(start, LANE), 2 * REST)
-            terms = [(ab.at[m, :, cols], gin.at[m, :, side]) for m in range(2)]
-            terms += [(rA.at[m, :, cols], rG.at[m, :, side]) for m in range(2)]
-            own = pick(products(terms), j)
-            if sub == 2:
-                return own
-            cols = lanes(j // 2, 2 * REST)
-            terms = [(xA.at[m, :, cols], gout.at[m, :, side]) for m in range(2)]
-            terms += [(xA.at[2 + m, :, cols], xG.at[m, :, side]) for m in range(2)]
-            return jnp.concatenate([own, pick(products(terms), j)], axis=0)
         return products(terms)
 
-    sizes = (COLS // 3 * 2, WIDE, REST, 2 * REST, COLS // 3)
-    parts = [pl.ds(sum(sizes[:i]), size) for i, size in enumerate(sizes)]
+    sizes = (COLS // 3 * 2, WIDE, REST, REST, COLS // 3)
+    starts = (0, COLS, COLS + WIDE, COLS + WIDE, COLS // 3 * 2)
+    parts = [pl.ds(start, size) for start, size in zip(starts, sizes)]
     subs = range(len(sizes))
     odd = c == 1
-    active = (None, odd, odd, helper, None)
+    active = (None, odd, s == 3, helper, None)
 
     def first_rows(sub, h):
         return pl.ds(h * COLS + (0 if sub == 0 else sizes[0]), sizes[sub])
@@ -547,10 +538,7 @@
     def gathered(sub, h, j):
         if sub in (0, 4):
             return wf.at[0, first_rows(sub, h), lanes(j, COLS)]
-        if sub == 3:
-            rows = pl.ds(pl.multiple_of(lax.rem(j, n // 2) * sizes[3], 16), sizes[3])
-            return wf.at[1, rows, lanes(2 * (j // (n // 2)) + h, COLS)]
-        first_row = 0 if sub == 1 else FIFTH
+        first_row = 0 if sub == 1 else THIRD
         return w2.at[pl.ds(pl.multiple_of(first_row + j * sizes[sub], 16), sizes[sub]), pl.ds(h * COLS, COLS)]
 
     def scatter(h, t, sub):
@@ -563,18 +551,16 @@
 
     half_shards = n * 3 // 4
 
-    def write(h, j, sub, part=0):
+    def write(h, j, sub):
         src, side = gathered(sub, h, j), pl.ds(h * COLS, COLS)
         if sub in (0, 4):
             dst = out1.at[first_rows(sub, h), lanes(j, COLS)]
         elif sub == 1:
             dst = out2.at[pl.ds(pl.multiple_of((j - half_shards) * WIDE, 16), WIDE), side]
         else:
-            first_row = (FIFTH if sub == 2 else SIXTH) - FF // 2
-            dst = out2.at[pl.ds(pl.multiple_of(first_row + j * REST, 16), REST), side]
-            src = src.at[pl.ds(part * REST, REST), :]
-        if part == 1:
-            return remote(src, dst, bs.at[h, j], br.at[h, j], opposite)
+            dst = out2.at[pl.ds(pl.multiple_of(THIRD - FF // 2 + j * REST, 16), REST), side]
+        if sub == 3:
+            return remote(src, dst, bs.at[h, j], br.at[h, j], diagonal)
         return pltpu.make_async_copy(src, dst, osem.at[h, j, sub])
 
     def hand_over(h, j):
@@ -594,14 +580,12 @@
 
         else:
             write(h, j, sub).start()
-            if sub == 3:
-                write(h, j, sub, 1).start()
 
     def lend(m):
-        cols = pl.ds(SIXTH, FF - SIXTH)
+        cols = pl.ds(THIRD, FF - THIRD)
         return (
-            remote(ab.at[m, :, cols], xA.at[m], xs.at[m], xr.at[m], opposite),
-            remote(rA.at[m, :, cols], xA.at[2 + m], xs.at[2 + m], xr.at[2 + m], opposite),
+            remote(ab.at[m, :, cols], xA.at[m], xs.at[m], xr.at[m], diagonal),
+            remote(rA.at[m, :, cols], xA.at[2 + m], xs.at[2 + m], xr.at[2 + m], diagonal),
         )
 
     def share(m):
@@ -653,7 +637,7 @@
         @pl.when(odd)
         def _():
             for sub in which:
-                event(sub, e)
+                where_active(sub, lambda: event(sub, e))
 
     def small(r):
         return remote(acc.at[r], got.at[r], sms.at[r], smr.at[r], partners[r])
@@ -824,7 +808,7 @@
             0, m, msk, pr, U, T, tail_lanes, xh, rs, sgp, lambda i: gout.at[m, :, lanes(i)], send_half
         )
 
-        @pl.when(s == 2)
+        @pl.when(s == 3)
         def _():
             share(m).start()
 
@@ -948,7 +932,7 @@
 
             @pl.when(odd)
             def _():
-                write(h, j, 2).wait()
+                where_active(2, lambda: write(h, j, 2).wait())
 
                 @pl.when(j < half_shards)
                 def _():
@@ -964,12 +948,11 @@
 
             @pl.when(helper)
             def _():
-                write(h, j, 3).wait()
-                write(h, j, 3, 1).wait_send()
+                write(h, j, 3).wait_send()
 
             @pl.when(lender)
             def _():
-                write(h, j, 3, 1).wait_recv()
+                write(h, j, 3).wait_recv()
 
         return carry
 
@@ -981,7 +964,7 @@
             for copy in lend(m):
                 copy.wait_send()
 
-    @pl.when(s == 2)
+    @pl.when(s == 3)
     def _():
         for m in range(2):
             share(m).wait_send()
@@ -1050,9 +1033,9 @@
             pltpu.VMEM((2, ROWS, FF), BF),
             pltpu.VMEM((2, ROWS, FF), BF),
             pltpu.VMEM((2,) + image, BF),
-            pltpu.VMEM((4, ROWS, FF - SIXTH), BF),
+            pltpu.VMEM((4, ROWS, FF - THIRD), BF),
             pltpu.VMEM((2,) + image, BF),
-            pltpu.VMEM((2, RING, COLS + WIDE + 3 * REST, COLS), BF),
+            pltpu.VMEM((2, RING, COLS + WIDE + REST, COLS), BF),
             pltpu.VMEM((rounds + 1, 16, D), F32),
             pltpu.VMEM((rounds, 16, D), F32),
             dma((5,)),

time: 233 us -> 231 us (level)
  the two profiles are of different devices: /device:TPU:0 before, /device:TPU:19 now
where the time goes in v9:
time: 231 us; the launch traced here: 230 us
  Pallas kernels  230 us (100%)
    pallas_call x1, Pallas kernels, relay(): pl.pallas_call(relay_kernel, out_shape=[shape(slot, BF), shape(slot, BF),...  222 us
    pallas_call x1, Pallas kernels, finish(): pl.pallas_call(finish_kernel, out_shape=[shape(out1.shape, F32), shape(ou...  7.58 us

profile of v9, /device:TPU:19, one launch (start us, length us, event | category | flops | bytes accessed | tf_op | source)
XLA Modules:
  0.0 230.4 jit_solution(3279621784237875434)
XLA Ops:
  0.6 222.0 %relay.1 = (bf16[14,14,768]{2,1,0:T(8,128)(2,1)}, bf16[14,14,768]{2,1,0:T(8,128)(2,1)}, bf16[768,3072]{1,0:T(8,128)(2,1)}, bf16[1536,768]{1,0:T(8,128)(2,1)}, f32[16,768]{1,0:T(8,128)}) custom-call(s32[4]{0:T(128)} %wrows.1, s32[4]{0:T(128)} %wcols.1, bf16[14,14,768]{2,1,0:T(8,128)(2,1)} %bitcast.9, bf16[14,14,768]{2,1,0:T(8,128)(2,1)} %bitcast.10, ...), custom_call_target="tpu_custom_call" | custom-call | tf_op jit(solution)/shard_map/relay/pallas_call | solution.py:999
  222.7 7.6 %finish.1 = (f32[768,3072]{1,0:T(8,128)}, f32[1536,768]{1,0:T(8,128)}, bf16[14,14,768]{2,1,0:T(8,128)(2,1)}, f32[14,14,1,768]{3,2,1,0:T(1,128)}, f32[9,1,768]{2,...) custom-call(bf16[768,3072]{1,0:T(8,128)(2,1)} %get-tuple-element.21.out1, ...), custom_call_target="tpu_custom_call" | custom-call | tf_op jit(solution)/shard_map/finish/pallas_call | solution.py:1131

commit v10 on v9

--- a/solution.py
+++ b/solution.py
@@ -84,13 +84,13 @@
             sums.append(acc)
         return total + jnp.concatenate(sums, axis=0)
 
-    mean = jnp.sum(lax.fori_loop(0, D // LANE, conv, zero), axis=-1, keepdims=True) * (1.0 / D)
+    mean = jnp.sum(lax.fori_loop(0, D // LANE, conv, zero, unroll=True), axis=-1, keepdims=True) * (1.0 / D)
 
     def spread(i, total):
         centred = C[:, lanes(i)] - mean
         return total + centred * centred
 
-    var = jnp.sum(lax.fori_loop(0, D // LANE, spread, zero), axis=-1, keepdims=True) * (1.0 / D)
+    var = jnp.sum(lax.fori_loop(0, D // LANE, spread, zero, unroll=True), axis=-1, keepdims=True) * (1.0 / D)
     rstd = lax.rsqrt(var + EPS)
     rs[sec, m] = jnp.broadcast_to(rstd, (ROWS, LANE))
 
@@ -101,7 +101,7 @@
         zz[m, 2 * sec, :, ls] = (xhat * pr[sec, 10:11, ls] + pr[sec, 11:12, ls]).astype(BF)
         return carry
 
-    lax.fori_loop(0, D // LANE, norm, 0)
+    lax.fori_loop(0, D // LANE, norm, 0, unroll=True)
 
 
 def fold(value):
@@ -122,7 +122,7 @@
         gain = pr[sec, 10:11, ls]
         return s1 + dz * gain, s2 + both * gain
 
-    s1, s2 = lax.fori_loop(0, D // LANE, sums, (zero, zero))
+    s1, s2 = lax.fori_loop(0, D // LANE, sums, (zero, zero), unroll=True)
     m1 = jnp.sum(s1, axis=-1, keepdims=True) * (1.0 / D)
     m2 = jnp.sum(s2, axis=-1, keepdims=True) * (1.0 / D)
 
@@ -149,9 +149,9 @@
         out(i)[...] = jnp.concatenate(du, axis=0).astype(BF)
         return carry
 
-    lax.fori_loop(0, D // LANE // 2, back, 0)
+    lax.fori_loop(0, D // LANE // 2, back, 0, unroll=True)
     sent(0)
-    lax.fori_loop(D // LANE // 2, D // LANE, back, 0)
+    lax.fori_loop(D // LANE // 2, D // LANE, back, 0, unroll=True)
     sent(1)
 
 
@@ -221,7 +221,7 @@
             T[rows[w], cols[0]] = out[w]
         return carry
 
-    lax.fori_loop(0, UNITS // 2, unit, 0)
+    lax.fori_loop(0, UNITS // 2, unit, 0, unroll=2)
 
 
 def window_backward(m, qkv, pw, T):
@@ -293,6 +293,7 @@
 WIDE = FF // 12 * 8 // RING
 REST = FF // 3 // RING
 THIRD = FF // 3 * 2
+LENT = RING * 3 // 4
 EARLY = 2
 
 
@@ -447,19 +448,19 @@
     def factor_copies(k, m):
         if k == 0:
             parts = [
-                ("F", zz.at[m, 0], rL.at[m, 0]),
-                ("F", zz.at[m, 1], rL.at[m, 1]),
+                ("F0", zz.at[m, 0], rL.at[m, 0]),
+                ("F1", zz.at[m, 1], rL.at[m, 1]),
                 ("G", rr.at[m, 0, :, pl.ds(3 * D, D)], rR.at[m, :, pl.ds(3 * D, D)]),
                 ("A", rr.at[m, 0, :, pl.ds(0, 3 * D)], rR.at[m, :, pl.ds(0, 3 * D)]),
             ]
         else:
             parts = [
-                ("F", zz.at[m, 2], rL.at[m, 0]),
-                ("F", ab.at[m], rA.at[m]),
+                ("F2", zz.at[m, 2], rL.at[m, 0]),
                 ("M", gin.at[m], rG.at[m]),
             ]
             for i in range(3):
                 cols = pl.ds(i * (FF // 3), FF // 3)
+                parts.append((f"X{i}", ab.at[m, :, cols], rA.at[m, :, cols]))
                 parts.append((f"H{i}", rr.at[m, 1, :, cols], rR.at[m, :, cols]))
         return [(w, remote(a, b, ss.at[m, i], rsem.at[m, i], mate)) for i, (w, a, b) in enumerate(parts)]
 
@@ -523,7 +524,15 @@
     parts = [pl.ds(start, size) for start, size in zip(starts, sizes)]
     subs = range(len(sizes))
     odd = c == 1
-    active = (None, odd, s == 3, helper, None)
+    active = (None, odd, odd, helper, None)
+
+    def where_live(sub, j, run):
+        if sub == 2:
+            pl.when(jnp.logical_not(lender) | (j >= LENT))(run)
+        elif sub == 3:
+            pl.when(j < LENT)(run)
+        else:
+            run()
 
     def first_rows(sub, h):
         return pl.ds(h * COLS + (0 if sub == 0 else sizes[0]), sizes[sub])
@@ -582,7 +591,7 @@
             write(h, j, sub).start()
 
     def lend(m):
-        cols = pl.ds(THIRD, FF - THIRD)
+        cols = pl.ds(THIRD, LENT * REST)
         return (
             remote(ab.at[m, :, cols], xA.at[m], xs.at[m], xr.at[m], diagonal),
             remote(rA.at[m, :, cols], xA.at[2 + m], xs.at[2 + m], xr.at[2 + m], diagonal),
@@ -592,27 +601,34 @@
         return remote(gout.at[m], xG.at[m], ys.at[m], yr.at[m], mate)
 
     def reduce_event(sub, h, e):
-        total = tile(sub, h, shard(me - sign(h) * e))
-
-        @pl.when(e == 0)
-        def _():
-            buf[h, 0, parts[sub], :] = total.astype(BF)
-            scatter(h, 0, sub).start()
-
-        @pl.when((e > 0) & (e < n - 1))
-        def _():
-            scatter(h, e - 1, sub).wait_recv()
-            buf[h, e, parts[sub], :] = (total + buf[h, e, parts[sub], :].astype(F32)).astype(BF)
-            scatter(h, e, sub).start()
+        j = shard(me - sign(h) * e)
 
         @pl.when(e == n - 1)
         def _():
-            j = home(h, 0)
-            scatter(h, n - 2, sub).wait_recv()
-            gathered(sub, h, j)[...] = (total + buf[h, n - 1, parts[sub], :].astype(F32)).astype(BF)
             pl.semaphore_wait(free.at[h, sub], 1)
-            spread(h, 0, sub, j).start()
-            deliver(h, j, sub)
+
+        def run():
+            total = tile(sub, h, j)
+
+            @pl.when(e == 0)
+            def _():
+                buf[h, 0, parts[sub], :] = total.astype(BF)
+                scatter(h, 0, sub).start()
+
+            @pl.when((e > 0) & (e < n - 1))
+            def _():
+                scatter(h, e - 1, sub).wait_recv()
+                buf[h, e, parts[sub], :] = (total + buf[h, e, parts[sub], :].astype(F32)).astype(BF)
+                scatter(h, e, sub).start()
+
+            @pl.when(e == n - 1)
+            def _():
+                scatter(h, n - 2, sub).wait_recv()
+                gathered(sub, h, j)[...] = (total + buf[h, n - 1, parts[sub], :].astype(F32)).astype(BF)
+                spread(h, 0, sub, j).start()
+                deliver(h, j, sub)
+
+        where_live(sub, j, run)
 
     def event(sub, e):
         for h in range(2):
@@ -625,13 +641,17 @@
             def _():
                 t = e - (n - 1)
                 j = home(h, t)
-                spread(h, t - 1, sub, j).wait_recv()
-
-                @pl.when(t < n - 1)
-                def _():
-                    spread(h, t, sub, j).start()
-
-                deliver(h, j, sub)
+
+                def run():
+                    spread(h, t - 1, sub, j).wait_recv()
+
+                    @pl.when(t < n - 1)
+                    def _():
+                        spread(h, t, sub, j).start()
+
+                    deliver(h, j, sub)
+
+                where_live(sub, j, run)
 
     def early_event(e, which):
         @pl.when(odd)
@@ -662,6 +682,7 @@
 
         first_time(0, 5)
         front_forward(0, m, ubuf, msk, pr, U, C, zz, xh, rs)
+        start_factors(m, "F0")
         for i in range(3):
             first_time(0, i)
             qkv[m, :, pl.ds(i * D, D)] = dot(zz[m, 0], wf[0, :, pl.ds(i * D, D)])
@@ -675,11 +696,13 @@
         def _():
             channel_forward(m, qkv, pw, zz, msk)
 
+        start_factors(m, "F1")
         first_time(0, 3)
         ubuf[1, m] = (C[...] + dot(zz[m, 1], wf[0, :, pl.ds(3 * D, D)])).astype(BF)
 
         first_time(1, 5)
         front_forward(1, m, ubuf, msk, pr, U, C, zz, xh, rs)
+        start_factors(m, "F2")
         for i in range(4):
             first_time(1, i)
         first_time(0, 4)
@@ -695,6 +718,8 @@
             before = a.astype(BF)
             ab[m, :, cols] = before
             rr[m, 1, :, cols] = d.astype(BF)
+            if t % 2 == 1:
+                start_factors(m, f"X{t // 2}")
         for i in range(2):
             cols = pl.ds(i * D // 2, D // 2)
             part = total[:, i * D // 2 : (i + 1) * D // 2]
@@ -720,11 +745,9 @@
         def _():
             pltpu.make_async_copy(flat.at[1], act, es.at[0]).start()
 
-        start_factors(m, "F")
-
         @pl.when(early & (m == 1))
         def _():
-            wait_factors("F")
+            wait_factors("FX")
 
         @pl.when(lender & (m == 1))
         def _():
@@ -750,7 +773,7 @@
         def _():
             @pl.when(jnp.logical_not(early))
             def _():
-                wait_factors("F")
+                wait_factors("FX")
 
             wait_factors("M")
             early_event(0, (1, 2))
@@ -916,8 +939,8 @@
             for sub in subs:
 
                 def sent():
-                    scatter(h, t, sub).wait_send()
-                    spread(h, t, sub, home(h, t)).wait_send()
+                    where_live(sub, shard(me - sign(h) * t), lambda: scatter(h, t, sub).wait_send())
+                    where_live(sub, home(h, t), lambda: spread(h, t, sub, home(h, t)).wait_send())
 
                 where_active(sub, sent)
 
@@ -932,7 +955,7 @@
 
             @pl.when(odd)
             def _():
-                where_active(2, lambda: write(h, j, 2).wait())
+                where_live(2, j, lambda: write(h, j, 2).wait())
 
                 @pl.when(j < half_shards)
                 def _():
@@ -946,11 +969,11 @@
             def _():
                 hand_over(h, j).wait_recv()
 
-            @pl.when(helper)
+            @pl.when(helper & (j < LENT))
             def _():
                 write(h, j, 3).wait_send()
 
-            @pl.when(lender)
+            @pl.when(lender & (j < LENT))
             def _():
                 write(h, j, 3).wait_recv()
 
@@ -1033,7 +1056,7 @@
             pltpu.VMEM((2, ROWS, FF), BF),
             pltpu.VMEM((2, ROWS, FF), BF),
             pltpu.VMEM((2,) + image, BF),
-            pltpu.VMEM((4, ROWS, FF - THIRD), BF),
+            pltpu.VMEM((4, ROWS, LENT * REST), BF),
             pltpu.VMEM((2,) + image, BF),
             pltpu.VMEM((2, RING, COLS + WIDE + REST, COLS), BF),
             pltpu.VMEM((rounds + 1, 16, D), F32),
@@ -1046,8 +1069,8 @@
             dma((2, 2)),
             dma((2, 2)),
             dma((2, 2)),
-            dma((2, 6)),
-            dma((2, 6)),
+            dma((2, 8)),
+            dma((2, 8)),
             dma((2,)),
             dma((2,)),
             dma((2,)),

time: 231 us -> 228 us (0.987)
  the two profiles are of different devices: /device:TPU:19 before, /device:TPU:0 now
where the time goes in v10:
time: 228 us; the launch traced here: 226 us
  Pallas kernels  225 us (99%)
    pallas_call x1, Pallas kernels, relay(): pl.pallas_call(relay_kernel, out_shape=[shape(slot, BF), shape(slot, BF),...  218 us
    pallas_call x1, Pallas kernels, finish(): pl.pallas_call(finish_kernel, out_shape=[shape(out1.shape, F32), shape(ou...  7.58 us

profile of v10, /device:TPU:0, one launch (start us, length us, event | category | flops | bytes accessed | tf_op | source)
XLA Modules:
  0.0 226.2 jit_solution(5530306268352848902)
XLA Ops:
  0.6 217.8 %relay.1 = (bf16[14,14,768]{2,1,0:T(8,128)(2,1)}, bf16[14,14,768]{2,1,0:T(8,128)(2,1)}, bf16[768,3072]{1,0:T(8,128)(2,1)}, bf16[1536,768]{1,0:T(8,128)(2,1)}, f32[16,768]{1,0:T(8,128)}) custom-call(s32[4]{0:T(128)} %wrows.1, s32[4]{0:T(128)} %wcols.1, bf16[14,14,768]{2,1,0:T(8,128)(2,1)} %bitcast.9, bf16[14,14,768]{2,1,0:T(8,128)(2,1)} %bitcast.10, ...), custom_call_target="tpu_custom_call" | custom-call | tf_op jit(solution)/shard_map/relay/pallas_call | solution.py:1022
  218.5 7.6 %finish.1 = (f32[768,3072]{1,0:T(8,128)}, f32[1536,768]{1,0:T(8,128)}, bf16[14,14,768]{2,1,0:T(8,128)(2,1)}, f32[14,14,1,768]{3,2,1,0:T(1,128)}, f32[9,1,768]{2,...) custom-call(bf16[768,3072]{1,0:T(8,128)(2,1)} %get-tuple-element.21.out1, ...), custom_call_target="tpu_custom_call" | custom-call | tf_op jit(solution)/shard_map/finish/pallas_call | solution.py:1154
